TPU v7x, 32 devices: a whole 2x2x4 slice. The times are simulated.
32 devices in a mesh: rows: 8 (over y, x, core), width: 4 (over z).
Axes of the slice: x: 2, y: 2, z: 4, core: 2. Of those that a mesh axis runs over, the one named last changes fastest.
Arguments:
- history: bfloat16 [25, 768, 16384], P(None, 'width', 'rows'), may hold values from -24 to 24
- cotangent: bfloat16 [768, 16384], P('width', 'rows'), may hold values from -12 to 12
- segments: int32 [16, 1024], P('rows'), may hold values from 0 to 15, never falling along the last dimension, each value on 1 to 256 neighbouring positions
- w_attend: float32 [3, 768, 768], P(None, 'rows', 'width'), may hold values from -0.21875 to 0.21875
- m_attend: float32 [3, 768, 768], P(None, 'rows', 'width'), may hold values from -160 to 160
- v_attend: float32 [3, 768, 768], P(None, 'rows', 'width'), may hold values from 3276.8 to 13107.2
- w_output: float32 [768, 768], P('width', 'rows'), may hold values from -1.25 to 1.25
- m_output: float32 [768, 768], P('width', 'rows'), may hold values from -48 to 48
- v_output: float32 [768, 768], P('width', 'rows'), may hold values from 311.296 to 1245.184
- w_expand: float32 [768, 3072], P('rows', 'width'), may hold values from -0.21875 to 0.21875
- m_expand: float32 [768, 3072], P('rows', 'width'), may hold values from -96 to 96
- v_expand: float32 [768, 3072], P('rows', 'width'), may hold values from 1245.184 to 4915.2
- w_reduce: float32 [3072, 768], P('width', 'rows'), may hold values from -0.21875 to 0.21875
- m_reduce: float32 [3072, 768], P('width', 'rows'), may hold values from -112 to 112
- v_reduce: float32 [3072, 768], P('width', 'rows'), may hold values from 1638.4 to 6225.92
- gains: float32 [2, 768], P(None, 'width'), may hold values from 0.5 to 1.5
- m_gains: float32 [2, 768], P(None, 'width'), may hold values from -160 to 160
- v_gains: float32 [2, 768], P(None, 'width'), may hold values from 3276.8 to 13107.2
- mix: float32 [25], replicated, may hold values from -4 to 4
- m_mix: float32 [25], replicated, may hold values from -12288 to 12288
- v_mix: float32 [25], replicated, may hold values from 16357786 to 66689432
Outputs:
- block_output: bfloat16 [768, 16384], P('width', 'rows')
- history_grad: bfloat16 [25, 768, 16384], P(None, 'width', 'rows')
- w_attend_new: float32 [3, 768, 768], P(None, 'rows', 'width')
- m_attend_new: float32 [3, 768, 768], P(None, 'rows', 'width')
- v_attend_new: float32 [3, 768, 768], P(None, 'rows', 'width')
- w_output_new: float32 [768, 768], P('width', 'rows')
- m_output_new: float32 [768, 768], P('width', 'rows')
- v_output_new: float32 [768, 768], P('width', 'rows')
- w_expand_new: float32 [768, 3072], P('rows', 'width')
- m_expand_new: float32 [768, 3072], P('rows', 'width')
- v_expand_new: float32 [768, 3072], P('rows', 'width')
- w_reduce_new: float32 [3072, 768], P('width', 'rows')
- m_reduce_new: float32 [3072, 768], P('width', 'rows')
- v_reduce_new: float32 [3072, 768], P('width', 'rows')
- gains_new: float32 [2, 768], P(None, 'width')
- m_gains_new: float32 [2, 768], P(None, 'width')
- v_gains_new: float32 [2, 768], P(None, 'width')
- mix_new: float32 [25], replicated
- m_mix_new: float32 [25], replicated
- v_mix_new: float32 [25], replicated
Inputs may be any that keep to these rules, and one draw needn't show every extreme that they name: In each row of segments the numbers never fall; a run of equal numbers is one document.
All inputs are finite; a program needn't handle non-finite values.
Results may differ from a plain program's by a relative error of at most 0.012.
Values may be sent and summed in bfloat16 or wider, within the bound.
A program may use at most 192 MiB of HBM per device.

v0:
```python
import math

import jax
import jax.numpy as jnp
from jax import lax
from jax.sharding import PartitionSpec as P

D = 768
HEAD = 64
STEP = 10


EPS_NORM = 1e-05
EPS_ADAM = 1e-08
BETA_ONE = 0.9
BETA_TWO = 0.95
RATE_MATRIX = 0.02
RATE_OUTPUT = 0.12
RATE_GAIN = 0.4
RATE_MIX = 0.05
DECAY = 0.1
MASKED = -1e30


def rotary(heads_in, cosine, sine):
    halfway = heads_in.shape[-1] // 2
    leading = heads_in[..., :halfway]
    trailing = heads_in[..., halfway:]
    return jnp.concatenate(
        [leading * cosine - trailing * sine, trailing * cosine + leading * sine], -1
    )


def angles(segments):
    row_length = segments.shape[-1]
    places = jnp.arange(row_length, dtype=jnp.int32)
    changed = jnp.concatenate(
        [jnp.ones_like(segments[:, :1]), (segments[:, 1:] != segments[:, :-1]).astype(jnp.int32)], 1
    )
    doc_starts = lax.cummax(changed * places[None, :], axis=1)
    position = (places[None, :] - doc_starts).astype(jnp.float32)
    halfway = HEAD // 2
    frequency = jnp.exp(jnp.arange(halfway, dtype=jnp.float32) * (-2.0 * math.log(10000.0) / HEAD))
    turned = position[:, :, None] * frequency[None, None, :]
    return (jnp.cos(turned)[:, :, None, :], jnp.sin(turned)[:, :, None, :])


def allowed_pairs(segment_row):
    places = jnp.arange(segment_row.shape[0], dtype=jnp.int32)
    return (segment_row[:, None] == segment_row[None, :]) & (places[None, :] <= places[:, None])


def norm_sums(totals, squares):
    return lax.psum((totals, squares), "width")


def widen(piece_low):
    return lax.all_gather(piece_low, "width", axis=1, tiled=True)


def narrow(term):
    return lax.psum_scatter(term, "width", scatter_dimension=1, tiled=True)


def normalize(stream, gain):
    totals, squares = norm_sums(jnp.sum(stream, 1), jnp.sum(stream * stream, 1))
    centre = totals / D
    spread = squares / D - centre * centre
    scaling = lax.rsqrt(spread + EPS_NORM)
    centred = (stream - centre[:, None]) * scaling[:, None]
    return (centred, scaling, (gain * centred).astype(jnp.bfloat16))


def normalize_back(upstream, centred, scaling, gain):
    scaled = upstream * gain
    totals, crossed = norm_sums(jnp.sum(scaled, 1), jnp.sum(scaled * centred, 1))
    back = scaling[:, None] * (scaled - totals[:, None] / D - centred * (crossed[:, None] / D))
    return (back, jnp.sum(upstream * centred, 0))


def head_scores(queries, key_heads, segment_row):
    scores = jnp.einsum(
        "qhd,khd->hqk", queries, key_heads, preferred_element_type=jnp.float32
    ) * HEAD ** (-0.5)
    return (scores, allowed_pairs(segment_row)[None])


def attend_forward(entry):
    queries, key_heads, value_heads, segment_row = entry
    scores, allowed = head_scores(queries, key_heads, segment_row)
    scores = jnp.where(allowed, scores, MASKED)
    highest = jnp.max(scores, -1, keepdims=True)
    raised = jnp.exp(scores - highest)
    summed = jnp.sum(raised, -1, keepdims=True)
    weights_low = (raised / summed).astype(jnp.bfloat16)
    attended = jnp.einsum(
        "hqk,khd->qhd", weights_low, value_heads, preferred_element_type=jnp.float32
    )
    return (attended, (highest + jnp.log(summed))[..., 0])


def attend_back(entry):
    queries, key_heads, value_heads, segment_row, log_total, upstream = entry
    scores, allowed = head_scores(queries, key_heads, segment_row)
    weights = jnp.exp(jnp.where(allowed, scores - log_total[..., None], MASKED))
    grad_values = jnp.einsum(
        "hqk,qhd->khd", weights.astype(jnp.bfloat16), upstream, preferred_element_type=jnp.float32
    )
    grad_weights = jnp.einsum(
        "qhd,khd->hqk", upstream, value_heads, preferred_element_type=jnp.float32
    )
    inner = jnp.sum(weights * grad_weights, -1, keepdims=True)
    grad_scores = (weights * (grad_weights - inner)).astype(jnp.bfloat16)
    grad_queries = jnp.einsum(
        "hqk,khd->qhd", grad_scores, key_heads, preferred_element_type=jnp.float32
    ) * HEAD ** (-0.5)
    grad_keys = jnp.einsum(
        "hqk,qhd->khd", grad_scores, queries, preferred_element_type=jnp.float32
    ) * HEAD ** (-0.5)
    return (grad_queries, grad_keys, grad_values)


def optimize(weight, gradient, first_moment, second_moment, rate, decay):
    first_moment = BETA_ONE * first_moment + (1.0 - BETA_ONE) * gradient
    second_moment = BETA_TWO * second_moment + (1.0 - BETA_TWO) * gradient * gradient
    first_fixed = first_moment / (1.0 - BETA_ONE**STEP)
    second_fixed = second_moment / (1.0 - BETA_TWO**STEP)
    weight = weight - rate * (first_fixed / (jnp.sqrt(second_fixed) + EPS_ADAM) + decay * weight)
    return (weight, first_moment, second_moment)


def on_device(
    history,
    cotangent,
    segments,
    w_attend,
    m_attend,
    v_attend,
    w_output,
    m_output,
    v_output,
    w_expand,
    m_expand,
    v_expand,
    w_reduce,
    m_reduce,
    v_reduce,
    gains,
    m_gains,
    v_gains,
    mix,
    m_mix,
    v_mix,
):
    layer_count = history.shape[0]
    feature_count = history.shape[1]
    tokens = history.shape[2]
    head_count = feature_count // HEAD
    seq_count = segments.shape[0]
    seq_len = segments.shape[1]
    attend_full, output_full, expand_full, reduce_full = (
        lax.all_gather(w_attend.astype(jnp.bfloat16), "rows", axis=1, tiled=True),
        lax.all_gather(w_output.astype(jnp.bfloat16), "rows", axis=1, tiled=True),
        lax.all_gather(w_expand.astype(jnp.bfloat16), "rows", axis=0, tiled=True),
        lax.all_gather(w_reduce.astype(jnp.bfloat16), "rows", axis=1, tiled=True),
    )

    def mix_step(depth_at, running):
        return running + mix[depth_at] * history[depth_at].astype(jnp.float32)

    stream = jnp.transpose(
        lax.fori_loop(0, layer_count, mix_step, jnp.zeros((feature_count, tokens), jnp.float32))
    )
    centred_one, scaling_one, normed_one = normalize(stream, gains[0])
    full_one = widen(normed_one)
    projected = jnp.einsum("td,kdc->ktc", full_one, attend_full, preferred_element_type=jnp.float32)
    projected = projected.reshape(3, seq_count, seq_len, head_count, HEAD)
    cosine, sine = angles(segments)
    queries = rotary(projected[0], cosine, sine).astype(jnp.bfloat16)
    key_heads = rotary(projected[1], cosine, sine).astype(jnp.bfloat16)
    value_heads = projected[2].astype(jnp.bfloat16)
    attended, log_total = lax.map(attend_forward, (queries, key_heads, value_heads, segments))
    attended = attended.reshape(tokens, feature_count).astype(jnp.bfloat16)
    middle = stream + narrow(jnp.dot(attended, output_full, preferred_element_type=jnp.float32))
    centred_two, scaling_two, normed_two = normalize(middle, gains[1])
    full_two = widen(normed_two)
    hidden_in = jnp.dot(full_two, expand_full, preferred_element_type=jnp.float32)
    hidden, gelu_back = jax.vjp(jax.nn.gelu, hidden_in)
    hidden = hidden.astype(jnp.bfloat16)
    block_output = jnp.transpose(
        middle + narrow(jnp.dot(hidden, reduce_full, preferred_element_type=jnp.float32))
    ).astype(jnp.bfloat16)
    cot_rows = jnp.transpose(cotangent)
    cot_full = widen(cot_rows)
    grad_reduce = jnp.einsum("tf,td->fd", hidden, cot_full, preferred_element_type=jnp.float32)
    grad_hidden = jnp.einsum("td,fd->tf", cot_full, reduce_full, preferred_element_type=jnp.float32)
    grad_in = gelu_back(grad_hidden)[0].astype(jnp.bfloat16)
    grad_expand = jnp.einsum("td,tf->df", full_two, grad_in, preferred_element_type=jnp.float32)
    grad_normed_two = narrow(
        jnp.einsum("tf,df->td", grad_in, expand_full, preferred_element_type=jnp.float32)
    )
    back_two, gain_two = normalize_back(grad_normed_two, centred_two, scaling_two, gains[1])
    grad_middle = cot_rows.astype(jnp.float32) + back_two
    middle_full = widen(grad_middle.astype(jnp.bfloat16))
    grad_output = jnp.einsum("tc,td->cd", attended, middle_full, preferred_element_type=jnp.float32)
    grad_attended = jnp.einsum(
        "td,cd->tc", middle_full, output_full, preferred_element_type=jnp.float32
    ).astype(jnp.bfloat16)
    grad_queries, grad_keys, grad_values = lax.map(
        attend_back,
        (
            queries,
            key_heads,
            value_heads,
            segments,
            log_total,
            grad_attended.reshape(seq_count, seq_len, head_count, HEAD),
        ),
    )
    grad_projected = (
        jnp.stack(
            [rotary(grad_queries, cosine, -sine), rotary(grad_keys, cosine, -sine), grad_values]
        )
        .reshape(3, tokens, feature_count)
        .astype(jnp.bfloat16)
    )
    grad_attend = jnp.einsum(
        "td,ktc->kdc", full_one, grad_projected, preferred_element_type=jnp.float32
    )
    sum_attend, sum_output, sum_expand, sum_reduce = (
        lax.psum_scatter(grad_attend, "rows", scatter_dimension=1, tiled=True),
        lax.psum_scatter(grad_output, "rows", scatter_dimension=1, tiled=True),
        lax.psum_scatter(grad_expand, "rows", scatter_dimension=0, tiled=True),
        lax.psum_scatter(grad_reduce, "rows", scatter_dimension=1, tiled=True),
    )
    grad_normed_one = narrow(
        jnp.einsum("ktc,kdc->td", grad_projected, attend_full, preferred_element_type=jnp.float32)
    )
    back_one, gain_one = normalize_back(grad_normed_one, centred_one, scaling_one, gains[0])
    grad_columns = jnp.transpose(grad_middle + back_one)
    history_grad = (mix[:, None, None] * grad_columns[None]).astype(jnp.bfloat16)

    def mix_grad(depth_at, running):
        return running.at[depth_at].set(
            jnp.sum(history[depth_at].astype(jnp.float32) * grad_columns)
        )

    mix_part = lax.fori_loop(0, layer_count, mix_grad, jnp.zeros((layer_count,), jnp.float32))
    sum_gains, mix_rows = lax.psum((jnp.stack([gain_one, gain_two]), mix_part), "rows")
    sum_mix = lax.psum(mix_rows, "width")
    w_attend_new, m_attend_new, v_attend_new = optimize(
        w_attend, sum_attend, m_attend, v_attend, RATE_MATRIX, DECAY
    )
    w_output_new, m_output_new, v_output_new = optimize(
        w_output, sum_output, m_output, v_output, RATE_OUTPUT, DECAY
    )
    w_expand_new, m_expand_new, v_expand_new = optimize(
        w_expand, sum_expand, m_expand, v_expand, RATE_MATRIX, DECAY
    )
    w_reduce_new, m_reduce_new, v_reduce_new = optimize(
        w_reduce, sum_reduce, m_reduce, v_reduce, RATE_MATRIX, DECAY
    )
    gains_new, m_gains_new, v_gains_new = optimize(
        gains, sum_gains, m_gains, v_gains, RATE_GAIN, 0.0
    )
    mix_new, m_mix_new, v_mix_new = optimize(mix, sum_mix, m_mix, v_mix, RATE_MIX, 0.0)
    return (
        block_output,
        history_grad,
        w_attend_new,
        m_attend_new,
        v_attend_new,
        w_output_new,
        m_output_new,
        v_output_new,
        w_expand_new,
        m_expand_new,
        v_expand_new,
        w_reduce_new,
        m_reduce_new,
        v_reduce_new,
        gains_new,
        m_gains_new,
        v_gains_new,
        mix_new,
        m_mix_new,
        v_mix_new,
    )


def solution(mesh):
    in_specs = (
        P(None, "width", "rows"),
        P("width", "rows"),
        P("rows", None),
        P(None, "rows", "width"),
        P(None, "rows", "width"),
        P(None, "rows", "width"),
        P("width", "rows"),
        P("width", "rows"),
        P("width", "rows"),
        P("rows", "width"),
        P("rows", "width"),
        P("rows", "width"),
        P("width", "rows"),
        P("width", "rows"),
        P("width", "rows"),
        P(None, "width"),
        P(None, "width"),
        P(None, "width"),
        P(),
        P(),
        P(),
    )
    out_specs = (
        P("width", "rows"),
        P(None, "width", "rows"),
        P(None, "rows", "width"),
        P(None, "rows", "width"),
        P(None, "rows", "width"),
        P("width", "rows"),
        P("width", "rows"),
        P("width", "rows"),
        P("rows", "width"),
        P("rows", "width"),
        P("rows", "width"),
        P("width", "rows"),
        P("width", "rows"),
        P("width", "rows"),
        P(None, "width"),
        P(None, "width"),
        P(None, "width"),
        P(),
        P(),
        P(),
    )
    return jax.shard_map(
        on_device, mesh=mesh, in_specs=in_specs, out_specs=out_specs, check_vma=False
    )
```

profile of v0, /device:TPU:0, one launch (start us, length us, event | category | flops | bytes accessed | tf_op | source)
XLA Modules:
  0.0 1282.3 jit_solution(4899681531657097995)
XLA Ops:
  9.4 91.0 %while.61 = (s32[]{:T(128)}, f32[192,2048]{1,0:T(8,128)S(1)}, f32[25]{0:T(128)}, bf16[25,192,2048]{2,1,0:T(8,128)(2,1)}) while((s32[]{:T(128)}, f32[192,2048]{1,0:T(8,128)S(1)}, f32[25]{0:T(128)}, bf16[25,192,2048]{2,1,0:T(8,128)(2,1)}) %tuple.163), condition=%wide.region_1.0_spmd.clone.clone, body=%wide.region_0.0_spmd.clone.sunk.clone | while | flops 1572867 | bytes 3932251 | solution.py:172
  100.7 20.6 %all-reduce.5 = (f32[2048]{0:T(1024)S(1)}, f32[2048]{0:T(1024)S(1)}) all-reduce(f32[2048]{0:T(1024)S(1)} %fusion.66, f32[2048]{0:T(1024)S(1)} %reduce_sum.121), channel_id=1, replica_groups=mesh['rows'=8,'width'=4] {'width'}, use_global_device_ids=true, to_apply=%region_5.0 | all-reduce | flops 4096 | bytes 32768 | tf_op jit(solution)/shard_map/psum | solution.py:54
  125.9 13.2 %all_gather.25 = bf16[3,768,192]{2,0,1:T(4,128)(2,1)S(1)} all-gather(bf16[3,96,192]{2,0,1:T(4,128)(2,1)S(1)} %copy.118), channel_id=1, replica_groups=mesh['rows'=8,'width'=4] {'rows'}, dimensions={1}, use_global_device_ids=true | all-gather | bytes 995328 | tf_op jit(solution)/shard_map/all_gather | solution.py:162
  140.0 9.9 all_gather.26
  151.7 32.6 %all-gather.7.cloned.1.call-done = bf16[2048,768]{0,1:T(8,128)(2,1)} async-done(((bf16[2048,192]{0,1:T(8,128)(2,1)}), bf16[2048,768]{0,1:T(8,128)(2,1)}) %all-gather.7.cloned.1.call-update) | async-done | bytes 3145744 | tf_op jit(solution)/shard_map/all_gather | solution.py:58
  205.8 30.4 %while.58 = (s32[]{:T(128)}, bf16[2,1024,3,64]{1,3,2,0:T(8,128)(2,1)}, f32[2,3,1024]{2,1,0:T(4,128)}, bf16[2,1024,3,64]{1,3,2,0:T(8,128)(2,1)}, s32[2,1024]{1,0:...) while((s32[]{:T(128)}, ...), condition=%wide.region_11.12_spmd.clone, body=%wide.region_8.11_spmd.sunk.clone | while | flops 846197760 | bytes 48220280 | solution.py:182
  244.7 107.9 %reduce-scatter.13.cloned.1.call-done = f32[2048,192]{0,1:T(8,128)} async-done(((f32[2048,768]{0,1:T(8,128)}), f32[2048,192]{0,1:T(8,128)}) %reduce-scatter.13.cloned.1.call-update) | async-done | bytes 1572880 | tf_op jit(solution)/shard_map/reduce_scatter | solution.py:62
  354.9 17.9 %all-reduce.4 = (f32[2048]{0:T(1024)S(1)}, f32[2048]{0:T(1024)S(1)}) all-reduce(f32[2048]{0:T(1024)} %get-tuple-element.469, f32[2048]{0:T(1024)S(1)} %get-tuple-element.468), channel_id=1, replica_groups=mesh['rows'=8,'width'=4] {'width'}, use_global_device_ids=true, to_apply=%region_16.17 | all-reduce | flops 4096 | bytes 32768 | tf_op jit(solution)/shard_map/psum | solution.py:54
  375.8 60.7 %all-gather.9.cloned.1.call-done = bf16[2048,768]{0,1:T(8,128)(2,1)} async-done(((bf16[2048,192]{0,1:T(8,128)(2,1)}), bf16[2048,768]{0,1:T(8,128)(2,1)}) %all-gather.9.cloned.1.call-update) | async-done | bytes 3145744 | tf_op jit(solution)/shard_map/all_gather | solution.py:58
  444.0 55.9 %all-gather.15.cloned.1.call-done = bf16[2048,768]{0,1:T(8,128)(2,1)} async-done(((bf16[2048,192]{0,1:T(8,128)(2,1)}), bf16[2048,768]{0,1:T(8,128)(2,1)}) %all-gather.15.cloned.1.call-update) | async-done | bytes 3145744 | tf_op jit(solution)/shard_map/all_gather | solution.py:58
  507.9 41.0 %reduce-scatter.23.cloned.1.call-done = f32[768,96]{0,1:T(8,128)} async-done(((f32[768,768]{0,1:T(8,128)}), f32[768,96]{0,1:T(8,128)}) %reduce-scatter.23.cloned.1.call-update) | async-done | bytes 294928 | tf_op jit(solution)/shard_map/reduce_scatter | solution.py:234
  551.1 24.4 %all-gather.13.cloned.1.call-done = bf16[768,768]{0,1:T(8,128)(2,1)} async-done(((bf16[768,96]{0,1:T(8,128)(2,1)}), bf16[768,768]{0,1:T(8,128)(2,1)}) %all-gather.13.cloned.1.call-update) | async-done | bytes 1179664 | tf_op jit(solution)/shard_map/all_gather | solution.py:165
  575.5 8.9 fusion.62
  590.7 110.7 %reduce-scatter.17.cloned.1.call-done = f32[2048,192]{0,1:T(8,128)} async-done(((f32[2048,768]{0,1:T(8,128)}), f32[2048,192]{0,1:T(8,128)}) %reduce-scatter.17.cloned.1.call-update) | async-done | bytes 1572880 | tf_op jit(solution)/shard_map/reduce_scatter | solution.py:62
  704.2 19.2 %all-reduce.3 = (f32[2048]{0:T(1024)}, f32[2048]{0:T(1024)}) all-reduce(f32[2048]{0:T(1024)} %get-tuple-element.465, f32[2048]{0:T(1024)} %get-tuple-element.466), channel_id=1, replica_groups=mesh['rows'=8,'width'=4] {'width'}, use_global_device_ids=true, to_apply=%region_22.23 | all-reduce | flops 4096 | bytes 32768 | tf_op jit(solution)/shard_map/psum | solution.py:54
  735.4 54.8 %all-gather.17.cloned.1.call-done = bf16[2048,768]{0,1:T(8,128)(2,1)} async-done(((bf16[2048,192]{0,1:T(8,128)(2,1)}), bf16[2048,768]{0,1:T(8,128)(2,1)}) %all-gather.17.cloned.1.call-update) | async-done | bytes 3145744 | tf_op jit(solution)/shard_map/all_gather | solution.py:58
  795.7 51.7 %while.59 = (s32[]{:T(128)}, f32[2,1024,3,64]{1,3,2,0:T(8,128)}, f32[2,1024,3,64]{1,3,2,0:T(8,128)}, bf16[2,1024,3,64]{1,3,2,0:T(8,128)(2,1)}, bf16[2,1024,3,64]...) while((s32[]{:T(128)}, f32[2,1024,3,64]{1,3,2,0:T(8,128)}, ...), condition=%wide.region_25.26_spmd.clone, body=%wide.region_23.25_spmd.sunk.clone | while | flops 2063987712 | bytes 135247168 | solution.py:209
  895.0 39.8 %reduce-scatter.25.cloned.1.call-done = f32[96,576]{1,0:T(8,128)} async-done(((f32[768,576]{1,0:T(8,128)}), f32[96,576]{1,0:T(8,128)}) %reduce-scatter.25.cloned.1.call-update) | async-done | bytes 221200
  940.7 107.8 %reduce-scatter.19.cloned.1.call-done = f32[2048,192]{0,1:T(8,128)} async-done(((f32[2048,768]{0,1:T(8,128)}), f32[2048,192]{0,1:T(8,128)}) %reduce-scatter.19.cloned.1.call-update) | async-done | bytes 1572880 | tf_op jit(solution)/shard_map/reduce_scatter | solution.py:62
  1050.6 18.5 %all-reduce.2 = (f32[2048]{0:T(1024)S(1)}, f32[2048]{0:T(1024)S(1)}) all-reduce(f32[2048]{0:T(1024)S(1)} %get-tuple-element.463, f32[2048]{0:T(1024)S(1)} %get-tuple-element.467), channel_id=1, replica_groups=mesh['rows'=8,'width'=4] {'width'}, use_global_device_ids=true, to_apply=%region_30.31 | all-reduce | flops 4096 | bytes 32768 | tf_op jit(solution)/shard_map/psum | solution.py:54
  1069.1 93.2 %reduce-scatter.15.cloned.1.call-done = f32[2048,192]{0,1:T(8,128)} async-done(((f32[2048,768]{0,1:T(8,128)}), f32[2048,192]{0,1:T(8,128)}) %reduce-scatter.15.cloned.1.call-update) | async-done | bytes 1572880 | tf_op jit(solution)/shard_map/reduce_scatter | solution.py:62
  1174.7 74.0 %while.60 = (s32[]{:T(128)}, f32[25]{0:T(128)S(1)}, bf16[25,192,2048]{2,1,0:T(8,128)(2,1)}, f32[192,2048]{1,0:T(8,128)S(1)}) while((s32[]{:T(128)}, f32[25]{0:T(128)S(1)}, bf16[25,192,2048]{2,1,0:T(8,128)(2,1)}, f32[192,2048]{1,0:T(8,128)S(1)}) %tuple.207), condition=%wide.region_40.41_spmd.clone, body=%wide.region_38.40_spmd.sunk.clone | while | flops 1179653 | bytes 2359595 | solution.py:248
  1248.6 13.6 %all-reduce.1 = (f32[2,192]{1,0:T(2,128)S(1)}, f32[25]{0:T(128)S(1)}) all-reduce(f32[2,192]{1,0:T(2,128)S(1)} %pad_maximum_fusion.4, f32[25]{0:T(128)S(1)} %get-tuple-element.298), channel_id=1, replica_groups=mesh['rows'=8,'width'=4] {'rows'}, use_global_device_ids=true, to_apply=%region_37.38 | all-reduce | flops 409 | bytes 3272 | tf_op jit(solution)/shard_map/psum | solution.py:249
  1262.2 11.1 psum.87
  (403 shorter events, 402.4 us)
Async XLA Ops:
  8.0 176.4 %all-gather.7.cloned.1.call-start = ((), (), s32[]{:S(2)}) async-start(), calls=%async_computation.8 | async-start | bytes 3932160 | tf_op jit(solution)/shard_map/all_gather | solution.py:58
  122.5 230.0 %reduce-scatter.13.cloned.1.call-start = ((), (), s32[]{:S(2)}) async-start(), calls=%async_computation.9 | async-start | bytes 7864320 | tf_op jit(solution)/shard_map/reduce_scatter | solution.py:62
  243.0 132.8 %all-gather.11.cloned.1.call-start = ((), (), s32[]{:S(2)}) async-start(), calls=%async_computation.11 | async-start | bytes 1327104 | tf_op jit(solution)/shard_map/all_gather | solution.py:164
  244.6 191.8 %all-gather.9.cloned.1.call-start = ((), (), s32[]{:S(2)}) async-start(), calls=%async_computation.10 | async-start | bytes 3932160 | tf_op jit(solution)/shard_map/all_gather | solution.py:58
  354.9 370.0 %copy-start.4 = (f32[2048,192]{0,1:T(8,128)}, f32[2048,192]{0,1:T(8,128)S(1)}, u32[]{:S(2)}) copy-start(f32[2048,192]{0,1:T(8,128)S(1)} %get-tuple-element.548) | copy-start | bytes 4718596
  372.8 352.1 %copy-start.40 = (f32[2048]{0:T(1024)}, f32[2048]{0:T(1024)S(1)}, u32[]{:S(2)}) copy-start(f32[2048]{0:T(1024)S(1)} %get-tuple-element.579) | copy-start | bytes 24580
  374.6 125.3 %all-gather.15.cloned.1.call-start = ((), (), s32[]{:S(2)}) async-start(), calls=%async_computation.14 | async-start | bytes 3932160 | tf_op jit(solution)/shard_map/all_gather | solution.py:58
  375.2 173.8 %reduce-scatter.23.cloned.1.call-start = ((), (), s32[]{:S(2)}) async-start(), calls=%async_computation.19 | async-start | bytes 2654208 | tf_op jit(solution)/shard_map/reduce_scatter | solution.py:234
  507.9 67.7 %all-gather.13.cloned.1.call-start = ((), (), s32[]{:S(2)}) async-start(), calls=%async_computation.12 | async-start | bytes 1327104 | tf_op jit(solution)/shard_map/all_gather | solution.py:165
  551.1 150.3 %reduce-scatter.17.cloned.1.call-start = ((), (), s32[]{:S(2)}) async-start(), calls=%async_computation.15 | async-start | bytes 7864320 | tf_op jit(solution)/shard_map/reduce_scatter | solution.py:62
  590.6 199.5 %all-gather.17.cloned.1.call-start = ((), (), s32[]{:S(2)}) async-start(), calls=%async_computation.16 | async-start | bytes 3932160 | tf_op jit(solution)/shard_map/all_gather | solution.py:58
  728.1 162.9 %reduce-scatter.21.cloned.1.call-start = ((), (), s32[]{:S(2)}) async-start(), calls=%async_computation.18 | async-start | bytes 2654208 | tf_op jit(solution)/shard_map/reduce_scatter | solution.py:233
  735.3 157.8 %reduce-scatter.27.cloned.1.call-start = ((), (), s32[]{:S(2)}) async-start(), calls=%async_computation.21 | async-start | bytes 884736
  857.6 77.2 %reduce-scatter.25.cloned.1.call-start = ((), (), s32[]{:S(2)}) async-start(), calls=%async_computation.20 | async-start | bytes 2211840
  872.7 175.8 %reduce-scatter.19.cloned.1.call-start = ((), (), s32[]{:S(2)}) async-start(), calls=%async_computation.17 | async-start | bytes 7864320 | tf_op jit(solution)/shard_map/reduce_scatter | solution.py:62
  880.1 282.2 %reduce-scatter.15.cloned.1.call-start = ((), (), s32[]{:S(2)}) async-start(), calls=%async_computation.13 | async-start | bytes 7864320 | tf_op jit(solution)/shard_map/reduce_scatter | solution.py:62
  893.1 155.4 %copy-start.45 = (f32[2048]{0:T(1024)S(1)}, f32[2048]{0:T(1024)}, u32[]{:S(2)}) copy-start(f32[2048]{0:T(1024)} %copy-done.44) | copy-start | bytes 24580
  893.1 155.4 %copy-start.47 = (f32[2048]{0:T(1024)S(1)}, f32[2048]{0:T(1024)}, u32[]{:S(2)}) copy-start(f32[2048]{0:T(1024)} %copy-done.46) | copy-start | bytes 24580
  893.1 155.4 %copy-start.56 = (f32[1,192]{1,0:T(1,128)S(1)}, f32[1,192]{1,0:T(1,128)}, u32[]{:S(2)}) copy-start(f32[1,192]{1,0:T(1,128)} %copy-done.55) | copy-start | bytes 2308
  936.8 225.5 %copy-start.41 = (f32[2048]{0:T(1024)S(1)}, f32[2048]{0:T(1024)}, u32[]{:S(2)}) copy-start(f32[2048]{0:T(1024)} %copy-done.40) | copy-start | bytes 24580
  936.8 225.5 %copy-start.43 = (f32[2048]{0:T(1024)S(1)}, f32[2048]{0:T(1024)}, u32[]{:S(2)}) copy-start(f32[2048]{0:T(1024)} %copy-done.42) | copy-start | bytes 24580
  936.8 225.5 %copy-start.51 = (f32[2048]{0:T(1024)S(1)}, f32[2048]{0:T(1024)}, u32[]{:S(2)}) copy-start(f32[2048]{0:T(1024)} %copy-done.50) | copy-start | bytes 24580
  936.8 225.5 %copy-start.53 = (f32[2048]{0:T(1024)S(1)}, f32[2048]{0:T(1024)}, u32[]{:S(2)}) copy-start(f32[2048]{0:T(1024)} %copy-done.52) | copy-start | bytes 24580
  936.8 225.5 %copy-start.54 = (f32[1,192]{1,0:T(1,128)S(1)}, f32[1,192]{1,0:T(1,128)}, u32[]{:S(2)}) copy-start(f32[1,192]{1,0:T(1,128)} %get-tuple-element.583) | copy-start | bytes 2308
  (64 other events, 2004.1 us)
Sparse Core Ops, SparseCore 0:
  122.6 61.7 all-gather.6
  243.1 109.3 reduce-scatter.12
  728.2 61.8 all-gather.16
Sparse Core Ops, SparseCore 1:
  245.9 22.5 all-gather.10
  374.7 61.7 all-gather.8
  437.9 62.0 all-gather.14
  508.0 41.0 reduce-scatter.22
  551.6 23.9 all-gather.12
  590.7 110.6 reduce-scatter.16
  735.4 40.7 reduce-scatter.20
  857.7 33.6 reduce-scatter.26
  894.6 40.1 reduce-scatter.24
  937.8 110.6 reduce-scatter.18
  1050.8 111.5 reduce-scatter.14
where the time goes:
time: 1290 us; the launch traced here: 1280 us
  waiting for transfers between devices  730 us (57%)
  other arithmetic  201 us (16%)
  blocking collectives  124 us (10%)
  matrix products  123 us (10%)
  local copies, waits for them, and re-layouts  84.4 us (7%)
  between operations  16.8 us (1%)
    reduce_scatter x4, waiting for transfers between devices, narrow(): return lax.psum_scatter(term, 'width', scatter_dimension=1, tiled=True)  420 us
    all_gather x4, waiting for transfers between devices, widen(): return lax.all_gather(piece_low, 'width', axis=1, tiled=True)  204 us
    psum x4, blocking collectives, norm_sums(): return lax.psum((totals, squares), 'width')  76.3 us
    add x25, other arithmetic, mix_step(): return running + mix[depth_at] * history[depth_at].astype(jnp.float32)  59.5 us
    reduce_sum x25, other arithmetic, mix_grad(): jnp.sum(history[depth_at].astype(jnp.float32) * grad_columns)  53.6 us
    reduce_scatter x1, waiting for transfers between devices, on_device(): lax.psum_scatter(grad_reduce, 'rows', scatter_dimension=1, tiled=True)  41 us
    unnamed x16, waiting for transfers between devices  40.6 us
    dynamic_slice x25, local copies, waits for them, and re-layouts, mix_step(): return running + mix[depth_at] * history[depth_at].astype(jnp.float32)  31 us
  transfers between devices with their start and end apart: 14, of which 11 were waited for; matrix products, arithmetic and copies ran while one was open for 10% of the time, Pallas kernels for 0%

commit v1 on v0

v1 whole, which is shorter than its diff:
```python
import functools
import math
from types import SimpleNamespace

import jax
import jax.numpy as jnp
from jax import lax
from jax.experimental import pallas as pl
from jax.experimental.pallas import tpu as pltpu
from jax.sharding import PartitionSpec as P

D = 768
HEAD = 64
STEP = 10
HALO = 256
LANES = 128


EPS_NORM = 1e-05
EPS_ADAM = 1e-08
BETA_ONE = 0.9
BETA_TWO = 0.95
RATE_MATRIX = 0.02
RATE_OUTPUT = 0.12
RATE_GAIN = 0.4
RATE_MIX = 0.05
DECAY = 0.1
MASKED = -1e30

MESH = pl.DeviceIdType.MESH
F32 = jnp.float32
BF16 = jnp.bfloat16
MIB = 1 << 20


def optimize(weight, gradient, first_moment, second_moment, rate, decay):
    first_moment = BETA_ONE * first_moment + (1.0 - BETA_ONE) * gradient
    second_moment = BETA_TWO * second_moment + (1.0 - BETA_TWO) * gradient * gradient
    first_fixed = first_moment / (1.0 - BETA_ONE**STEP)
    second_fixed = second_moment / (1.0 - BETA_TWO**STEP)
    weight = weight - rate * (first_fixed / (jnp.sqrt(second_fixed) + EPS_ADAM) + decay * weight)
    return (weight, first_moment, second_moment)


def flip(index, bit):
    return index + bit - 2 * bit * ((index // bit) % 2)


def flips(index, bits):
    for bit in bits:
        index = flip(index, bit)
    return index


def subsets(bits):
    found = [()]
    for bit in bits:
        found = found + [one + (bit,) for one in found]
    return found


def row_bits(rows):
    digits = [1 << place for place in range(rows.bit_length() - 1)]
    return digits[0], digits[1:]


def tiles(count, body):
    def step(at, carry):
        body(at)
        return carry

    lax.fori_loop(0, count, step, 0)


def lane_tile(at, size=LANES, base=0):
    return pl.ds(pl.multiple_of(base + at * size, LANES), size)


def dot(a, b):
    return jnp.dot(a, b, preferred_element_type=F32)


def dot_rows(a, b):
    return lax.dot_general(a, b, (((1,), (1,)), ((), ())), preferred_element_type=F32)


def dot_cols(a, b):
    return lax.dot_general(a, b, (((0,), (0,)), ((), ())), preferred_element_type=F32)


def greet(z, r, width, bits):
    bar = pltpu.get_barrier_semaphore()
    places = [(r, lax.rem(z + k, width)) for k in range(1, width)] + [(flip(r, b), z) for b in bits]
    for place in places:
        pl.semaphore_signal(bar, inc=1, device_id=place, device_id_type=MESH)
    pl.semaphore_wait(bar, len(places))


class Sends:
    def __init__(self, send, recv):
        self.send, self.recv, self.used = send, recv, 0

    def make(self, src, dst, place):
        at = self.used
        self.used += 1
        return pltpu.make_async_remote_copy(
            src_ref=src, dst_ref=dst, send_sem=self.send.at[at], recv_sem=self.recv.at[at],
            device_id=place, device_id_type=MESH,
        )


class Gather:
    def __init__(self, sends, own, full, z, r, width, rows):
        self.core, self.bits = row_bits(rows)
        shard = own.shape[0]
        self.full, self.own, self.z, self.r, self.shard = full, own, z, r, shard

        def block(index):
            return pl.ds(pl.multiple_of(index * shard, 16), shard)

        self.block = block
        self.over_width = [
            sends.make(own, full.at[z, block(r)], (r, lax.rem(z + k, width))) for k in range(1, width)
        ]
        half = width // 2
        self.steps = []
        for step in range(len(self.bits)):
            here = []
            for start, order in ((0, self.bits), (half, self.bits[::-1])):
                for sub in subsets(order[:step]):
                    part = full.at[pl.ds(start, half), block(flips(r, sub))]
                    here.append(sends.make(part, part, (flip(r, order[step]), z)))
            self.steps.append(here)
        last = []
        for sub in subsets(self.bits):
            part = full.at[:, block(flips(r, sub))]
            last.append(sends.make(part, part, (flip(r, self.core), z)))
        self.steps.append(last)

    def start(self):
        for copy in self.over_width:
            copy.start()
        self.full[self.z, self.block(self.r), :] = self.own[...]

    def advance(self, step):
        for copy in self.over_width if step == 0 else self.steps[step - 1]:
            copy.wait_recv()
        if step < len(self.steps):
            for copy in self.steps[step]:
                copy.start()

    def end(self):
        for copy in self.over_width + [one for step in self.steps for one in step]:
            copy.wait_send()

    @staticmethod
    def copies(width, rows):
        bits = rows.bit_length() - 2
        return width - 1 + sum(2 * 2**step for step in range(bits)) + 2**bits


class Scatter:
    def __init__(self, sends, grads, boxes, last_box, final, total, z, r, width, rows):
        self.core, self.bits = row_bits(rows)
        shard = total.shape[0]
        self.grads, self.boxes, self.last_box, self.final, self.total = grads, boxes, last_box, final, total
        self.z, self.width, self.shard = z, width, shard
        half = width // 2
        self.half = half

        def block(index):
            return pl.ds(pl.multiple_of(index * shard, 16), shard)

        self.block = block
        self.r = r
        other = flip(r, self.core)
        self.places = subsets(self.bits)
        self.steps = [
            [
                sends.make(grads.at[:, block(flips(other, sub))], boxes[0].at[at], (other, z))
                for at, sub in enumerate(self.places)
            ]
        ]
        self.where = [{(h, sub): boxes[0].at[at, pl.ds(h * half, half)] for at, sub in enumerate(self.places) for h in (0, 1)}]
        self.box_refs = [None]
        self.orders = (self.bits, self.bits[::-1])
        for step in range(len(self.bits)):
            here, kept, plan = [], {}, []
            for h, order in enumerate(self.orders):
                bit = order[step]
                for at, sub in enumerate(subsets(order[step + 1 :])):
                    far = tuple(sorted(sub + (bit,)))
                    near = tuple(sorted(sub))
                    slot = boxes[step + 1].at[h, at]
                    here.append(sends.make(self.where[step][(h, far)], slot, (flip(r, bit), z)))
                    plan.append((slot, self.where[step][(h, near)], h))
                    kept[(h, near)] = slot
            self.steps.append(here)
            self.where.append(kept)
            self.box_refs.append(plan)
        self.over_width = [
            sends.make(final.at[lax.rem(z + k, width)], last_box.at[k - 1], (r, lax.rem(z + k, width)))
            for k in range(1, width)
        ]

    def start(self):
        for copy in self.steps[0]:
            copy.start()

    def advance(self, step):
        for copy in self.steps[step]:
            copy.wait_recv()
        if step == 0:
            for at, sub in enumerate(self.places):
                rows = self.block(flips(self.r, sub))

                def add(w, at=at, rows=rows):
                    box = self.boxes[0].at[at, w]
                    box[...] = (box[...].astype(F32) + self.grads[w, rows, :].astype(F32)).astype(BF16)

                tiles(self.width, add)
        else:
            is_last = step == len(self.bits)
            for slot, kept, h in self.box_refs[step]:
                for w in range(self.half):
                    value = slot[w].astype(F32) + kept[w].astype(F32)
                    if is_last:
                        self.final[h * self.half + w] = value.astype(BF16)
                    else:
                        slot[w] = value.astype(BF16)
        following = self.over_width if step == len(self.bits) else self.steps[step + 1]
        for copy in following:
            copy.start()

    def finish(self):
        for copy in self.over_width:
            copy.wait_recv()
        value = self.final[self.z].astype(F32)
        for k in range(self.width - 1):
            value = value + self.last_box[k].astype(F32)
        self.total[...] = value

    def end(self):
        for copy in self.over_width + [one for step in self.steps for one in step]:
            copy.wait_send()

    @staticmethod
    def copies(width, rows):
        bits = rows.bit_length() - 2
        return width - 1 + sum(2 * 2 ** (bits - 1 - step) for step in range(bits)) + 2**bits

    @staticmethod
    def box_shapes(width, rows, shard):
        bits = rows.bit_length() - 2
        shapes = [(2**bits, width, shard, D)]
        for step in range(bits):
            shapes.append((2, 2 ** (bits - 1 - step), width // 2, shard, D))
        return shapes


def mix_stream(mix_ref, pair_ref, out_ref, base, layers):
    features, size = pair_ref.shape[1], pair_ref.shape[2]
    strip = 16

    def body(at):
        rows = pl.ds(pl.multiple_of(at * strip, strip), strip)
        total = mix_ref[0] * pair_ref[0, rows, :].astype(F32)
        for j in range(1, layers):
            total = total + mix_ref[j] * pair_ref[j, rows, :].astype(F32)
        out_ref[rows, base] = total.astype(BF16)

    tiles(features // strip, body)


def spread_gains(box_ref, gain_ref, width, piece):
    for w in range(width):
        for i in range(2):
            row = box_ref[w, pl.ds(i, 1), :]
            full = jnp.transpose(jnp.broadcast_to(row, (LANES, row.shape[1])))
            gain_ref[i, pl.ds(w * piece, piece), :] = full[:piece]


def norm_forward(x_ref, x_base, gain_ref, i, out_ref, stat_ref, count):
    def body(at):
        cols = lane_tile(at)
        x = x_ref[:, lane_tile(at, base=x_base)].astype(F32)
        centre = jnp.sum(x, 0, keepdims=True) / D
        spread = jnp.sum(x * x, 0, keepdims=True) / D - centre * centre
        scaling = lax.rsqrt(spread + EPS_NORM)
        out_ref[:, cols] = (gain_ref[i] * ((x - centre) * scaling)).astype(BF16)
        stat_ref[0:1, cols] = centre
        stat_ref[1:2, cols] = scaling

    tiles(count // LANES, body)


def norm_back(u_ref, u_base, x_ref, x_base, stat_ref, stat_base, gain_ref, i, residual, write, gain_acc, count):
    gain_acc[...] = jnp.zeros_like(gain_acc)

    def body(at):
        u = u_ref[:, lane_tile(at, base=u_base)].astype(F32)
        x = x_ref[:, lane_tile(at, base=x_base)].astype(F32)
        cols = lane_tile(at, base=stat_base)
        scaling = stat_ref[1:2, cols]
        centred = (x - stat_ref[0:1, cols]) * scaling
        gain_acc[...] += u * centred
        s = u * gain_ref[i]
        mean_s = jnp.sum(s, 0, keepdims=True) / D
        mean_c = jnp.sum(s * centred, 0, keepdims=True) / D
        write(lane_tile(at), residual(lane_tile(at)) + scaling * (s - mean_s - centred * mean_c))

    tiles(count // LANES, body)


def document_starts(seg_ref, start_ref, trig_ref, row, own_at, own):
    seg = seg_ref[pl.ds(row, 1), :]
    length = seg.shape[1]
    place = lax.broadcasted_iota(jnp.int32, (8, length), 1)
    seg = jnp.broadcast_to(seg, (8, length))
    before = pltpu.roll(seg, 1, 1)
    start = jnp.where((place > 0) & (seg == before), 0, place)
    step = 1
    while step < length:
        moved = pltpu.roll(start, step, 1)
        start = jnp.maximum(start, jnp.where(place >= step, moved, 0))
        step *= 2
    position = (place - start).astype(F32)
    scratch = start_ref.at[0:8]
    ext = HALO + own
    scratch[:, pl.ds(0, HALO)] = jnp.zeros((8, HALO), F32)
    scratch[:, pl.ds(HALO, length)] = position
    window = scratch[:, pl.ds(pl.multiple_of(own_at, LANES), ext)][0:1]
    half = HEAD // 2
    freq = jnp.exp(
        lax.broadcasted_iota(jnp.int32, (half, ext), 0).astype(F32) * (-2.0 * math.log(10000.0) / HEAD)
    )
    angle = freq * window
    trig_ref[0] = jnp.cos(angle)
    trig_ref[1] = jnp.sin(angle)
    scratch[:, pl.ds(HALO, length)] = start.astype(F32)
    kept = scratch[:, pl.ds(pl.multiple_of(own_at, LANES), ext)]
    scratch[:, pl.ds(0, ext)] = kept - (own_at - HALO).astype(F32)


def rotated(heads, cosine, sine):
    half = HEAD // 2
    a, b = heads[:half], heads[half:]
    return jnp.concatenate([a * cosine - b * sine, b * cosine + a * sine], 0)


def project(x_ref, wa_ref, trig_ref, q_ref, k_ref, v_ref, wo_ref, width, per, own):
    ext = HALO + own
    group = per * HEAD
    scale = HEAD**-0.5

    def body(w):
        turned = jnp.transpose(wa_ref[w])
        wo_ref[w] = turned[3 * group :]
        queries = dot(turned[:group], x_ref[:, HALO:])
        cosine, sine = trig_ref[0], trig_ref[1]
        for i in range(per):
            rows = queries[i * HEAD : (i + 1) * HEAD]
            q_ref[w * per + i] = (rotated(rows, cosine[:, HALO:], sine[:, HALO:]).astype(BF16) * scale).astype(BF16)
        keys = dot(turned[group : 2 * group], x_ref[...])
        for i in range(per):
            rows = keys[i * HEAD : (i + 1) * HEAD]
            k_ref[w * per + i] = rotated(rows, cosine, sine).astype(BF16)
        values = dot(turned[2 * group : 3 * group], x_ref[...])
        for i in range(per):
            v_ref[w * per + i] = values[i * HEAD : (i + 1) * HEAD].astype(BF16)

    tiles(width, body)


def attend(q_ref, k_ref, v_ref, start_ref, bias_ref, p_ref, ao_ref, width, per, own):
    blocks = own // HALO
    for b in range(blocks):
        key_at = lax.broadcasted_iota(jnp.int32, (2 * HALO, HALO), 0).astype(F32) + float(b * HALO)
        query_at = lax.broadcasted_iota(jnp.int32, (2 * HALO, HALO), 1).astype(F32) + float((b + 1) * HALO)
        first = start_ref[0:1, (b + 1) * HALO : (b + 2) * HALO]
        bias_ref[b] = jnp.where((key_at >= first) & (key_at <= query_at), 0.0, MASKED)

    def body(w):
        ao_ref[w, 0:HEAD, :] = jnp.zeros((HEAD, own), BF16)
        for i in range(per):
            h = w * per + i
            for b in range(blocks):
                keys = k_ref[h, :, b * HALO : (b + 2) * HALO]
                scores = dot_cols(keys, q_ref[h, :, b * HALO : (b + 1) * HALO]) + bias_ref[b]
                top = jnp.max(scores, 0, keepdims=True)
                raised = jnp.exp(scores - top)
                total = jnp.sum(raised, 0, keepdims=True)
                p_ref[h, b] = (raised * (1.0 / total)).astype(BF16)
                out = dot(v_ref[h, :, b * HALO : (b + 2) * HALO], p_ref[h, b])
                ao_ref[w, (i + 1) * HEAD : (i + 2) * HEAD, b * HALO : (b + 1) * HALO] = out.astype(BF16)

    tiles(width, body)


def out_project(st_ref, wa_ref, ao_ref, mid_ref, width, per):
    group = 3 * per * HEAD - HEAD
    mid_ref[...] = st_ref[:, HALO:].astype(F32)

    def body(w):
        mid_ref[...] += dot(wa_ref[w, :, group:], ao_ref[w])

    tiles(width, body)


def feed_forward(x_ref, ct_ref, wb_ref, wc_ref, gb_ref, gc_ref, acc_ref, u_ref, xt_ref, ctt_ref, pre_ref, gh_ref, hid_ref, gi_ref, width):
    own = x_ref.shape[1]
    xt_ref[...] = jnp.transpose(x_ref[...])
    ctt_ref[...] = jnp.transpose(ct_ref[...])
    u_ref[...] = jnp.zeros_like(u_ref)
    strip = 32

    def body(w):
        pre_ref[...] = dot(xt_ref[...], wb_ref[w])
        gh_ref[...] = dot(ctt_ref[...], wc_ref[w])

        def gelu(at):
            rows = pl.ds(pl.multiple_of(at * strip, strip), strip)
            x = pre_ref[rows, :]
            root = math.sqrt(2.0 / math.pi)
            square = x * x
            bent = jnp.tanh(root * (x + 0.044715 * (square * x)))
            hid_ref[rows, :] = (0.5 * x * (1.0 + bent)).astype(BF16)
            slope = 0.5 * (1.0 + bent) + (0.5 * root) * x * (1.0 - bent * bent) * (1.0 + (3 * 0.044715) * square)
            gi_ref[rows, :] = (gh_ref[rows, :] * slope).astype(BF16)

        tiles(own // strip, gelu)
        acc_ref[...] += dot_rows(wc_ref[w], hid_ref[...])
        gc_ref[w] = dot(ct_ref[...], hid_ref[...]).astype(BF16)
        u_ref[...] += dot_rows(wb_ref[w], gi_ref[...])
        gb_ref[w] = dot(x_ref[...], gi_ref[...]).astype(BF16)

    tiles(width, body)


def attend_back(low_ref, wo_ref, p_ref, q_ref, k_ref, v_ref, trig_ref, gp_ref, width, per, own):
    ext = HALO + own
    group = per * HEAD
    blocks = own // HALO
    scale = HEAD**-0.5

    def body(w):
        gp_ref[w, 3 * group :, :] = jnp.zeros((group, ext), BF16)
        gp_ref[w, :group, :HALO] = jnp.zeros((group, HALO), BF16)
        upstream = dot(wo_ref[w], low_ref[...]).astype(BF16)
        for i in range(per):
            h = w * per + i
            grad_keys, grad_values = [None] * (blocks + 1), [None] * (blocks + 1)
            for b in range(blocks):
                q = q_ref[h, :, b * HALO : (b + 1) * HALO]
                k = k_ref[h, :, b * HALO : (b + 2) * HALO]
                v = v_ref[h, :, b * HALO : (b + 2) * HALO]
                up = upstream[i * HEAD : (i + 1) * HEAD, b * HALO : (b + 1) * HALO]
                weights = p_ref[h, b]
                wide = weights.astype(F32)
                grad_weights = dot_cols(v, up)
                inner = jnp.sum(wide * grad_weights, 0, keepdims=True)
                grad_scores = (wide * (grad_weights - inner)).astype(BF16)
                gv = dot_rows(up, weights)
                gk = dot_rows(q, grad_scores)
                gq = dot(k, grad_scores) * scale
                cols = slice((b + 1) * HALO, (b + 2) * HALO)
                gp_ref[w, i * HEAD : (i + 1) * HEAD, cols] = rotated(gq, trig_ref[0, :, cols], -trig_ref[1, :, cols]).astype(BF16)
                for part in range(2):
                    piece = slice(part * HALO, (part + 1) * HALO)
                    at = b + part
                    grad_keys[at] = gk[:, piece] if grad_keys[at] is None else grad_keys[at] + gk[:, piece]
                    grad_values[at] = gv[:, piece] if grad_values[at] is None else grad_values[at] + gv[:, piece]
            for at in range(blocks + 1):
                cols = slice(at * HALO, (at + 1) * HALO)
                gp_ref[w, group + i * HEAD : group + (i + 1) * HEAD, cols] = rotated(
                    grad_keys[at], trig_ref[0, :, cols], -trig_ref[1, :, cols]
                ).astype(BF16)
                gp_ref[w, 2 * group + i * HEAD : 2 * group + (i + 1) * HEAD, cols] = grad_values[at].astype(BF16)

    tiles(width, body)


def project_back(x_ref, low_ref, ao_ref, wa_ref, gp_ref, ga_ref, u_ref, width, per):
    group = 3 * per * HEAD - HEAD
    u_ref[...] = jnp.zeros_like(u_ref)

    def body(w):
        u_ref[...] += dot(wa_ref[w], gp_ref[w])
        ga_ref[w, :, :group] = dot_rows(x_ref[...], gp_ref[w, :group, :]).astype(BF16)
        ga_ref[w, :, group:] = (
            dot_rows(x_ref[...], gp_ref[w, group:, :]) + dot_rows(low_ref[...], ao_ref[w])
        ).astype(BF16)

    tiles(width, body)


def bring_kernel(width, rows, mix_ref, hist_ref, cot_ref, own_ref, box_ref, st_ref, ct_ref, full_ref, boxes_ref,
                 pair, mixed, load_sem, here_sem, send_sem, recv_sem):
    r, z = lax.axis_index("rows"), lax.axis_index("width")
    layers, piece, tokens = hist_ref.shape
    own = tokens // width
    _, bits = row_bits(rows)
    greet(z, r, width, [1] + bits)
    sends = Sends(send_sem, recv_sem)
    gathers = []
    if own_ref is not None:
        gathers = [Gather(sends, own_ref.at[x], full_ref.at[x], z, r, width, rows) for x in range(3)]
    first = 1 - z // 2
    chunks = []
    for at in range(width):
        low = flip(first, 1) if at // 2 else first
        chunks.append(2 * low + at % 2)
    loads = []
    for at in range(width):
        cols = pl.ds(pl.multiple_of(chunks[at] * own, LANES), own)
        load = pltpu.make_async_copy(hist_ref.at[:, :, cols], pair.at[at], load_sem.at[at])
        load.start()
        loads.append(load)
    if gathers:
        gathers[0].start()
    mine = pl.ds(pl.multiple_of(z * piece, 16), piece)
    st_even = st_ref.at[mine, pl.ds(HALO, own)]
    st_odd = st_ref.at[mine, :]
    gain_sends = [sends.make(box_ref, boxes_ref.at[z], (r, lax.rem(z + k, width))) for k in range(1, width)]
    for copy in gain_sends:
        copy.start()
    boxes_ref[z] = box_ref[...]
    base = sends.used
    sends.used += width - 1

    def stream_copy(k, target, odd, start):
        if odd:
            src = mixed.at[:, pl.ds(pl.multiple_of(start - HALO, LANES), HALO + own)]
            dst = st_odd
        else:
            src = mixed.at[:, pl.ds(pl.multiple_of(start, LANES), own)]
            dst = st_even
        return pltpu.make_async_remote_copy(
            src_ref=src, dst_ref=dst, send_sem=send_sem.at[base + k - 1], recv_sem=recv_sem.at[base + k - 1],
            device_id=(r, target), device_id_type=MESH,
        )

    for at in range(width):
        target = chunks[at]
        start = pl.multiple_of(target * own, LANES)
        loads[at].wait()
        mix_stream(mix_ref, pair.at[at], mixed, pl.ds(start, own), layers)
        odd = at % 2 == 1
        for k in range(1, width):
            @pl.when(lax.rem(z + k, width) == target)
            def _(k=k, target=target, odd=odd, start=start):
                stream_copy(k, target, odd, start).start()

        @pl.when(target == z)
        def _(odd=odd, start=start):
            if odd:
                st_odd[...] = mixed[:, pl.ds(pl.multiple_of(start - HALO, LANES), HALO + own)]
            else:
                st_even[...] = mixed[:, pl.ds(start, own)]
                st_ref[:, 0:HALO] = jnp.zeros((D, HALO), BF16)

    for gather in gathers[1:]:
        gather.start()
    cot_sends = []
    for k in range(1, width):
        target = lax.rem(z + k, width)
        cols = pl.ds(pl.multiple_of(target * own, LANES), own)
        cot_sends.append(sends.make(cot_ref.at[:, cols], ct_ref.at[mine, :], (r, target)))
    for copy in cot_sends:
        copy.start()
    cot_here = pltpu.make_async_copy(
        cot_ref.at[:, pl.ds(pl.multiple_of(z * own, LANES), own)], ct_ref.at[mine, :], here_sem
    )
    cot_here.start()
    for step in range(len(bits) + 2):
        for gather in gathers:
            gather.advance(step)
    for k in range(1, width):
        for odd in (False, True):
            @pl.when(lax.rem(z, 2) == int(odd))
            def _(k=k, odd=odd):
                stream_copy(k, lax.rem(z + k, width), odd, HALO if odd else 0).wait_recv()

            @pl.when(lax.rem(z + k, 2) == int(odd))
            def _(k=k, odd=odd):
                stream_copy(k, lax.rem(z + k, width), odd, HALO if odd else 0).wait_send()
    cot_here.wait()
    for copy in gain_sends + cot_sends:
        copy.wait()
    for gather in gathers:
        gather.end()


def middle_kernel(width, per, seg_ref, st_ref, ct_ref, full_ref, boxes_ref,
                  blk_ref, gmid_ref, u_ref, ga_ref, gb_ref, gc_ref, gain_ref, gacc_ref, stat_ref,
                  x_ref, start_ref, trig, q_ref, k_ref, v_ref, wo_ref, bias, prob, ao, mid, stat_two, u_two, low):
    z = lax.axis_index("width")
    own = ct_ref.shape[1]
    per_row = seg_ref.shape[1] // own
    spread_gains(boxes_ref, gain_ref, width, D // width)
    document_starts(seg_ref, start_ref, trig, z // per_row, lax.rem(z, per_row) * own, own)
    norm_forward(st_ref, 0, gain_ref, 0, x_ref, stat_ref, HALO + own)
    project(x_ref, full_ref.at[0], trig, q_ref, k_ref, v_ref, wo_ref, width, per, own)
    attend(q_ref, k_ref, v_ref, start_ref, bias, prob, ao, width, per, own)
    out_project(st_ref, full_ref.at[0], ao, mid, width, per)
    gmid_ref[...] = mid[...]

    def inner(x_two, xt, ctt, pre, gh, hid, gi):
        norm_forward(mid, 0, gain_ref, 1, x_two, stat_two, own)
        feed_forward(x_two, ct_ref, full_ref.at[1], full_ref.at[2], gb_ref, gc_ref, gmid_ref, u_two, xt, ctt, pre, gh, hid, gi, width)

    pl.run_scoped(
        inner, pltpu.VMEM((D, own), BF16), pltpu.VMEM((own, D), BF16), pltpu.VMEM((own, D), BF16), pltpu.VMEM((own, D), F32),
        pltpu.VMEM((own, D), F32), pltpu.VMEM((own, D), BF16), pltpu.VMEM((own, D), BF16),
    )
    blk_ref[...] = gmid_ref[...].astype(BF16)

    def write(cols, value):
        gmid_ref[:, cols] = value
        low[:, cols] = value.astype(BF16)

    norm_back(u_two, 0, mid, 0, stat_two, 0, gain_ref, 1, lambda cols: ct_ref[:, cols].astype(F32), write, gacc_ref, own)

    def last(gp):
        attend_back(low, wo_ref, prob, q_ref, k_ref, v_ref, trig, gp, width, per, own)
        project_back(x_ref, low, ao, full_ref.at[0], gp, ga_ref, u_ref, width, per)

    pl.run_scoped(last, pltpu.VMEM((width, 4 * per * HEAD, HALO + own), BF16))


def return_kernel(width, rows, mix_ref, hist_ref, u_ref, gmid_ref, st_ref, stat_ref, gain_ref, gtwo_ref, blk_ref,
                  ga_ref, gb_ref, gc_ref, hgrad_ref, bout_ref, total_ref, small_ref,
                  pair, uh, halo_out, halo_in, gs, gcol, gone, macc, small_out, small_in, small_step,
                  final, last_box, boxes, load_sem, store_sem, here_sem, send_sem, recv_sem):
    r, z = lax.axis_index("rows"), lax.axis_index("width")
    layers, piece, tokens = hist_ref.shape
    own = tokens // width
    core, bits = row_bits(rows)
    greet(z, r, width, [1] + bits)
    sends = Sends(send_sem, recv_sem)
    loads, order = [], []
    for k in range(width):
        chunk = lax.rem(z + width - k, width)
        cols = pl.ds(pl.multiple_of(chunk * own, LANES), own)
        load = pltpu.make_async_copy(hist_ref.at[:, :, cols], pair.at[k], load_sem.at[k])
        load.start()
        loads.append(load)
        order.append(cols)
    scatters = []
    if total_ref is not None:
        scatters = [
            Scatter(sends, grads, [box.at[x] for box in boxes], last_box.at[x], final.at[x], total_ref.at[x], z, r, width, rows)
            for x, grads in ((2, gc_ref), (1, gb_ref), (0, ga_ref))
        ]
    odd = lax.rem(z, 2) == 1
    halo = sends.make(halo_out, halo_in, (r, flip(z, 1)))

    @pl.when(odd)
    def _():
        halo_out[...] = u_ref[:, 0:HALO].astype(BF16)
        halo.start()

    for scatter in scatters:
        scatter.start()
    uh[...] = u_ref[:, HALO:]

    @pl.when(jnp.logical_not(odd))
    def _():
        halo.wait_recv()
        uh[:, own - HALO : own] += halo_in[...].astype(F32)

    def write(cols, value):
        gs[:, cols] = value.astype(BF16)

    norm_back(uh, 0, st_ref, HALO, stat_ref, HALO, gain_ref, 0, lambda cols: gmid_ref[:, cols], write, gone, own)
    gs_sends, blk_sends = [], []
    mine = pl.ds(pl.multiple_of(z * own, LANES), own)
    for k in range(1, width):
        target = lax.rem(z + k, width)
        part = pl.ds(pl.multiple_of(target * piece, 16), piece)
        gs_sends.append(sends.make(gs.at[part, :], gcol.at[k], (r, target)))
        blk_sends.append(sends.make(blk_ref.at[part, :], bout_ref.at[:, mine], (r, target)))
    for copy in gs_sends + blk_sends:
        copy.start()
    part = pl.ds(pl.multiple_of(z * piece, 16), piece)
    bout_ref[:, mine] = blk_ref[part, :]
    gcol[0] = gs[part, :]
    macc[...] = jnp.zeros_like(macc)
    strip = 16
    stores = []
    for k in range(width):
        if k:
            gs_sends[k - 1].wait_recv()
        loads[k].wait()

        def body(at, k=k):
            cut = pl.ds(pl.multiple_of(at * strip, strip), strip)
            g = gcol[k, cut, :].astype(F32)
            for j in range(layers):
                crossed = pair[k, j, cut, :].astype(F32) * g
                folded = crossed[:8] + crossed[8:]
                part = folded[:, :LANES]
                for lane in range(1, own // LANES):
                    part = part + folded[:, lane * LANES : (lane + 1) * LANES]
                macc[j] += part
                pair[k, j, cut, :] = (mix_ref[j] * g).astype(BF16)

        tiles(piece // strip, body)
        store = pltpu.make_async_copy(pair.at[k], hgrad_ref.at[:, :, order[k]], store_sem.at[k])
        store.start()
        stores.append(store)
        if k <= len(bits):
            for scatter in scatters:
                scatter.advance(k)
    for step in range(width, len(bits) + 1):
        for scatter in scatters:
            scatter.advance(step)
    small_out[...] = jnp.zeros_like(small_out)
    first = jnp.sum(jnp.transpose(gone[...]), 0, keepdims=True)
    second = jnp.sum(jnp.transpose(gtwo_ref[...]), 0, keepdims=True)
    summed = jnp.sum(macc[...], 1)
    depth = jnp.sum(jnp.transpose(summed), 0, keepdims=True)
    for w in range(width):
        small_out[w, 0:1, 0:piece] = first[:, w * piece : (w + 1) * piece]
        small_out[w, 1:2, 0:piece] = second[:, w * piece : (w + 1) * piece]
        small_out[w, 2:3, 0 : depth.shape[1]] = depth
    small_sends = [
        sends.make(small_out.at[lax.rem(z + k, width)], small_in.at[k - 1], (r, lax.rem(z + k, width))) for k in range(1, width)
    ]
    for copy in small_sends:
        copy.start()
    current = small_out[z]
    for k in range(1, width):
        small_sends[k - 1].wait_recv()
        current = current + small_in[k - 1]
    for at, bit in enumerate([core] + bits):
        small_step[at, 0] = current
        copy = sends.make(small_step.at[at, 0], small_step.at[at, 1], (flip(r, bit), z))
        copy.start()
        copy.wait_recv()
        current = current + small_step[at, 1]
        small_sends.append(copy)
    small_ref[...] = current
    for scatter in scatters:
        scatter.finish()
    for copy in blk_sends:
        copy.wait_recv()
    for copy in gs_sends + blk_sends + small_sends:
        copy.wait_send()

    @pl.when(odd)
    def _():
        halo.wait_send()

    for scatter in scatters:
        scatter.end()
    for store in stores:
        store.wait()


def vmem(count):
    return [pl.BlockSpec(memory_space=pltpu.VMEM)] * count


def shape(*sizes, dtype=F32):
    return jax.ShapeDtypeStruct(sizes, dtype)


def bring(width, rows, mix, history, cotangent, own_three, box):
    layers, piece, tokens = history.shape
    own = tokens // width
    inside = own_three.shape[1] % 16 == 0
    count = (width - 1) * 3 + 3 * Gather.copies(width, rows) + 4
    any_space = pl.BlockSpec(memory_space=pl.ANY)
    outs = [shape(D, HALO + own, dtype=BF16), shape(D, own, dtype=BF16), shape(width, 8, 2 * LANES)]
    if inside:
        outs.append(shape(3, width, D, D, dtype=BF16))

    def kernel(mix_ref, hist_ref, cot_ref, own_ref, box_ref, st, ct, boxes, *rest):
        full, rest = (rest[0], rest[1:]) if inside else (None, rest)
        bring_kernel(width, rows, mix_ref, hist_ref, cot_ref, own_ref if inside else None, box_ref, st, ct, full, boxes, *rest)

    found = pl.pallas_call(
        kernel,
        out_shape=outs,
        in_specs=[pl.BlockSpec(memory_space=pltpu.SMEM), any_space] + vmem(3),
        out_specs=vmem(len(outs)),
        scratch_shapes=[
            pltpu.VMEM((width, layers, piece, own), BF16),
            pltpu.VMEM((piece, tokens), BF16),
            pltpu.SemaphoreType.DMA((width,)),
            pltpu.SemaphoreType.DMA,
            pltpu.SemaphoreType.DMA((count,)),
            pltpu.SemaphoreType.DMA((count,)),
        ],
        compiler_params=pltpu.CompilerParams(collective_id=0, has_side_effects=True, vmem_limit_bytes=60 * MIB),
    )(mix, history, cotangent, own_three, box)
    if inside:
        return found
    full = lax.all_gather(lax.all_gather(own_three, "rows", axis=1, tiled=True), "width", axis=1)
    return (*found, full)


def middle(width, segments, st, ct, boxes, full):
    own = ct.shape[1]
    ext = HALO + own
    heads = D // HEAD
    per = heads // width
    group = per * HEAD
    blocks = own // HALO
    outs = [
        shape(D, own, dtype=BF16), shape(D, own), shape(D, ext),
        shape(width, D, D, dtype=BF16), shape(width, D, D, dtype=BF16), shape(width, D, D, dtype=BF16),
        shape(2, D, LANES), shape(D, LANES), shape(8, ext),
    ]
    scratch = [
        pltpu.VMEM((D, ext), BF16), pltpu.VMEM((8, HALO + segments.shape[1]), F32), pltpu.VMEM((2, HEAD // 2, ext), F32),
        pltpu.VMEM((heads, HEAD, own), BF16), pltpu.VMEM((heads, HEAD, ext), BF16), pltpu.VMEM((heads, HEAD, ext), BF16),
        pltpu.VMEM((width, group, D), BF16), pltpu.VMEM((blocks, 2 * HALO, HALO), F32),
        pltpu.VMEM((heads, blocks, 2 * HALO, HALO), BF16), pltpu.VMEM((width, HEAD + group, own), BF16),
        pltpu.VMEM((D, own), F32), pltpu.VMEM((8, own), F32), pltpu.VMEM((D, own), F32), pltpu.VMEM((D, own), BF16),
    ]
    return pl.pallas_call(
        functools.partial(middle_kernel, width, per),
        out_shape=outs,
        in_specs=vmem(5),
        out_specs=vmem(len(outs)),
        scratch_shapes=scratch,
        compiler_params=pltpu.CompilerParams(vmem_limit_bytes=62 * MIB),
    )(segments, st, ct, full, boxes)


def give_back(width, rows, shard, mix, history, u, gmid, st, stat, gain, gtwo, blk, ga, gb, gc):
    layers, piece, tokens = history.shape
    own = tokens // width
    inside = shard % 16 == 0
    row_digits = rows.bit_length() - 1
    count = 3 * Scatter.copies(width, rows) + 1 + 3 * (width - 1) + row_digits
    any_space = pl.BlockSpec(memory_space=pl.ANY)
    outs = [shape(*history.shape, dtype=BF16), shape(piece, tokens, dtype=BF16), shape(8, 2 * LANES)]
    specs = [any_space] + vmem(2)
    box_shapes = []
    if inside:
        outs.append(shape(3, shard, D))
        specs += vmem(1)
        box_shapes = Scatter.box_shapes(width, rows, shard)
    ins = [mix, history, u, gmid, st, stat, gain, gtwo, blk] + ([ga, gb, gc] if inside else [])

    def kernel(*refs):
        given, rest = refs[: len(ins)], refs[len(ins) :]
        hgrad, bout, small = rest[:3]
        rest = rest[3:]
        total, grads = None, (None, None, None)
        final, last_box, boxes = None, None, ()
        if inside:
            total, rest = rest[0], rest[1:]
            grads = given[9:]
        common, rest = rest[:11], rest[11:]
        if inside:
            final, last_box = rest[:2]
            boxes = rest[2 : 2 + len(box_shapes)]
            rest = rest[2 + len(box_shapes) :]
        return_kernel(width, rows, *given[:9], *grads, hgrad, bout, total, small, *common, final, last_box, boxes, *rest)

    scratch = [
        pltpu.VMEM((width, layers, piece, own), BF16),
        pltpu.VMEM((D, own), F32),
        pltpu.VMEM((D, HALO), BF16),
        pltpu.VMEM((D, HALO), BF16),
        pltpu.VMEM((D, own), BF16),
        pltpu.VMEM((width, piece, own), BF16),
        pltpu.VMEM((D, LANES), F32),
        pltpu.VMEM((layers, 8, LANES), F32),
        pltpu.VMEM((width, 8, 2 * LANES), F32),
        pltpu.VMEM((width - 1, 8, 2 * LANES), F32),
    ]
    scratch.append(pltpu.VMEM((row_digits, 2, 8, 2 * LANES), F32))
    if inside:
        scratch += [pltpu.VMEM((3, width, shard, D), BF16), pltpu.VMEM((3, width - 1, shard, D), BF16)]
        scratch += [pltpu.VMEM((3, *one), BF16) for one in box_shapes]
    scratch += [
        pltpu.SemaphoreType.DMA((width,)), pltpu.SemaphoreType.DMA((width,)), pltpu.SemaphoreType.DMA,
        pltpu.SemaphoreType.DMA((count,)), pltpu.SemaphoreType.DMA((count,)),
    ]
    found = pl.pallas_call(
        kernel,
        out_shape=outs,
        in_specs=[pl.BlockSpec(memory_space=pltpu.SMEM), any_space] + vmem(len(ins) - 2),
        out_specs=specs,
        scratch_shapes=scratch,
        compiler_params=pltpu.CompilerParams(collective_id=1, has_side_effects=True, vmem_limit_bytes=63 * MIB),
    )(*ins)
    if inside:
        return found
    total = lax.psum_scatter(jnp.stack([ga, gb, gc], 1), "width", scatter_dimension=0)
    return (*found, lax.psum_scatter(total, "rows", scatter_dimension=1, tiled=True).astype(F32))


def on_device(
    width, rows, history, cotangent, segments, w_attend, m_attend, v_attend, w_output, m_output, v_output,
    w_expand, m_expand, v_expand, w_reduce, m_reduce, v_reduce, gains, m_gains, v_gains, mix, m_mix, v_mix,
):
    layers, piece, _ = history.shape
    own_three = jnp.stack([
        jnp.concatenate([w_attend[0], w_attend[1], w_attend[2], jnp.transpose(w_output)], 1),
        w_expand,
        jnp.transpose(w_reduce),
    ]).astype(BF16)
    shard = own_three.shape[1]
    box = jnp.pad(gains, ((0, 8 - gains.shape[0]), (0, 2 * LANES - piece)))
    st, ct, boxes, full = bring(width, rows, mix, history, cotangent, own_three, box)
    blk, gmid, u, ga, gb, gc, gain, gtwo, stat = middle(width, segments, st, ct, boxes, full)
    history_grad, block_output, small, total = give_back(
        width, rows, shard, mix, history, u, gmid, st, stat, gain, gtwo, blk, ga, gb, gc
    )
    first = total[0]
    sum_attend = jnp.stack([first[:, k * piece : (k + 1) * piece] for k in range(3)])
    sum_output = jnp.transpose(first[:, 3 * piece :])
    new_attend = optimize(w_attend, sum_attend, m_attend, v_attend, RATE_MATRIX, DECAY)
    new_output = optimize(w_output, sum_output, m_output, v_output, RATE_OUTPUT, DECAY)
    new_expand = optimize(w_expand, total[1], m_expand, v_expand, RATE_MATRIX, DECAY)
    new_reduce = optimize(w_reduce, jnp.transpose(total[2]), m_reduce, v_reduce, RATE_MATRIX, DECAY)
    new_gains = optimize(gains, small[0:2, :piece], m_gains, v_gains, RATE_GAIN, 0.0)
    new_mix = optimize(mix, small[2, :layers], m_mix, v_mix, RATE_MIX, 0.0)
    return (block_output, history_grad, *new_attend, *new_output, *new_expand, *new_reduce, *new_gains, *new_mix)


def solution(mesh):
    square, tall, wide = P(None, "rows", "width"), P("width", "rows"), P("rows", "width")
    weights = (square,) * 3 + (tall,) * 3 + (wide,) * 3 + (tall,) * 3 + (P(None, "width"),) * 3 + (P(),) * 3
    return jax.shard_map(
        functools.partial(on_device, mesh.shape["width"], mesh.shape["rows"]),
        mesh=mesh,
        in_specs=(P(None, "width", "rows"), P("width", "rows"), P("rows", None)) + weights,
        out_specs=(P("width", "rows"), P(None, "width", "rows")) + weights,
        check_vma=False,
    )
```

time: 1290 us -> 356 us (0.28)
  waiting for transfers between devices: 730 us -> 0 us
  Pallas kernels: 0 us -> 317 us
  other arithmetic: 201 us -> 11.8 us
  blocking collectives: 124 us -> 0 us
  matrix products: 123 us -> 0 us
  local copies, waits for them, and re-layouts: 84.4 us -> 25.4 us
  between operations: 16.8 us -> 0.85 us
    reduce_scatter x6 -> x0, waiting for transfers between devices: 461 us -> none  [the longest x4 420 us: narrow(): return lax.psum_scatter(term, 'width', scatter_dimension=1, tiled=True)]
    pallas_call x0 -> x3, Pallas kernels: none -> 317 us  [the longest x1 129 us: bring(): pl.pallas_call(kernel, out_shape=outs, in_specs=[pl.BlockSpec(memory_spac...]
    all_gather x6 -> x0, waiting for transfers between devices: 228 us -> none  [the longest x4 204 us: widen(): return lax.all_gather(piece_low, 'width', axis=1, tiled=True)]
    dot_general x24 -> x0, matrix products: 116 us -> none  [the longest x2 14.4 us: attend_back(): jnp.einsum('qhd,khd->hqk', upstream, value_heads, preferred_element_type=...]
    psum x6 -> x0, blocking collectives: 101 us -> none  [the longest x4 76.3 us: norm_sums(): return lax.psum((totals, squares), 'width')]
    reduce_sum x32 -> x0, other arithmetic: 68.8 us -> none  [the longest x25 53.6 us: mix_grad(): jnp.sum(history[depth_at].astype(jnp.float32) * grad_columns)]
    add x25 -> x0, other arithmetic: 59.5 us -> none  [mix_step(): return running + mix[depth_at] * history[depth_at].astype(jnp.float32)]
    unnamed x16 -> x0, waiting for transfers between devices: 40.6 us -> none
  transfers between devices with their start and end apart: 14 -> 0, of which waited for: 11 -> 0; matrix products, arithmetic and copies ran while one was open for 10% -> 0% of each run, Pallas kernels for 0% -> 0%
where the time goes in v1:
time: 356 us; the launch traced here: 355 us
  Pallas kernels  317 us (89%)
  local copies, waits for them, and re-layouts  25.4 us (7%)
  other arithmetic  11.8 us (3%)
    pallas_call x1, Pallas kernels, bring(): pl.pallas_call(kernel, out_shape=outs, in_specs=[pl.BlockSpec(memory_spac...  129 us
    pallas_call x1, Pallas kernels, give_back(): pl.pallas_call(kernel, out_shape=outs, in_specs=[pl.BlockSpec(memory_spac...  114 us
    pallas_call x1, Pallas kernels, middle(): pl.pallas_call(functools.partial(middle_kernel, width, per), out_shape=ou...  74.6 us
    unnamed x34, local copies, waits for them, and re-layouts  22.9 us
    sub x6, other arithmetic, optimize(): weight - rate * (first_fixed / (jnp.sqrt(second_fixed) + EPS_ADAM) + deca...  7.92 us

profile of v1, /device:TPU:0, one launch (start us, length us, event | category | flops | bytes accessed | tf_op | source)
XLA Modules:
  0.0 355.3 jit_solution(13241861982640552450)
XLA Ops:
  0.7 1.0 convert.26
  1.7 1.0 copy.41
  2.7 0.1 maximum_bitcast_fusion
  2.8 1.0 convert_bitcast_fusion
  3.8 1.0 convert_bitcast_fusion.1
  4.7 0.8 pad_maximum_fusion.own_ref
  5.6 1.3 pad.4.box_ref
  6.8 128.8 %shard_map.356 = (bf16[768,768]{1,0:T(8,128)(2,1)}, bf16[768,512]{1,0:T(8,128)(2,1)}, f32[4,8,256]{2,1,0:T(8,128)}, bf16[3,4,768,768]{3,2,1,0:T(8,128)(2,1)}) custom-call(f32[25]{0:T(128)} %refs_0_.1, bf16[25,192,2048]{2,1,0:T(8,128)(2,1)} %refs_1_.1, bf16[192,2048]{1,0:T(8,128)(2,1)} %cot_ref.1, bf16[3,96,768]{2,1,0:T(8,128)(2,1)} %pad_maximum_fusion.own_ref, ...), custom_call_target="tpu_custom_call" | custom-call | tf_op jit(solution)/shard_map/pallas_call | solution.py:783
  135.6 74.6 %shard_map.357 = (bf16[768,512]{1,0:T(8,128)(2,1)}, f32[768,512]{1,0:T(8,128)}, f32[768,768]{1,0:T(8,128)}, bf16[4,768,768]{2,1,0:T(8,128)(2,1)}, bf16[4,768,768...) custom-call(s32[2,1024]{1,0:T(2,128)} %seg_ref.1, ...), custom_call_target="tpu_custom_call" | custom-call | tf_op jit(solution)/shard_map/pallas_call | solution.py:823
  210.3 113.8 %shard_map.358 = (bf16[25,192,2048]{2,1,0:T(8,128)(2,1)}, bf16[192,2048]{1,0:T(8,128)(2,1)}, f32[8,256]{1,0:T(8,128)}, f32[3,96,768]{2,1,0:T(8,128)}) custom-call(f32[25]{0:T(128)} %refs_0_.1, bf16[25,192,2048]{2,1,0:T(8,128)(2,1)} %refs_1_.1, f32[768,768]{1,0:T(8,128)} %get-tuple-element.41.refs_2_, f32[768,512]{1,0:T(8,128)} %get-tuple-element.42.refs_3_, ...), custom_call_target="tpu_custom_call" | custom-call | tf_op jit(solution)/shard_map/pallas_call | solution.py:885
  324.2 1.1 slice_bitcast_fusion
  325.4 1.1 multiply_subtract_fusion.2
  326.5 1.0 copy.42
  327.5 1.0 copy.43
  328.5 0.2 multiply_subtract_fusion.3
  328.7 0.7 copy.46
  329.4 0.7 copy.47
  330.1 0.7 copy.48
  330.9 2.1 multiply_subtract_fusion.1
  333.0 2.1 multiply_subtract_fusion
  335.1 1.3 multiply_subtract_fusion.4
  336.4 1.2 multiply_subtract_fusion.5
  337.6 0.9 copy.51
  338.5 16.8 %copy.52 = bf16[25,192,2048]{2,1,0:T(8,128)(2,1)} copy(bf16[25,192,2048]{2,1,0:T(8,128)(2,1)} %get-tuple-element.119) | data formatting | bytes 39321600
  (29 shorter events, 0.2 us)
Async XLA Ops:
  210.3 115.1 %copy-start = (f32[3,96,192]{2,1,0:T(8,128)S(1)}, f32[3,96,192]{2,1,0:T(8,128)}, u32[]{:S(2)}) copy-start(f32[3,96,192]{2,1,0:T(8,128)} %param.24) | copy-start | bytes 663556
  210.3 115.2 %copy-start.5 = (f32[3,96,192]{2,1,0:T(8,128)S(1)}, f32[3,96,192]{2,1,0:T(8,128)}, u32[]{:S(2)}) copy-start(f32[3,96,192]{2,1,0:T(8,128)} %param.25) | copy-start | bytes 663556
  210.3 115.2 %copy-start.6 = (f32[3,96,192]{2,1,0:T(8,128)S(1)}, f32[3,96,192]{2,1,0:T(8,128)}, u32[]{:S(2)}) copy-start(f32[3,96,192]{2,1,0:T(8,128)} %param.26) | copy-start | bytes 663556
  324.1 6.8 %copy-start.1 = (f32[96,768]{1,0:T(8,128)S(1)}, f32[96,768]{1,0:T(8,128)}, u32[]{:S(2)}) copy-start(f32[96,768]{1,0:T(8,128)} %param.30) | copy-start | bytes 884740
  324.1 6.8 %copy-start.3 = (f32[3,96,768]{2,1,0:T(8,128)S(1)}, f32[3,96,768]{2,1,0:T(8,128)}, u32[]{:S(2)}) copy-start(f32[3,96,768]{2,1,0:T(8,128)} %get-tuple-element.52) | copy-start | bytes 2654212
  324.1 8.9 %copy-start.2 = (f32[768,96]{0,1:T(8,128)S(1)}, f32[768,96]{0,1:T(8,128)}, u32[]{:S(2)}) copy-start(f32[768,96]{0,1:T(8,128)} %param.33) | copy-start | bytes 884740
  324.1 10.9 %copy-start.7 = (f32[2,192]{1,0:T(2,128)S(1)}, f32[2,192]{1,0:T(2,128)}, u32[]{:S(2)}) copy-start(f32[2,192]{1,0:T(2,128)} %param.36) | copy-start | bytes 4612
  324.2 10.9 %copy-start.9 = (f32[2,192]{1,0:T(2,128)S(1)}, f32[2,192]{1,0:T(2,128)}, u32[]{:S(2)}) copy-start(f32[2,192]{1,0:T(2,128)} %param.37) | copy-start | bytes 4612
  324.2 10.9 %copy-start.10 = (f32[2,192]{1,0:T(2,128)S(1)}, f32[2,192]{1,0:T(2,128)}, u32[]{:S(2)}) copy-start(f32[2,192]{1,0:T(2,128)} %param.38) | copy-start | bytes 4612
  324.2 12.2 %copy-start.8 = (f32[25]{0:T(128)S(1)}, f32[25]{0:T(128)}, u32[]{:S(2)}) copy-start(f32[25]{0:T(128)} %refs_0_.1) | copy-start | bytes 304
  324.2 13.4 %copy-start.4 = (bf16[192,2048]{1,0:T(8,128)(2,1)S(1)}, bf16[192,2048]{1,0:T(8,128)(2,1)}, u32[]{:S(2)}) copy-start(bf16[192,2048]{1,0:T(8,128)(2,1)} %get-tuple-element.118) | copy-start | bytes 2359300
  326.5 9.9 %copy-start.11 = (f32[25]{0:T(128)S(1)}, f32[25]{0:T(128)}, u32[]{:S(2)}) copy-start(f32[25]{0:T(128)} %param.40) | copy-start | bytes 304
  326.5 9.9 %copy-start.12 = (f32[25]{0:T(128)S(1)}, f32[25]{0:T(128)}, u32[]{:S(2)}) copy-start(f32[25]{0:T(128)} %param.41) | copy-start | bytes 304

commit v2 on v1

--- a/solution.py
+++ b/solution.py
@@ -94,6 +94,17 @@
     for place in places:
         pl.semaphore_signal(bar, inc=1, device_id=place, device_id_type=MESH)
     pl.semaphore_wait(bar, len(places))
+
+
+def at_steps(table):
+    def hook(step):
+        for at, actions in table.items():
+            @pl.when(step == at)
+            def _(actions=actions):
+                for action in actions:
+                    action()
+
+    return hook
 
 
 class Sends:
@@ -348,12 +359,13 @@
     return jnp.concatenate([a * cosine - b * sine, b * cosine + a * sine], 0)
 
 
-def project(x_ref, wa_ref, trig_ref, q_ref, k_ref, v_ref, wo_ref, width, per, own):
+def project(x_ref, wa_ref, trig_ref, q_ref, k_ref, v_ref, wo_ref, width, per, own, hook):
     ext = HALO + own
     group = per * HEAD
     scale = HEAD**-0.5
 
     def body(w):
+        hook(w)
         turned = jnp.transpose(wa_ref[w])
         wo_ref[w] = turned[3 * group :]
         queries = dot(turned[:group], x_ref[:, HALO:])
@@ -372,7 +384,7 @@
     tiles(width, body)
 
 
-def attend(q_ref, k_ref, v_ref, start_ref, bias_ref, p_ref, ao_ref, width, per, own):
+def attend(q_ref, k_ref, v_ref, start_ref, bias_ref, p_ref, ao_ref, width, per, own, hook):
     blocks = own // HALO
     for b in range(blocks):
         key_at = lax.broadcasted_iota(jnp.int32, (2 * HALO, HALO), 0).astype(F32) + float(b * HALO)
@@ -381,6 +393,7 @@
         bias_ref[b] = jnp.where((key_at >= first) & (key_at <= query_at), 0.0, MASKED)
 
     def body(w):
+        hook(w)
         ao_ref[w, 0:HEAD, :] = jnp.zeros((HEAD, own), BF16)
         for i in range(per):
             h = w * per + i
@@ -407,7 +420,7 @@
     tiles(width, body)
 
 
-def feed_forward(x_ref, ct_ref, wb_ref, wc_ref, gb_ref, gc_ref, acc_ref, u_ref, xt_ref, ctt_ref, pre_ref, gh_ref, hid_ref, gi_ref, width):
+def feed_forward(x_ref, ct_ref, wb_ref, wc_ref, gb_ref, gc_ref, acc_ref, u_ref, xt_ref, ctt_ref, pre_ref, gh_ref, hid_ref, gi_ref, width, hook):
     own = x_ref.shape[1]
     xt_ref[...] = jnp.transpose(x_ref[...])
     ctt_ref[...] = jnp.transpose(ct_ref[...])
@@ -415,6 +428,7 @@
     strip = 32
 
     def body(w):
+        hook(w)
         pre_ref[...] = dot(xt_ref[...], wb_ref[w])
         gh_ref[...] = dot(ctt_ref[...], wc_ref[w])
 
@@ -437,13 +451,14 @@
     tiles(width, body)
 
 
-def attend_back(low_ref, wo_ref, p_ref, q_ref, k_ref, v_ref, trig_ref, gp_ref, width, per, own):
+def attend_back(low_ref, wo_ref, p_ref, q_ref, k_ref, v_ref, trig_ref, gp_ref, width, per, own, hook):
     ext = HALO + own
     group = per * HEAD
     blocks = own // HALO
     scale = HEAD**-0.5
 
     def body(w):
+        hook(w)
         gp_ref[w, 3 * group :, :] = jnp.zeros((group, ext), BF16)
         gp_ref[w, :group, :HALO] = jnp.zeros((group, HALO), BF16)
         upstream = dot(wo_ref[w], low_ref[...]).astype(BF16)
@@ -480,11 +495,12 @@
     tiles(width, body)
 
 
-def project_back(x_ref, low_ref, ao_ref, wa_ref, gp_ref, ga_ref, u_ref, width, per):
+def project_back(x_ref, low_ref, ao_ref, wa_ref, gp_ref, ga_ref, u_ref, width, per, hook):
     group = 3 * per * HEAD - HEAD
     u_ref[...] = jnp.zeros_like(u_ref)
 
     def body(w):
+        hook(w)
         u_ref[...] += dot(wa_ref[w], gp_ref[w])
         ga_ref[w, :, :group] = dot_rows(x_ref[...], gp_ref[w, :group, :]).astype(BF16)
         ga_ref[w, :, group:] = (
@@ -494,245 +510,285 @@
     tiles(width, body)
 
 
-def bring_kernel(width, rows, mix_ref, hist_ref, cot_ref, own_ref, box_ref, st_ref, ct_ref, full_ref, boxes_ref,
-                 pair, mixed, load_sem, here_sem, send_sem, recv_sem):
+def block_kernel(width, rows, per, mix_ref, hist_ref, cot_ref, seg_ref, box_ref, own_ref, given_ref,
+                 gcol_ref, bout_ref, small_ref, total_ref, left_ref,
+                 full, st, ct, boxes_in, gain, x_one, stat_one, starts, trig, q, k, v, wo, ao, prob, mid, stat_two, gmid, low, blk,
+                 gacc_one, gacc_two, halo_out, halo_in, macc, small_out, small_in, small_step,
+                 final, last_box, boxes, load_sem, here_sem, send_sem, recv_sem):
     r, z = lax.axis_index("rows"), lax.axis_index("width")
     layers, piece, tokens = hist_ref.shape
     own = tokens // width
-    _, bits = row_bits(rows)
-    greet(z, r, width, [1] + bits)
+    ext = HALO + own
+    per_row = seg_ref.shape[1] // own
+    core, bits = row_bits(rows)
+    hops = len(bits)
+    cut = own // 2
+    greet(z, r, width, [core] + bits)
     sends = Sends(send_sem, recv_sem)
+    inside = own_ref is not None
     gathers = []
-    if own_ref is not None:
-        gathers = [Gather(sends, own_ref.at[x], full_ref.at[x], z, r, width, rows) for x in range(3)]
-    first = 1 - z // 2
+    if inside:
+        gathers = [Gather(sends, own_ref.at[at], full.at[at], z, r, width, rows) for at in range(3)]
+        first, second, third = gathers
+    odd = lax.rem(z, 2) == 1
+    mine = pl.ds(pl.multiple_of(z * piece, 16), piece)
+
+    far = 1 - z // 2
     chunks = []
     for at in range(width):
-        low = flip(first, 1) if at // 2 else first
-        chunks.append(2 * low + at % 2)
-    loads = []
-    for at in range(width):
-        cols = pl.ds(pl.multiple_of(chunks[at] * own, LANES), own)
-        load = pltpu.make_async_copy(hist_ref.at[:, :, cols], pair.at[at], load_sem.at[at])
-        load.start()
-        loads.append(load)
-    if gathers:
-        gathers[0].start()
-    mine = pl.ds(pl.multiple_of(z * piece, 16), piece)
-    st_even = st_ref.at[mine, pl.ds(HALO, own)]
-    st_odd = st_ref.at[mine, :]
-    gain_sends = [sends.make(box_ref, boxes_ref.at[z], (r, lax.rem(z + k, width))) for k in range(1, width)]
-    for copy in gain_sends:
-        copy.start()
-    boxes_ref[z] = box_ref[...]
+        low_half = flip(far, 1) if at // 2 else far
+        chunks.append(2 * low_half + at % 2)
+    st_even = st.at[mine, pl.ds(HALO, own)]
+    st_odd = st.at[mine, :]
+    gain_sends = [sends.make(box_ref, boxes_in.at[z], (r, lax.rem(z + step, width))) for step in range(1, width)]
     base = sends.used
     sends.used += width - 1
 
-    def stream_copy(k, target, odd, start):
-        if odd:
-            src = mixed.at[:, pl.ds(pl.multiple_of(start - HALO, LANES), HALO + own)]
-            dst = st_odd
-        else:
-            src = mixed.at[:, pl.ds(pl.multiple_of(start, LANES), own)]
-            dst = st_even
-        return pltpu.make_async_remote_copy(
-            src_ref=src, dst_ref=dst, send_sem=send_sem.at[base + k - 1], recv_sem=recv_sem.at[base + k - 1],
-            device_id=(r, target), device_id_type=MESH,
-        )
-
-    for at in range(width):
-        target = chunks[at]
-        start = pl.multiple_of(target * own, LANES)
-        loads[at].wait()
-        mix_stream(mix_ref, pair.at[at], mixed, pl.ds(start, own), layers)
-        odd = at % 2 == 1
-        for k in range(1, width):
-            @pl.when(lax.rem(z + k, width) == target)
-            def _(k=k, target=target, odd=odd, start=start):
-                stream_copy(k, target, odd, start).start()
-
-        @pl.when(target == z)
-        def _(odd=odd, start=start):
-            if odd:
-                st_odd[...] = mixed[:, pl.ds(pl.multiple_of(start - HALO, LANES), HALO + own)]
+    def scoped_stream(pair, mixed):
+        def load(at):
+            cols = pl.ds(pl.multiple_of(chunks[at // 2] * own + (at % 2) * cut, LANES), cut)
+            return pltpu.make_async_copy(hist_ref.at[:, :, cols], pair.at[at % 3], load_sem.at[at % 3])
+
+        def stream_copy(step, target, is_odd):
+            start = pl.multiple_of(target * own, LANES)
+            if is_odd:
+                src, dst = mixed.at[:, pl.ds(pl.multiple_of(start - HALO, LANES), ext)], st_odd
             else:
-                st_even[...] = mixed[:, pl.ds(start, own)]
-                st_ref[:, 0:HALO] = jnp.zeros((D, HALO), BF16)
-
-    for gather in gathers[1:]:
-        gather.start()
+                src, dst = mixed.at[:, pl.ds(start, own)], st_even
+            return pltpu.make_async_remote_copy(
+                src_ref=src, dst_ref=dst, send_sem=send_sem.at[base + step - 1], recv_sem=recv_sem.at[base + step - 1],
+                device_id=(r, target), device_id_type=MESH,
+            )
+
+        for at in range(3):
+            load(at).start()
+        if inside:
+            first.start()
+        for copy in gain_sends:
+            copy.start()
+        boxes_in[z] = box_ref[...]
+        for at in range(2 * width):
+            load(at).wait()
+            target = chunks[at // 2]
+            start = pl.multiple_of(target * own + (at % 2) * cut, LANES)
+            mix_stream(mix_ref, pair.at[at % 3], mixed, pl.ds(start, cut), layers)
+            if at + 3 < 2 * width:
+                load(at + 3).start()
+            if at % 2 == 0:
+                continue
+            is_odd = at // 2 % 2 == 1
+            for step in range(1, width):
+                @pl.when(lax.rem(z + step, width) == target)
+                def _(step=step, target=target, is_odd=is_odd):
+                    stream_copy(step, target, is_odd).start()
+
+            @pl.when(target == z)
+            def _(is_odd=is_odd, target=target):
+                start = pl.multiple_of(target * own, LANES)
+                if is_odd:
+                    st_odd[...] = mixed[:, pl.ds(pl.multiple_of(start - HALO, LANES), ext)]
+                else:
+                    st_even[...] = mixed[:, pl.ds(start, own)]
+                    st[:, 0:HALO] = jnp.zeros((D, HALO), BF16)
+
+        for gather in gathers[1:]:
+            gather.start()
+        for copy in cot_sends:
+            copy.start()
+        cot_here.start()
+        for copy in gain_sends:
+            copy.wait()
+        spread_gains(boxes_in, gain, width, piece)
+        document_starts(seg_ref, starts, trig, z // per_row, lax.rem(z, per_row) * own, own)
+        if inside:
+            first.advance(0)
+            first.advance(1)
+        for step in range(1, width):
+            for is_odd in (False, True):
+                @pl.when(lax.rem(z, 2) == int(is_odd))
+                def _(step=step, is_odd=is_odd):
+                    stream_copy(step, z, is_odd).wait_recv()
+
+                @pl.when(lax.rem(z + step, 2) == int(is_odd))
+                def _(step=step, is_odd=is_odd):
+                    stream_copy(step, lax.rem(z + step, width), is_odd).wait_send()
+
     cot_sends = []
-    for k in range(1, width):
-        target = lax.rem(z + k, width)
+    for step in range(1, width):
+        target = lax.rem(z + step, width)
         cols = pl.ds(pl.multiple_of(target * own, LANES), own)
-        cot_sends.append(sends.make(cot_ref.at[:, cols], ct_ref.at[mine, :], (r, target)))
+        cot_sends.append(sends.make(cot_ref.at[:, cols], ct.at[mine, :], (r, target)))
+    cot_here = pltpu.make_async_copy(
+        cot_ref.at[:, pl.ds(pl.multiple_of(z * own, LANES), own)], ct.at[mine, :], here_sem
+    )
+    if not inside:
+        given = pltpu.make_async_copy(given_ref, full, load_sem.at[3])
+        given.start()
+    pl.run_scoped(scoped_stream, pltpu.VMEM((3, layers, piece, cut), BF16), pltpu.VMEM((piece, tokens), BF16))
+
+    norm_forward(st, 0, gain, 0, x_one, stat_one, ext)
+    if inside:
+        for step in range(2, hops + 2):
+            first.advance(step)
+    else:
+        given.wait()
+    project(x_one, full.at[0], trig, q, k, v, wo, width, per, own, at_steps({}))
+    when_attend = at_steps({2: [lambda: second.advance(0)]}) if inside else at_steps({})
+    pl.run_scoped(
+        lambda bias: attend(q, k, v, starts, bias, prob, ao, width, per, own, when_attend),
+        pltpu.VMEM((own // HALO, 2 * HALO, HALO), F32),
+    )
+    if inside:
+        second.advance(1)
+        third.advance(0)
+    out_project(st, full.at[0], ao, mid, width, per)
+    gmid[...] = mid[...]
+    if inside:
+        for step in range(1, hops + 1):
+            second.advance(step + 1)
+            third.advance(step)
+        third.advance(hops + 1)
+        for gather in gathers:
+            gather.end()
+
+    scatters = []
+    if inside:
+        scatters = [
+            Scatter(sends, full.at[at], [box.at[at] for box in boxes], last_box.at[at], final.at[at], total_ref.at[at], z, r, width, rows)
+            for at in (2, 1, 0)
+        ]
     for copy in cot_sends:
+        copy.wait()
+    cot_here.wait()
+
+    def scoped_feed(x_two, xt, ctt, pre, gh, hid, gi, u_two):
+        norm_forward(mid, 0, gain, 1, x_two, stat_two, own)
+        feed_forward(x_two, ct, full.at[1], full.at[2], full.at[1], full.at[2], gmid, u_two, xt, ctt, pre, gh, hid, gi, width, at_steps({}))
+        blk[...] = gmid[...].astype(BF16)
+
+        def write(cols, value):
+            gmid[:, cols] = value
+            low[:, cols] = value.astype(BF16)
+
+        norm_back(u_two, 0, mid, 0, stat_two, 0, gain, 1, lambda cols: ct[:, cols].astype(F32), write, gacc_two, own)
+
+    pl.run_scoped(
+        scoped_feed, pltpu.VMEM((D, own), BF16), pltpu.VMEM((own, D), BF16), pltpu.VMEM((own, D), BF16), pltpu.VMEM((own, D), F32),
+        pltpu.VMEM((own, D), F32), pltpu.VMEM((own, D), BF16), pltpu.VMEM((own, D), BF16), pltpu.VMEM((D, own), F32),
+    )
+    for scatter in scatters[:2]:
+        scatter.start()
+    blk_sends, gs_sends = [], []
+    here = pl.ds(pl.multiple_of(z * own, LANES), own)
+    for step in range(1, width):
+        target = lax.rem(z + step, width)
+        part = pl.ds(pl.multiple_of(target * piece, 16), piece)
+        blk_sends.append(sends.make(blk.at[part, :], bout_ref.at[:, here], (r, target)))
+    for copy in blk_sends:
         copy.start()
-    cot_here = pltpu.make_async_copy(
-        cot_ref.at[:, pl.ds(pl.multiple_of(z * own, LANES), own)], ct_ref.at[mine, :], here_sem
-    )
-    cot_here.start()
-    for step in range(len(bits) + 2):
-        for gather in gathers:
-            gather.advance(step)
-    for k in range(1, width):
-        for odd in (False, True):
-            @pl.when(lax.rem(z, 2) == int(odd))
-            def _(k=k, odd=odd):
-                stream_copy(k, lax.rem(z + k, width), odd, HALO if odd else 0).wait_recv()
-
-            @pl.when(lax.rem(z + k, 2) == int(odd))
-            def _(k=k, odd=odd):
-                stream_copy(k, lax.rem(z + k, width), odd, HALO if odd else 0).wait_send()
-    cot_here.wait()
-    for copy in gain_sends + cot_sends:
-        copy.wait()
-    for gather in gathers:
-        gather.end()
-
-
-def middle_kernel(width, per, seg_ref, st_ref, ct_ref, full_ref, boxes_ref,
-                  blk_ref, gmid_ref, u_ref, ga_ref, gb_ref, gc_ref, gain_ref, gacc_ref, stat_ref,
-                  x_ref, start_ref, trig, q_ref, k_ref, v_ref, wo_ref, bias, prob, ao, mid, stat_two, u_two, low):
-    z = lax.axis_index("width")
-    own = ct_ref.shape[1]
-    per_row = seg_ref.shape[1] // own
-    spread_gains(boxes_ref, gain_ref, width, D // width)
-    document_starts(seg_ref, start_ref, trig, z // per_row, lax.rem(z, per_row) * own, own)
-    norm_forward(st_ref, 0, gain_ref, 0, x_ref, stat_ref, HALO + own)
-    project(x_ref, full_ref.at[0], trig, q_ref, k_ref, v_ref, wo_ref, width, per, own)
-    attend(q_ref, k_ref, v_ref, start_ref, bias, prob, ao, width, per, own)
-    out_project(st_ref, full_ref.at[0], ao, mid, width, per)
-    gmid_ref[...] = mid[...]
-
-    def inner(x_two, xt, ctt, pre, gh, hid, gi):
-        norm_forward(mid, 0, gain_ref, 1, x_two, stat_two, own)
-        feed_forward(x_two, ct_ref, full_ref.at[1], full_ref.at[2], gb_ref, gc_ref, gmid_ref, u_two, xt, ctt, pre, gh, hid, gi, width)
-
-    pl.run_scoped(
-        inner, pltpu.VMEM((D, own), BF16), pltpu.VMEM((own, D), BF16), pltpu.VMEM((own, D), BF16), pltpu.VMEM((own, D), F32),
-        pltpu.VMEM((own, D), F32), pltpu.VMEM((own, D), BF16), pltpu.VMEM((own, D), BF16),
-    )
-    blk_ref[...] = gmid_ref[...].astype(BF16)
-
-    def write(cols, value):
-        gmid_ref[:, cols] = value
-        low[:, cols] = value.astype(BF16)
-
-    norm_back(u_two, 0, mid, 0, stat_two, 0, gain_ref, 1, lambda cols: ct_ref[:, cols].astype(F32), write, gacc_ref, own)
-
-    def last(gp):
-        attend_back(low, wo_ref, prob, q_ref, k_ref, v_ref, trig, gp, width, per, own)
-        project_back(x_ref, low, ao, full_ref.at[0], gp, ga_ref, u_ref, width, per)
-
-    pl.run_scoped(last, pltpu.VMEM((width, 4 * per * HEAD, HALO + own), BF16))
-
-
-def return_kernel(width, rows, mix_ref, hist_ref, u_ref, gmid_ref, st_ref, stat_ref, gain_ref, gtwo_ref, blk_ref,
-                  ga_ref, gb_ref, gc_ref, hgrad_ref, bout_ref, total_ref, small_ref,
-                  pair, uh, halo_out, halo_in, gs, gcol, gone, macc, small_out, small_in, small_step,
-                  final, last_box, boxes, load_sem, store_sem, here_sem, send_sem, recv_sem):
-    r, z = lax.axis_index("rows"), lax.axis_index("width")
-    layers, piece, tokens = hist_ref.shape
-    own = tokens // width
-    core, bits = row_bits(rows)
-    greet(z, r, width, [1] + bits)
-    sends = Sends(send_sem, recv_sem)
-    loads, order = [], []
-    for k in range(width):
-        chunk = lax.rem(z + width - k, width)
-        cols = pl.ds(pl.multiple_of(chunk * own, LANES), own)
-        load = pltpu.make_async_copy(hist_ref.at[:, :, cols], pair.at[k], load_sem.at[k])
-        load.start()
-        loads.append(load)
-        order.append(cols)
-    scatters = []
-    if total_ref is not None:
-        scatters = [
-            Scatter(sends, grads, [box.at[x] for box in boxes], last_box.at[x], final.at[x], total_ref.at[x], z, r, width, rows)
-            for x, grads in ((2, gc_ref), (1, gb_ref), (0, ga_ref))
-        ]
-    odd = lax.rem(z, 2) == 1
+    bout_ref[:, here] = blk[mine, :]
+
     halo = sends.make(halo_out, halo_in, (r, flip(z, 1)))
 
-    @pl.when(odd)
-    def _():
-        halo_out[...] = u_ref[:, 0:HALO].astype(BF16)
-        halo.start()
-
-    for scatter in scatters:
-        scatter.start()
-    uh[...] = u_ref[:, HALO:]
-
-    @pl.when(jnp.logical_not(odd))
-    def _():
-        halo.wait_recv()
-        uh[:, own - HALO : own] += halo_in[...].astype(F32)
-
-    def write(cols, value):
-        gs[:, cols] = value.astype(BF16)
-
-    norm_back(uh, 0, st_ref, HALO, stat_ref, HALO, gain_ref, 0, lambda cols: gmid_ref[:, cols], write, gone, own)
-    gs_sends, blk_sends = [], []
-    mine = pl.ds(pl.multiple_of(z * own, LANES), own)
-    for k in range(1, width):
-        target = lax.rem(z + k, width)
+    def scoped_back(gp, u):
+        when_attend, when_project = at_steps({}), at_steps({})
+        if inside:
+            when_attend = at_steps({1: [lambda: scatters[0].advance(0), lambda: scatters[1].advance(0)]})
+            when_project = at_steps({1: [lambda: scatters[0].advance(1)]})
+        attend_back(low, wo, prob, q, k, v, trig, gp, width, per, own, when_attend)
+        project_back(x_one, low, ao, full.at[0], gp, full.at[0], u, width, per, when_project)
+
+        @pl.when(odd)
+        def _():
+            halo_out[...] = u[:, 0:HALO].astype(BF16)
+            halo.start()
+
+        if inside:
+            scatters[2].start()
+            scatters[0].advance(2)
+
+        @pl.when(jnp.logical_not(odd))
+        def _():
+            halo.wait_recv()
+            u[:, own : own + HALO] += halo_in[...].astype(F32)
+
+        def write(cols, value):
+            blk[:, cols] = value.astype(BF16)
+
+        for copy in blk_sends:
+            copy.wait_send()
+        norm_back(u, HALO, st, HALO, stat_one, HALO, gain, 0, lambda cols: gmid[:, cols], write, gacc_one, own)
+
+    pl.run_scoped(scoped_back, pltpu.VMEM((width, 4 * per * HEAD, ext), BF16), pltpu.VMEM((D, ext), F32))
+
+    for step in range(1, width):
+        target = lax.rem(z + step, width)
         part = pl.ds(pl.multiple_of(target * piece, 16), piece)
-        gs_sends.append(sends.make(gs.at[part, :], gcol.at[k], (r, target)))
-        blk_sends.append(sends.make(blk_ref.at[part, :], bout_ref.at[:, mine], (r, target)))
-    for copy in gs_sends + blk_sends:
+        gs_sends.append(sends.make(blk.at[part, :], gcol_ref.at[:, here], (r, target)))
+    for copy in gs_sends:
         copy.start()
-    part = pl.ds(pl.multiple_of(z * piece, 16), piece)
-    bout_ref[:, mine] = blk_ref[part, :]
-    gcol[0] = gs[part, :]
+    gcol_ref[:, here] = blk[mine, :]
     macc[...] = jnp.zeros_like(macc)
     strip = 16
-    stores = []
-    for k in range(width):
-        if k:
-            gs_sends[k - 1].wait_recv()
-        loads[k].wait()
-
-        def body(at, k=k):
-            cut = pl.ds(pl.multiple_of(at * strip, strip), strip)
-            g = gcol[k, cut, :].astype(F32)
-            for j in range(layers):
-                crossed = pair[k, j, cut, :].astype(F32) * g
-                folded = crossed[:8] + crossed[8:]
-                part = folded[:, :LANES]
-                for lane in range(1, own // LANES):
-                    part = part + folded[:, lane * LANES : (lane + 1) * LANES]
-                macc[j] += part
-                pair[k, j, cut, :] = (mix_ref[j] * g).astype(BF16)
-
-        tiles(piece // strip, body)
-        store = pltpu.make_async_copy(pair.at[k], hgrad_ref.at[:, :, order[k]], store_sem.at[k])
-        store.start()
-        stores.append(store)
-        if k <= len(bits):
-            for scatter in scatters:
-                scatter.advance(k)
-    for step in range(width, len(bits) + 1):
-        for scatter in scatters:
-            scatter.advance(step)
+
+    def scoped_mix(pair):
+        def place(at):
+            chunk = lax.rem(z + width - at // 2, width)
+            return pl.ds(pl.multiple_of(chunk * own + (at % 2) * cut, LANES), cut)
+
+        def load(at):
+            return pltpu.make_async_copy(hist_ref.at[:, :, place(at)], pair.at[at % 3], load_sem.at[at % 3])
+
+        for at in range(3):
+            load(at).start()
+        for at in range(2 * width):
+            if at % 2 == 0 and at:
+                gs_sends[at // 2 - 1].wait_recv()
+            load(at).wait()
+            cols = place(at)
+
+            def body(row, at=at, cols=cols):
+                part = pl.ds(pl.multiple_of(row * strip, strip), strip)
+                g = gcol_ref[part, cols].astype(F32)
+                for j in range(layers):
+                    crossed = pair[at % 3, j, part, :].astype(F32) * g
+                    folded = crossed[:8] + crossed[8:]
+                    total = folded[:, :LANES]
+                    for lane in range(1, cut // LANES):
+                        total = total + folded[:, lane * LANES : (lane + 1) * LANES]
+                    macc[j] += total
+
+            tiles(piece // strip, body)
+            if at + 3 < 2 * width:
+                load(at + 3).start()
+            if inside:
+                if at == 0:
+                    scatters[1].advance(1)
+                    scatters[2].advance(0)
+                if at == 1:
+                    scatters[1].advance(2)
+                    scatters[2].advance(1)
+
+    pl.run_scoped(scoped_mix, pltpu.VMEM((3, layers, piece, cut), BF16))
+
     small_out[...] = jnp.zeros_like(small_out)
-    first = jnp.sum(jnp.transpose(gone[...]), 0, keepdims=True)
-    second = jnp.sum(jnp.transpose(gtwo_ref[...]), 0, keepdims=True)
-    summed = jnp.sum(macc[...], 1)
-    depth = jnp.sum(jnp.transpose(summed), 0, keepdims=True)
+    gain_one = jnp.sum(jnp.transpose(gacc_one[...]), 0, keepdims=True)
+    gain_two = jnp.sum(jnp.transpose(gacc_two[...]), 0, keepdims=True)
+    depth = jnp.sum(jnp.transpose(jnp.sum(macc[...], 1)), 0, keepdims=True)
     for w in range(width):
-        small_out[w, 0:1, 0:piece] = first[:, w * piece : (w + 1) * piece]
-        small_out[w, 1:2, 0:piece] = second[:, w * piece : (w + 1) * piece]
+        small_out[w, 0:1, 0:piece] = gain_one[:, w * piece : (w + 1) * piece]
+        small_out[w, 1:2, 0:piece] = gain_two[:, w * piece : (w + 1) * piece]
         small_out[w, 2:3, 0 : depth.shape[1]] = depth
     small_sends = [
-        sends.make(small_out.at[lax.rem(z + k, width)], small_in.at[k - 1], (r, lax.rem(z + k, width))) for k in range(1, width)
+        sends.make(small_out.at[lax.rem(z + step, width)], small_in.at[step - 1], (r, lax.rem(z + step, width)))
+        for step in range(1, width)
     ]
     for copy in small_sends:
         copy.start()
     current = small_out[z]
-    for k in range(1, width):
-        small_sends[k - 1].wait_recv()
-        current = current + small_in[k - 1]
+    for step in range(1, width):
+        small_sends[step - 1].wait_recv()
+        current = current + small_in[step - 1]
     for at, bit in enumerate([core] + bits):
         small_step[at, 0] = current
         copy = sends.make(small_step.at[at, 0], small_step.at[at, 1], (flip(r, bit), z))
@@ -741,11 +797,13 @@
         current = current + small_step[at, 1]
         small_sends.append(copy)
     small_ref[...] = current
+    if inside:
+        scatters[2].advance(2)
     for scatter in scatters:
         scatter.finish()
     for copy in blk_sends:
         copy.wait_recv()
-    for copy in gs_sends + blk_sends + small_sends:
+    for copy in gs_sends + small_sends:
         copy.wait_send()
 
     @pl.when(odd)
@@ -754,8 +812,10 @@
 
     for scatter in scatters:
         scatter.end()
-    for store in stores:
-        store.wait()
+    if not inside:
+        leave = pltpu.make_async_copy(full, left_ref, load_sem.at[3])
+        leave.start()
+        leave.wait()
 
 
 def vmem(count):
@@ -766,134 +826,71 @@
     return jax.ShapeDtypeStruct(sizes, dtype)
 
 
-def bring(width, rows, mix, history, cotangent, own_three, box):
+def block(width, rows, mix, history, cotangent, segments, box, own_three):
     layers, piece, tokens = history.shape
+    shard = own_three.shape[1]
     own = tokens // width
-    inside = own_three.shape[1] % 16 == 0
-    count = (width - 1) * 3 + 3 * Gather.copies(width, rows) + 4
-    any_space = pl.BlockSpec(memory_space=pl.ANY)
-    outs = [shape(D, HALO + own, dtype=BF16), shape(D, own, dtype=BF16), shape(width, 8, 2 * LANES)]
-    if inside:
-        outs.append(shape(3, width, D, D, dtype=BF16))
-
-    def kernel(mix_ref, hist_ref, cot_ref, own_ref, box_ref, st, ct, boxes, *rest):
-        full, rest = (rest[0], rest[1:]) if inside else (None, rest)
-        bring_kernel(width, rows, mix_ref, hist_ref, cot_ref, own_ref if inside else None, box_ref, st, ct, full, boxes, *rest)
-
-    found = pl.pallas_call(
-        kernel,
-        out_shape=outs,
-        in_specs=[pl.BlockSpec(memory_space=pltpu.SMEM), any_space] + vmem(3),
-        out_specs=vmem(len(outs)),
-        scratch_shapes=[
-            pltpu.VMEM((width, layers, piece, own), BF16),
-            pltpu.VMEM((piece, tokens), BF16),
-            pltpu.SemaphoreType.DMA((width,)),
-            pltpu.SemaphoreType.DMA,
-            pltpu.SemaphoreType.DMA((count,)),
-            pltpu.SemaphoreType.DMA((count,)),
-        ],
-        compiler_params=pltpu.CompilerParams(collective_id=0, has_side_effects=True, vmem_limit_bytes=60 * MIB),
-    )(mix, history, cotangent, own_three, box)
-    if inside:
-        return found
-    full = lax.all_gather(lax.all_gather(own_three, "rows", axis=1, tiled=True), "width", axis=1)
-    return (*found, full)
-
-
-def middle(width, segments, st, ct, boxes, full):
-    own = ct.shape[1]
     ext = HALO + own
     heads = D // HEAD
     per = heads // width
     group = per * HEAD
     blocks = own // HALO
-    outs = [
-        shape(D, own, dtype=BF16), shape(D, own), shape(D, ext),
-        shape(width, D, D, dtype=BF16), shape(width, D, D, dtype=BF16), shape(width, D, D, dtype=BF16),
-        shape(2, D, LANES), shape(D, LANES), shape(8, ext),
-    ]
-    scratch = [
-        pltpu.VMEM((D, ext), BF16), pltpu.VMEM((8, HALO + segments.shape[1]), F32), pltpu.VMEM((2, HEAD // 2, ext), F32),
-        pltpu.VMEM((heads, HEAD, own), BF16), pltpu.VMEM((heads, HEAD, ext), BF16), pltpu.VMEM((heads, HEAD, ext), BF16),
-        pltpu.VMEM((width, group, D), BF16), pltpu.VMEM((blocks, 2 * HALO, HALO), F32),
-        pltpu.VMEM((heads, blocks, 2 * HALO, HALO), BF16), pltpu.VMEM((width, HEAD + group, own), BF16),
-        pltpu.VMEM((D, own), F32), pltpu.VMEM((8, own), F32), pltpu.VMEM((D, own), F32), pltpu.VMEM((D, own), BF16),
-    ]
-    return pl.pallas_call(
-        functools.partial(middle_kernel, width, per),
-        out_shape=outs,
-        in_specs=vmem(5),
-        out_specs=vmem(len(outs)),
-        scratch_shapes=scratch,
-        compiler_params=pltpu.CompilerParams(vmem_limit_bytes=62 * MIB),
-    )(segments, st, ct, full, boxes)
-
-
-def give_back(width, rows, shard, mix, history, u, gmid, st, stat, gain, gtwo, blk, ga, gb, gc):
-    layers, piece, tokens = history.shape
-    own = tokens // width
+    digits = rows.bit_length() - 1
     inside = shard % 16 == 0
-    row_digits = rows.bit_length() - 1
-    count = 3 * Scatter.copies(width, rows) + 1 + 3 * (width - 1) + row_digits
     any_space = pl.BlockSpec(memory_space=pl.ANY)
-    outs = [shape(*history.shape, dtype=BF16), shape(piece, tokens, dtype=BF16), shape(8, 2 * LANES)]
-    specs = [any_space] + vmem(2)
+    ins = [mix, history, cotangent, segments, box]
+    specs = [pl.BlockSpec(memory_space=pltpu.SMEM), any_space, any_space] + vmem(2)
+    outs = [shape(piece, tokens, dtype=BF16), shape(piece, tokens, dtype=BF16), shape(8, 2 * LANES)]
+    out_specs = vmem(3)
     box_shapes = []
     if inside:
-        outs.append(shape(3, shard, D))
-        specs += vmem(1)
+        ins, specs = ins + [own_three], specs + vmem(1)
+        outs, out_specs = outs + [shape(3, shard, D)], out_specs + vmem(1)
         box_shapes = Scatter.box_shapes(width, rows, shard)
-    ins = [mix, history, u, gmid, st, stat, gain, gtwo, blk] + ([ga, gb, gc] if inside else [])
+    else:
+        gathered = lax.all_gather(lax.all_gather(own_three, "rows", axis=1, tiled=True), "width", axis=1)
+        ins, specs = ins + [gathered], specs + [any_space]
+        outs, out_specs = outs + [shape(3, width, D, D, dtype=BF16)], out_specs + [any_space]
+    low = lambda *sizes: pltpu.VMEM(sizes, BF16)
+    full = lambda *sizes: pltpu.VMEM(sizes, F32)
+    scratch = [
+        low(3, width, D, D), low(D, ext), low(D, own), full(width, 8, 2 * LANES), full(2, D, LANES), low(D, ext), full(8, ext),
+        full(8, HALO + segments.shape[1]), full(2, HEAD // 2, ext), low(heads, HEAD, own), low(heads, HEAD, ext), low(heads, HEAD, ext),
+        low(width, group, D), low(width, HEAD + group, own), low(heads, blocks, 2 * HALO, HALO), full(D, own), full(8, own),
+        full(D, own), low(D, own), low(D, own), full(D, LANES), full(D, LANES), low(D, HALO), low(D, HALO), full(layers, 8, LANES),
+        full(width, 8, 2 * LANES), full(width - 1, 8, 2 * LANES), full(digits, 2, 8, 2 * LANES),
+    ]
+    common = len(scratch)
+    if inside:
+        scratch += [low(3, width, shard, D), low(3, width - 1, shard, D)] + [low(3, *one) for one in box_shapes]
+    count = 5 * (width - 1) + 1 + (width - 1) + digits
+    count += 3 * Gather.copies(width, rows) + 3 * Scatter.copies(width, rows)
+    scratch += [
+        pltpu.SemaphoreType.DMA((4,)), pltpu.SemaphoreType.DMA, pltpu.SemaphoreType.DMA((count,)), pltpu.SemaphoreType.DMA((count,)),
+    ]
 
     def kernel(*refs):
-        given, rest = refs[: len(ins)], refs[len(ins) :]
-        hgrad, bout, small = rest[:3]
-        rest = rest[3:]
-        total, grads = None, (None, None, None)
+        given, found, rest = refs[:6], refs[6:10], refs[10:]
+        weights = (given[5], None) if inside else (None, given[5])
+        results = (found[3], None) if inside else (None, found[3])
+        kept, rest = rest[:common], rest[common:]
         final, last_box, boxes = None, None, ()
         if inside:
-            total, rest = rest[0], rest[1:]
-            grads = given[9:]
-        common, rest = rest[:11], rest[11:]
-        if inside:
-            final, last_box = rest[:2]
-            boxes = rest[2 : 2 + len(box_shapes)]
-            rest = rest[2 + len(box_shapes) :]
-        return_kernel(width, rows, *given[:9], *grads, hgrad, bout, total, small, *common, final, last_box, boxes, *rest)
-
-    scratch = [
-        pltpu.VMEM((width, layers, piece, own), BF16),
-        pltpu.VMEM((D, own), F32),
-        pltpu.VMEM((D, HALO), BF16),
-        pltpu.VMEM((D, HALO), BF16),
-        pltpu.VMEM((D, own), BF16),
-        pltpu.VMEM((width, piece, own), BF16),
-        pltpu.VMEM((D, LANES), F32),
-        pltpu.VMEM((layers, 8, LANES), F32),
-        pltpu.VMEM((width, 8, 2 * LANES), F32),
-        pltpu.VMEM((width - 1, 8, 2 * LANES), F32),
-    ]
-    scratch.append(pltpu.VMEM((row_digits, 2, 8, 2 * LANES), F32))
-    if inside:
-        scratch += [pltpu.VMEM((3, width, shard, D), BF16), pltpu.VMEM((3, width - 1, shard, D), BF16)]
-        scratch += [pltpu.VMEM((3, *one), BF16) for one in box_shapes]
-    scratch += [
-        pltpu.SemaphoreType.DMA((width,)), pltpu.SemaphoreType.DMA((width,)), pltpu.SemaphoreType.DMA,
-        pltpu.SemaphoreType.DMA((count,)), pltpu.SemaphoreType.DMA((count,)),
-    ]
+            final, last_box, boxes, rest = rest[0], rest[1], rest[2 : 2 + len(box_shapes)], rest[2 + len(box_shapes) :]
+        block_kernel(width, rows, per, *given[:5], *weights, *found[:3], *results, *kept, final, last_box, boxes, *rest)
+
     found = pl.pallas_call(
         kernel,
         out_shape=outs,
-        in_specs=[pl.BlockSpec(memory_space=pltpu.SMEM), any_space] + vmem(len(ins) - 2),
-        out_specs=specs,
+        in_specs=specs,
+        out_specs=out_specs,
         scratch_shapes=scratch,
-        compiler_params=pltpu.CompilerParams(collective_id=1, has_side_effects=True, vmem_limit_bytes=63 * MIB),
+        compiler_params=pltpu.CompilerParams(collective_id=0, has_side_effects=True, vmem_limit_bytes=64 * MIB - 128 * 1024),
     )(*ins)
     if inside:
         return found
-    total = lax.psum_scatter(jnp.stack([ga, gb, gc], 1), "width", scatter_dimension=0)
-    return (*found, lax.psum_scatter(total, "rows", scatter_dimension=1, tiled=True).astype(F32))
+    total = lax.psum_scatter(found[3], "width", scatter_dimension=1)
+    return (*found[:3], lax.psum_scatter(total, "rows", scatter_dimension=1, tiled=True).astype(F32))
 
 
 def on_device(
@@ -906,13 +903,9 @@
         w_expand,
         jnp.transpose(w_reduce),
     ]).astype(BF16)
-    shard = own_three.shape[1]
     box = jnp.pad(gains, ((0, 8 - gains.shape[0]), (0, 2 * LANES - piece)))
-    st, ct, boxes, full = bring(width, rows, mix, history, cotangent, own_three, box)
-    blk, gmid, u, ga, gb, gc, gain, gtwo, stat = middle(width, segments, st, ct, boxes, full)
-    history_grad, block_output, small, total = give_back(
-        width, rows, shard, mix, history, u, gmid, st, stat, gain, gtwo, blk, ga, gb, gc
-    )
+    grad_stream, block_output, small, total = block(width, rows, mix, history, cotangent, segments, box, own_three)
+    history_grad = (mix[:, None, None] * grad_stream[None].astype(F32)).astype(BF16)
     first = total[0]
     sum_attend = jnp.stack([first[:, k * piece : (k + 1) * piece] for k in range(3)])
     sum_output = jnp.transpose(first[:, 3 * piece :])

time: 356 us -> 276 us (0.78)
  Pallas kernels: 317 us -> 247 us
  local copies, waits for them, and re-layouts: 25.4 us -> 6.4 us
  other arithmetic: 11.8 us -> 20.4 us
    pallas_call x3 -> x1, Pallas kernels: 317 us -> 247 us  [block(): pl.pallas_call(kernel, out_shape=outs, in_specs=specs, out_specs=out_spec...]
    unnamed x34 -> x43, local copies, waits for them, and re-layouts: 22.9 us -> 4.99 us
    convert_element_type x0 -> x2, other arithmetic: none -> 8.65 us  [the longest x1 7.21 us: on_device(): (mix[:, None, None] * grad_stream[None].astype(F32)).astype(BF16)]
where the time goes in v2:
time: 276 us; the launch traced here: 275 us
  Pallas kernels  247 us (89%)
  other arithmetic  20.4 us (7%)
  local copies, waits for them, and re-layouts  6.4 us (2%)
    pallas_call x1, Pallas kernels, block(): pl.pallas_call(kernel, out_shape=outs, in_specs=specs, out_specs=out_spec...  247 us
    sub x6, other arithmetic, optimize(): weight - rate * (first_fixed / (jnp.sqrt(second_fixed) + EPS_ADAM) + deca...  7.85 us
    convert_element_type x1, other arithmetic, on_device(): (mix[:, None, None] * grad_stream[None].astype(F32)).astype(BF16)  7.21 us

profile of v2, /device:TPU:0, one launch (start us, length us, event | category | flops | bytes accessed | tf_op | source)
XLA Modules:
  0.0 275.2 jit_solution(17146359697726186704)
XLA Ops:
  0.7 1.3 pad.4.refs_4_
  2.0 1.0 convert_bitcast_fusion
  2.9 1.0 convert_bitcast_fusion.1
  3.9 1.0 copy.41
  4.9 0.6 copy-done.3
  5.6 1.0 convert.26
  6.6 0.1 maximum_bitcast_fusion
  6.7 0.8 pad_maximum_fusion.refs_5_
  7.5 247.5 %shard_map.356 = (bf16[192,2048]{1,0:T(8,128)(2,1)}, bf16[192,2048]{1,0:T(8,128)(2,1)}, f32[8,256]{1,0:T(8,128)}, f32[3,96,768]{2,1,0:T(8,128)}) custom-call(f32[25]{0:T(128)} %refs_0_.1, bf16[25,192,2048]{2,1,0:T(8,128)(2,1)} %refs_1_.1, bf16[192,2048]{1,0:T(8,128)(2,1)} %refs_2_.1, s32[2,1024]{1,0:T(2,128)} %refs_3_.1, f32[8,256]{1,0:T(8,128)} %pad.4.refs_4_, ...), custom_call_target="tpu_custom_call" | custom-call | tf_op jit(solution)/shard_map/pallas_call | solution.py:882
  255.2 1.4 convert_element_type.10
  256.6 7.2 %multiply_convert_fusion = bf16[25,192,2048]{2,1,0:T(8,128)(2,1)} fusion(f32[192,2048]{1,0:T(8,128)S(1)} %convert_element_type.10, f32[25]{0:T(128)S(1)} %copy-done.13), kind=kLoop, calls=%fused_computation | loop fusion | flops 19660800 | bytes 21233764 | tf_op jit(solution)/shard_map/convert_element_type | solution.py:908
  263.9 0.1 slice_bitcast_fusion.4
  264.0 1.1 multiply_subtract_fusion.2
  265.1 0.1 copy.42
  265.2 0.1 copy.43
  265.3 0.2 multiply_subtract_fusion.3
  265.4 0.7 copy.46
  266.2 0.7 copy.47
  266.9 0.7 copy.48
  267.6 2.0 multiply_subtract_fusion.1
  269.7 2.1 multiply_subtract_fusion
  271.8 1.3 multiply_subtract_fusion.4
  273.1 1.2 multiply_subtract_fusion.5
  274.3 0.9 copy.50
  (38 shorter events, 0.1 us)
Async XLA Ops:
  0.7 256.0 %copy-start.13 = (f32[25]{0:T(128)S(1)}, f32[25]{0:T(128)}, u32[]{:S(2)}) copy-start(f32[25]{0:T(128)} %refs_0_.1) | copy-start | bytes 304
  4.9 0.6 copy-start.3
  255.0 8.9 %copy-start.5 = (f32[3,96,768]{2,1,0:T(8,128)S(1)}, f32[3,96,768]{2,1,0:T(8,128)}, u32[]{:S(2)}) copy-start(f32[3,96,768]{2,1,0:T(8,128)} %get-tuple-element.26) | copy-start | bytes 2654212
  255.0 9.0 %copy-start = (f32[3,96,192]{2,1,0:T(8,128)S(1)}, f32[3,96,192]{2,1,0:T(8,128)}, u32[]{:S(2)}) copy-start(f32[3,96,192]{2,1,0:T(8,128)} %param.24) | copy-start | bytes 663556
  255.0 9.0 %copy-start.7 = (f32[3,96,192]{2,1,0:T(8,128)S(1)}, f32[3,96,192]{2,1,0:T(8,128)}, u32[]{:S(2)}) copy-start(f32[3,96,192]{2,1,0:T(8,128)} %param.25) | copy-start | bytes 663556
  255.0 9.0 %copy-start.8 = (f32[3,96,192]{2,1,0:T(8,128)S(1)}, f32[3,96,192]{2,1,0:T(8,128)}, u32[]{:S(2)}) copy-start(f32[3,96,192]{2,1,0:T(8,128)} %param.26) | copy-start | bytes 663556
  255.0 10.0 %copy-start.10 = (f32[192,96]{1,0:T(8,128)S(1)}, f32[192,96]{1,0:T(8,128)}, u32[]{:S(2)}) copy-start(f32[192,96]{1,0:T(8,128)} %param.28) | copy-start | bytes 221188
  255.0 10.1 %copy-start.11 = (f32[192,96]{1,0:T(8,128)S(1)}, f32[192,96]{1,0:T(8,128)}, u32[]{:S(2)}) copy-start(f32[192,96]{1,0:T(8,128)} %param.29) | copy-start | bytes 221188
  255.0 10.2 %copy-start.4 = (f32[192,96]{0,1:T(8,128)S(1)}, f32[192,96]{0,1:T(8,128)}, u32[]{:S(2)}) copy-start(f32[192,96]{0,1:T(8,128)} %copy-done.3) | copy-start | bytes 221188
  255.0 12.6 %copy-start.1 = (f32[96,768]{1,0:T(8,128)S(1)}, f32[96,768]{1,0:T(8,128)}, u32[]{:S(2)}) copy-start(f32[96,768]{1,0:T(8,128)} %param.30) | copy-start | bytes 884740
  255.1 12.6 %copy-start.9 = (f32[96,768]{1,0:T(8,128)S(1)}, f32[96,768]{1,0:T(8,128)}, u32[]{:S(2)}) copy-start(f32[96,768]{1,0:T(8,128)} %param.31) | copy-start | bytes 884740
  255.1 14.6 %copy-start.2 = (f32[768,96]{0,1:T(8,128)S(1)}, f32[768,96]{0,1:T(8,128)}, u32[]{:S(2)}) copy-start(f32[768,96]{0,1:T(8,128)} %param.33) | copy-start | bytes 884740
  255.1 16.7 %copy-start.12 = (f32[2,192]{1,0:T(2,128)S(1)}, f32[2,192]{1,0:T(2,128)}, u32[]{:S(2)}) copy-start(f32[2,192]{1,0:T(2,128)} %param.36) | copy-start | bytes 4612
  255.1 16.7 %copy-start.14 = (f32[2,192]{1,0:T(2,128)S(1)}, f32[2,192]{1,0:T(2,128)}, u32[]{:S(2)}) copy-start(f32[2,192]{1,0:T(2,128)} %param.37) | copy-start | bytes 4612
  255.1 16.6 %copy-start.15 = (f32[2,192]{1,0:T(2,128)S(1)}, f32[2,192]{1,0:T(2,128)}, u32[]{:S(2)}) copy-start(f32[2,192]{1,0:T(2,128)} %param.38) | copy-start | bytes 4612
  255.1 17.9 %copy-start.16 = (f32[25]{0:T(128)S(1)}, f32[25]{0:T(128)}, u32[]{:S(2)}) copy-start(f32[25]{0:T(128)} %param.40) | copy-start | bytes 304
  255.1 17.9 %copy-start.17 = (f32[25]{0:T(128)S(1)}, f32[25]{0:T(128)}, u32[]{:S(2)}) copy-start(f32[25]{0:T(128)} %param.41) | copy-start | bytes 304
  255.1 19.1 %copy-start.6 = (bf16[192,2048]{1,0:T(8,128)(2,1)S(1)}, bf16[192,2048]{1,0:T(8,128)(2,1)}, u32[]{:S(2)}) copy-start(bf16[192,2048]{1,0:T(8,128)(2,1)} %get-tuple-element.92) | copy-start | bytes 2359300

commit v3 on v2

v3 whole, which is shorter than its diff:
```python
import functools
import math
from types import SimpleNamespace

import jax
import jax.numpy as jnp
from jax import lax
from jax.experimental import pallas as pl
from jax.experimental.pallas import tpu as pltpu
from jax.sharding import PartitionSpec as P

D = 768
HEAD = 64
STEP = 10
HALO = 256
LANES = 128


EPS_NORM = 1e-05
EPS_ADAM = 1e-08
BETA_ONE = 0.9
BETA_TWO = 0.95
RATE_MATRIX = 0.02
RATE_OUTPUT = 0.12
RATE_GAIN = 0.4
RATE_MIX = 0.05
DECAY = 0.1
MASKED = -1e30

MESH = pl.DeviceIdType.MESH
F32 = jnp.float32
BF16 = jnp.bfloat16
MIB = 1 << 20


def optimize(weight, gradient, first_moment, second_moment, rate, decay):
    first_moment = BETA_ONE * first_moment + (1.0 - BETA_ONE) * gradient
    second_moment = BETA_TWO * second_moment + (1.0 - BETA_TWO) * gradient * gradient
    first_fixed = first_moment / (1.0 - BETA_ONE**STEP)
    second_fixed = second_moment / (1.0 - BETA_TWO**STEP)
    weight = weight - rate * (first_fixed / (jnp.sqrt(second_fixed) + EPS_ADAM) + decay * weight)
    return (weight, first_moment, second_moment)


def flip(index, bit):
    return index + bit - 2 * bit * lax.rem(lax.div(index, jnp.int32(bit)), 2)


def flips(index, bits):
    for bit in bits:
        index = flip(index, bit)
    return index


def subsets(bits):
    found = [()]
    for bit in bits:
        found = found + [one + (bit,) for one in found]
    return found


def row_bits(rows):
    digits = [1 << place for place in range(rows.bit_length() - 1)]
    return digits[0], digits[1:]


def tiles(count, body):
    def step(at, carry):
        body(at)
        return carry

    lax.fori_loop(0, count, step, 0)


def lane_tile(at, size=LANES, base=0):
    return pl.ds(pl.multiple_of(base + at * size, LANES), size)


def dot(a, b):
    return jnp.dot(a, b, preferred_element_type=F32)


def dot_rows(a, b):
    return lax.dot_general(a, b, (((1,), (1,)), ((), ())), preferred_element_type=F32)


def dot_cols(a, b):
    return lax.dot_general(a, b, (((0,), (0,)), ((), ())), preferred_element_type=F32)


def greet(z, r, width, bits):
    bar = pltpu.get_barrier_semaphore()
    places = [(r, lax.rem(z + k, width)) for k in range(1, width)] + [(flip(r, b), z) for b in bits]
    for place in places:
        pl.semaphore_signal(bar, inc=1, device_id=place, device_id_type=MESH)
    pl.semaphore_wait(bar, len(places))


def at_steps(table):
    def hook(step):
        for at, actions in table.items():
            @pl.when(step == at)
            def _(actions=actions):
                for action in actions:
                    action()

    return hook


class Sends:
    def __init__(self, send, recv):
        self.send, self.recv, self.used = send, recv, 0

    def reserve(self, count):
        at = self.used
        self.used += count
        return at

    def copy(self, at, src, dst, place):
        return pltpu.make_async_remote_copy(
            src_ref=src, dst_ref=dst, send_sem=self.send.at[at], recv_sem=self.recv.at[at],
            device_id=place, device_id_type=MESH,
        )

    def make(self, src, dst, place):
        return self.copy(self.reserve(1), src, dst, place)


def arrival(z, at, width):
    found = 0
    for own in range(width):
        order = sorted(range(width), key=lambda w, own=own: (abs(w - own), w))
        for place, w in enumerate(order):
            if w:
                found = found + w * jnp.where((z == own) & (at == place), 1, 0)
    return found


class Plane:
    def __init__(self, chunk, z, r, width, rows, shard):
        self.core, self.bits = row_bits(rows)
        self.chunk, self.z, self.r, self.width, self.shard = chunk, z, r, width, shard
        self.hops = len(self.bits)
        self.per_slab = 2 ** (self.hops + 1) - 1

    def rows(self, index):
        return pl.ds(pl.multiple_of(index * self.shard, 16), self.shard)

    def bit(self, w, at):
        one, other = self.bits[at], self.bits[::-1][at]
        return one + (other - one) * lax.rem(w + self.chunk, 2)

    def place(self, index, w, code):
        for at in range(self.hops):
            if code >> at & 1:
                index = flip(index, self.bit(w, at))
        return index


class Gather(Plane):
    def __init__(self, sends, chunk, own, full, z, r, width, rows):
        super().__init__(chunk, z, r, width, rows, own.shape[0])
        self.sends, self.own, self.full = sends, own, full
        self.line_base = sends.reserve(2 * (width - 1))
        self.slab_base = sends.reserve(width * self.per_slab)

    @staticmethod
    def copies(width, rows):
        return 2 * (width - 1) + width * (rows // 2 * 2 - 1)

    def line(self, w, up, distance, target):
        part = self.full.at[w, self.rows(self.r)]
        at = self.line_base + (1 - up) * (self.width - 1) + distance
        return self.sends.copy(at, part, part, (self.r, target))

    def start(self):
        self.full[self.z, self.rows(self.r), :] = self.own[...]
        for up, there, target in ((1, self.z + 1 < self.width, self.z + 1), (0, self.z > 0, self.z - 1)):
            @pl.when(there)
            def _(up=up, target=target):
                self.line(self.z, up, 0, target).start()

        self.spread(self.z)

    def hop(self, w):
        up = jnp.where(w < self.z, 1, 0)
        distance = (self.z - w) * (2 * up - 1)
        self.line(w, up, distance - 1, self.z).wait_recv()
        self.spread(w)

    def onward(self, w):
        up = jnp.where(w < self.z, 1, 0)
        distance = (self.z - w) * (2 * up - 1)
        target = self.z + 2 * up - 1
        return (target >= 0) & (target < self.width), self.line(w, up, distance, target)

    def forward(self, w):
        there, copy = self.onward(w)

        @pl.when(there)
        def _():
            copy.start()

    def step(self, w, at):
        peer = flip(self.r, self.bit(w, at) if at < self.hops else self.core)
        found = []
        for code in range(2**at):
            part = self.full.at[w, self.rows(self.place(self.r, w, code))]
            found.append(self.sends.copy(self.slab_base + w * self.per_slab + 2**at - 1 + code, part, part, (peer, self.z)))
        return found

    def spread(self, w):
        for copy in self.step(w, 0):
            copy.start()

    def pass_on(self, w, at):
        for copy in self.step(w, at - 1):
            copy.wait_recv()
        for copy in self.step(w, at):
            copy.start()

    def to_chips(self, w):
        for at in range(1, self.hops):
            self.pass_on(w, at)

    def to_core(self, w):
        if self.hops:
            self.pass_on(w, self.hops)

    def take(self, w):
        for copy in self.step(w, self.hops):
            copy.wait_recv()

    def clear(self, w):
        for at in range(self.hops + 1):
            for copy in self.step(w, at):
                copy.wait_send()

        @pl.when(w == self.z)
        def _():
            for up, there, target in ((1, self.z + 1 < self.width, self.z + 1), (0, self.z > 0, self.z - 1)):
                @pl.when(there)
                def _(up=up, target=target):
                    self.line(self.z, up, 0, target).wait_send()

        there, onward = self.onward(w)

        @pl.when((w != self.z) & there)
        def _():
            onward.wait_send()


class Scatter(Plane):
    def __init__(self, sends, chunk, grads, boxes, last_box, total, z, r, width, rows):
        super().__init__(chunk, z, r, width, rows, total.shape[0])
        self.sends, self.grads, self.boxes, self.last_box, self.total = sends, grads, boxes, last_box, total
        self.other = flip(r, self.core)
        self.slab_base = sends.reserve(width * self.per_slab)
        self.width_base = sends.reserve(width - 1)

    @staticmethod
    def copies(width, rows):
        return width - 1 + width * (rows // 2 * 2 - 1)

    @staticmethod
    def box_shapes(width, rows, shard):
        hops = rows.bit_length() - 2
        return [(2 ** (hops - at), width, shard, D) for at in range(hops + 1)]

    def step(self, w, at):
        base = self.slab_base + w * self.per_slab
        if at == 0:
            return [
                self.sends.copy(base + code, self.grads.at[w, self.rows(self.place(self.other, w, code))], self.boxes[0].at[code, w], (self.other, self.z))
                for code in range(2**self.hops)
            ]
        base += sum(2 ** (self.hops - one) for one in range(at))
        peer = flip(self.r, self.bit(w, at - 1))
        return [
            self.sends.copy(base + code, self.boxes[at - 1].at[2 * code + 1, w], self.boxes[at].at[code, w], (peer, self.z))
            for code in range(2 ** (self.hops - at))
        ]

    def over_width(self, w):
        ahead = lax.rem(w - self.z + self.width, self.width)
        return self.sends.copy(
            self.width_base + ahead - 1, self.boxes[self.hops].at[0, w], self.last_box.at[ahead - 1], (self.r, w)
        )

    def begin(self, w):
        for copy in self.step(w, 0):
            copy.start()

    def take(self, w, at):
        for copy in self.step(w, at):
            copy.wait_recv()
        for code in range(2 ** (self.hops - at)):
            box = self.boxes[at].at[code, w]
            if at == 0:
                kept = self.grads.at[w, self.rows(self.place(self.r, w, code))]
            else:
                kept = self.boxes[at - 1].at[2 * code, w]
            box[...] = (box[...].astype(F32) + kept[...].astype(F32)).astype(BF16)
        if at < self.hops:
            for copy in self.step(w, at + 1):
                copy.start()
        else:
            @pl.when(w != self.z)
            def _():
                self.over_width(w).start()

    def take_core(self, w):
        self.take(w, 0)

    def take_chips(self, w):
        for at in range(1, self.hops):
            self.take(w, at)

    def take_last(self, w):
        if self.hops:
            self.take(w, self.hops)

    def finish(self):
        for ahead in range(1, self.width):
            self.over_width(lax.rem(self.z + ahead, self.width)).wait_recv()
        value = self.boxes[self.hops][0, self.z].astype(F32)
        for ahead in range(1, self.width):
            value = value + self.last_box[ahead - 1].astype(F32)
        self.total[...] = value

    def end(self):
        def one(w):
            for at in range(self.hops + 1):
                for copy in self.step(w, at):
                    copy.wait_send()

            @pl.when(w != self.z)
            def _():
                self.over_width(w).wait_send()

        tiles(self.width, one)


def mix_stream(mix_ref, pair_ref, out_ref, base, layers):
    features, size = pair_ref.shape[1], pair_ref.shape[2]
    strip = 16

    def body(at):
        rows = pl.ds(pl.multiple_of(at * strip, strip), strip)
        total = mix_ref[0] * pair_ref[0, rows, :].astype(F32)
        for j in range(1, layers):
            total = total + mix_ref[j] * pair_ref[j, rows, :].astype(F32)
        out_ref[rows, base] = total.astype(BF16)

    tiles(features // strip, body)


def spread_gains(box_ref, gain_ref, width, piece):
    for w in range(width):
        for i in range(2):
            row = box_ref[w, pl.ds(i, 1), :]
            full = jnp.transpose(jnp.broadcast_to(row, (LANES, row.shape[1])))
            gain_ref[i, pl.ds(w * piece, piece), :] = full[:piece]


def norm_forward(x_ref, x_base, gain_ref, i, out_ref, stat_ref, count):
    def body(at):
        cols = lane_tile(at)
        x = x_ref[:, lane_tile(at, base=x_base)].astype(F32)
        centre = jnp.sum(x, 0, keepdims=True) / D
        spread = jnp.sum(x * x, 0, keepdims=True) / D - centre * centre
        scaling = lax.rsqrt(spread + EPS_NORM)
        out_ref[:, cols] = (gain_ref[i] * ((x - centre) * scaling)).astype(BF16)
        stat_ref[0:1, cols] = centre
        stat_ref[1:2, cols] = scaling

    tiles(count // LANES, body)


def norm_back(u_ref, u_base, x_ref, x_base, stat_ref, stat_base, gain_ref, i, residual, write, gain_acc, start, count):
    def body(step):
        at = step + start // LANES
        u = u_ref[:, lane_tile(at, base=u_base)].astype(F32)
        x = x_ref[:, lane_tile(at, base=x_base)].astype(F32)
        cols = lane_tile(at, base=stat_base)
        scaling = stat_ref[1:2, cols]
        centred = (x - stat_ref[0:1, cols]) * scaling
        gain_acc[...] += u * centred
        s = u * gain_ref[i]
        mean_s = jnp.sum(s, 0, keepdims=True) / D
        mean_c = jnp.sum(s * centred, 0, keepdims=True) / D
        write(lane_tile(at), residual(lane_tile(at)) + scaling * (s - mean_s - centred * mean_c))

    tiles(count // LANES, body)


def document_starts(seg_ref, start_ref, trig_ref, row, own_at, own):
    seg = seg_ref[pl.ds(row, 1), :]
    length = seg.shape[1]
    place = lax.broadcasted_iota(jnp.int32, (8, length), 1)
    seg = jnp.broadcast_to(seg, (8, length))
    before = pltpu.roll(seg, 1, 1)
    start = jnp.where((place > 0) & (seg == before), 0, place)
    step = 1
    while step < length:
        moved = pltpu.roll(start, step, 1)
        start = jnp.maximum(start, jnp.where(place >= step, moved, 0))
        step *= 2
    position = (place - start).astype(F32)
    scratch = start_ref.at[0:8]
    ext = HALO + own
    scratch[:, pl.ds(0, HALO)] = jnp.zeros((8, HALO), F32)
    scratch[:, pl.ds(HALO, length)] = position
    window = scratch[:, pl.ds(pl.multiple_of(own_at, LANES), ext)][0:1]
    half = HEAD // 2
    freq = jnp.exp(
        lax.broadcasted_iota(jnp.int32, (half, ext), 0).astype(F32) * (-2.0 * math.log(10000.0) / HEAD)
    )
    angle = freq * window
    trig_ref[0] = jnp.cos(angle)
    trig_ref[1] = jnp.sin(angle)
    scratch[:, pl.ds(HALO, length)] = start.astype(F32)
    kept = scratch[:, pl.ds(pl.multiple_of(own_at, LANES), ext)]
    scratch[:, pl.ds(0, ext)] = kept - (own_at - HALO).astype(F32)


def rotated(heads, cosine, sine):
    half = HEAD // 2
    a, b = heads[:half], heads[half:]
    return jnp.concatenate([a * cosine - b * sine, b * cosine + a * sine], 0)


def project(x_ref, wa_ref, trig_ref, q_ref, k_ref, v_ref, wo_ref, w, per):
    group = per * HEAD
    scale = HEAD**-0.5
    turned = jnp.transpose(wa_ref[w])
    wo_ref[w] = turned[3 * group :]
    queries = dot(turned[:group], x_ref[:, HALO:])
    cosine, sine = trig_ref[0], trig_ref[1]
    for i in range(per):
        rows = queries[i * HEAD : (i + 1) * HEAD]
        q_ref[w * per + i] = (rotated(rows, cosine[:, HALO:], sine[:, HALO:]).astype(BF16) * scale).astype(BF16)
    keys = dot(turned[group : 2 * group], x_ref[...])
    for i in range(per):
        rows = keys[i * HEAD : (i + 1) * HEAD]
        k_ref[w * per + i] = rotated(rows, cosine, sine).astype(BF16)
    values = dot(turned[2 * group : 3 * group], x_ref[...])
    for i in range(per):
        v_ref[w * per + i] = values[i * HEAD : (i + 1) * HEAD].astype(BF16)


def attend_bias(start_ref, bias_ref):
    for b in range(bias_ref.shape[0]):
        key_at = lax.broadcasted_iota(jnp.int32, (2 * HALO, HALO), 0).astype(F32) + float(b * HALO)
        query_at = lax.broadcasted_iota(jnp.int32, (2 * HALO, HALO), 1).astype(F32) + float((b + 1) * HALO)
        first = start_ref[0:1, (b + 1) * HALO : (b + 2) * HALO]
        bias_ref[b] = jnp.where((key_at >= first) & (key_at <= query_at), 0.0, MASKED)


def attend(q_ref, k_ref, v_ref, bias_ref, p_ref, ao_ref, w, per):
    ao_ref[w, 0:HEAD, :] = jnp.zeros((HEAD, ao_ref.shape[2]), BF16)
    for i in range(per):
        h = w * per + i
        for b in range(bias_ref.shape[0]):
            keys = k_ref[h, :, b * HALO : (b + 2) * HALO]
            scores = dot_cols(keys, q_ref[h, :, b * HALO : (b + 1) * HALO]) + bias_ref[b]
            top = jnp.max(scores, 0, keepdims=True)
            raised = jnp.exp(scores - top)
            total = jnp.sum(raised, 0, keepdims=True)
            p_ref[h, b] = (raised * (1.0 / total)).astype(BF16)
            out = dot(v_ref[h, :, b * HALO : (b + 2) * HALO], p_ref[h, b])
            ao_ref[w, (i + 1) * HEAD : (i + 2) * HEAD, b * HALO : (b + 1) * HALO] = out.astype(BF16)


def out_project(st_ref, wa_ref, ao_ref, mid_ref, width, per):
    group = 3 * per * HEAD - HEAD
    mid_ref[...] = st_ref[:, HALO:].astype(F32)

    def body(w):
        mid_ref[...] += dot(wa_ref[w, :, group:], ao_ref[w])

    tiles(width, body)


def feed_forward(xt_ref, wb_ref, wc_ref, acc_ref, pre_ref, hid_ref, slope_ref, width, slab, before):
    own = xt_ref.shape[0]
    strip = 32

    def body(at):
        w = slab(at)
        before(at, w)
        pre_ref[...] = dot(xt_ref[...], wb_ref[w])

        def gelu(part):
            rows = pl.ds(pl.multiple_of(part * strip, strip), strip)
            x = pre_ref[rows, :]
            root = math.sqrt(2.0 / math.pi)
            square = x * x
            bent = jnp.tanh(root * (x + 0.044715 * (square * x)))
            hid_ref[w, rows, :] = (0.5 * x * (1.0 + bent)).astype(BF16)
            slope = 0.5 * (1.0 + bent) + (0.5 * root) * x * (1.0 - bent * bent) * (1.0 + (3 * 0.044715) * square)
            slope_ref[w, rows, :] = slope.astype(BF16)

        tiles(own // strip, gelu)
        acc_ref[...] += dot_rows(wc_ref[w], hid_ref[w])

    tiles(width, body)


def feed_back(x_ref, ct_ref, ctt_ref, wb_ref, wc_ref, gb_ref, gc_ref, u_ref, gh_ref, hid_ref, slope_ref, width, slab, between, after):
    own = x_ref.shape[1]
    strip = 32
    u_ref[...] = jnp.zeros_like(u_ref)

    def body(at):
        w = slab(at)
        gh_ref[...] = dot(ctt_ref[...], wc_ref[w])
        between(at, w)

        def multiply(part):
            rows = pl.ds(pl.multiple_of(part * strip, strip), strip)
            slope_ref[w, rows, :] = (gh_ref[rows, :] * slope_ref[w, rows, :].astype(F32)).astype(BF16)

        tiles(own // strip, multiply)
        gc_ref[w] = dot(ct_ref[...], hid_ref[w]).astype(BF16)
        u_ref[...] += dot_rows(wb_ref[w], slope_ref[w])
        gb_ref[w] = dot(x_ref[...], slope_ref[w]).astype(BF16)
        after(at, w)

    tiles(width, body)


def attend_back(low_ref, wo_ref, p_ref, q_ref, k_ref, v_ref, trig_ref, gp_ref, width, per, own, hook):
    ext = HALO + own
    group = per * HEAD
    blocks = own // HALO
    scale = HEAD**-0.5

    def body(w):
        hook(w)
        gp_ref[w, 3 * group :, :] = jnp.zeros((group, ext), BF16)
        gp_ref[w, :group, :HALO] = jnp.zeros((group, HALO), BF16)
        upstream = dot(wo_ref[w], low_ref[...]).astype(BF16)
        for i in range(per):
            h = w * per + i
            grad_keys, grad_values = [None] * (blocks + 1), [None] * (blocks + 1)
            for b in range(blocks):
                q = q_ref[h, :, b * HALO : (b + 1) * HALO]
                k = k_ref[h, :, b * HALO : (b + 2) * HALO]
                v = v_ref[h, :, b * HALO : (b + 2) * HALO]
                up = upstream[i * HEAD : (i + 1) * HEAD, b * HALO : (b + 1) * HALO]
                weights = p_ref[h, b]
                wide = weights.astype(F32)
                grad_weights = dot_cols(v, up)
                inner = jnp.sum(wide * grad_weights, 0, keepdims=True)
                grad_scores = (wide * (grad_weights - inner)).astype(BF16)
                gv = dot_rows(up, weights)
                gk = dot_rows(q, grad_scores)
                gq = dot(k, grad_scores) * scale
                cols = slice((b + 1) * HALO, (b + 2) * HALO)
                gp_ref[w, i * HEAD : (i + 1) * HEAD, cols] = rotated(gq, trig_ref[0, :, cols], -trig_ref[1, :, cols]).astype(BF16)
                for part in range(2):
                    piece = slice(part * HALO, (part + 1) * HALO)
                    at = b + part
                    grad_keys[at] = gk[:, piece] if grad_keys[at] is None else grad_keys[at] + gk[:, piece]
                    grad_values[at] = gv[:, piece] if grad_values[at] is None else grad_values[at] + gv[:, piece]
            for at in range(blocks + 1):
                cols = slice(at * HALO, (at + 1) * HALO)
                gp_ref[w, group + i * HEAD : group + (i + 1) * HEAD, cols] = rotated(
                    grad_keys[at], trig_ref[0, :, cols], -trig_ref[1, :, cols]
                ).astype(BF16)
                gp_ref[w, 2 * group + i * HEAD : 2 * group + (i + 1) * HEAD, cols] = grad_values[at].astype(BF16)

    tiles(width, body)


def stream_back(wa_ref, gp_ref, u_ref, start, size, width):
    cols = slice(start, start + size)
    u_ref[:, cols] = dot(wa_ref[0], gp_ref[0, :, cols])

    def body(at):
        u_ref[:, cols] += dot(wa_ref[at + 1], gp_ref[at + 1, :, cols])

    tiles(width - 1, body)


def project_back(x_ref, low_ref, ao_ref, gp_ref, ga_ref, width, per, slab, before, after):
    group = 3 * per * HEAD - HEAD

    def body(at):
        w = slab(at)
        before(at, w)
        ga_ref[w, :, :group] = dot_rows(x_ref[...], gp_ref[w, :group, :]).astype(BF16)
        ga_ref[w, :, group:] = (
            dot_rows(x_ref[...], gp_ref[w, group:, :]) + dot_rows(low_ref[...], ao_ref[w])
        ).astype(BF16)
        after(at, w)

    tiles(width, body)


def block_kernel(width, rows, per, mix_ref, hist_ref, cot_ref, seg_ref, box_ref, own_ref, given_ref,
                 gcol_ref, bout_ref, small_ref, total_ref, left_ref,
                 full, st, ct, boxes_in, gain, x_one, stat_one, starts, trig, q, k, v, wo, ao, prob, mid, stat_two, gmid, low, blk,
                 gacc_one, gacc_two, halo_out, halo_in, macc, small_out, small_in, small_step,
                 last_box, boxes, load_sem, here_sem, send_sem, recv_sem):
    r, z = lax.axis_index("rows"), lax.axis_index("width")
    layers, piece, tokens = hist_ref.shape
    own = tokens // width
    ext = HALO + own
    per_row = seg_ref.shape[1] // own
    core, bits = row_bits(rows)
    hops = len(bits)
    cut = own // 2
    greet(z, r, width, [core] + bits)
    sends = Sends(send_sem, recv_sem)
    inside = own_ref is not None
    gathers = []
    if inside:
        gathers = [Gather(sends, at, own_ref.at[at], full.at[at], z, r, width, rows) for at in range(3)]
        first, second, third = gathers
    slab = functools.partial(arrival, z, width=width)

    def each(*actions):
        for method, chosen, distances in actions:
            for away in distances:
                if away == 0:
                    for one in chosen:
                        getattr(one, method)(z)
                    continue
                for w, there in ((z - away, z >= away), (z + away, z + away < width)):
                    @pl.when(there)
                    def _(w=w, method=method, chosen=chosen):
                        for one in chosen:
                            getattr(one, method)(w)
    odd = lax.rem(z, 2) == 1
    mine = pl.ds(pl.multiple_of(z * piece, 16), piece)

    far = 1 - z // 2
    chunks = []
    for at in range(width):
        low_half = flip(far, 1) if at // 2 else far
        chunks.append(2 * low_half + at % 2)
    st_even = st.at[mine, pl.ds(HALO, own)]
    st_odd = st.at[mine, :]
    gain_sends = [sends.make(box_ref, boxes_in.at[z], (r, lax.rem(z + step, width))) for step in range(1, width)]
    base = sends.used
    sends.used += width - 1

    def scoped_stream(pair, mixed):
        def load(at):
            cols = pl.ds(pl.multiple_of(chunks[at // 2] * own + (at % 2) * cut, LANES), cut)
            return pltpu.make_async_copy(hist_ref.at[:, :, cols], pair.at[at % 3], load_sem.at[at % 3])

        def stream_copy(step, target, is_odd):
            start = pl.multiple_of(target * own, LANES)
            if is_odd:
                src, dst = mixed.at[:, pl.ds(pl.multiple_of(start - HALO, LANES), ext)], st_odd
            else:
                src, dst = mixed.at[:, pl.ds(start, own)], st_even
            return pltpu.make_async_remote_copy(
                src_ref=src, dst_ref=dst, send_sem=send_sem.at[base + step - 1], recv_sem=recv_sem.at[base + step - 1],
                device_id=(r, target), device_id_type=MESH,
            )

        for at in range(3):
            load(at).start()
        for gather in gathers:
            gather.start()
        for copy in gain_sends:
            copy.start()
        boxes_in[z] = box_ref[...]
        for at in range(2 * width):
            load(at).wait()
            target = chunks[at // 2]
            start = pl.multiple_of(target * own + (at % 2) * cut, LANES)
            mix_stream(mix_ref, pair.at[at % 3], mixed, pl.ds(start, cut), layers)
            if at + 3 < 2 * width:
                load(at + 3).start()
            if at % 2 == 0:
                continue
            is_odd = at // 2 % 2 == 1
            for step in range(1, width):
                @pl.when(lax.rem(z + step, width) == target)
                def _(step=step, target=target, is_odd=is_odd):
                    stream_copy(step, target, is_odd).start()

            @pl.when(target == z)
            def _(is_odd=is_odd, target=target):
                start = pl.multiple_of(target * own, LANES)
                if is_odd:
                    st_odd[...] = mixed[:, pl.ds(pl.multiple_of(start - HALO, LANES), ext)]
                else:
                    st_even[...] = mixed[:, pl.ds(start, own)]
                    st[:, 0:HALO] = jnp.zeros((D, HALO), BF16)

        if inside:
            each(("hop", gathers, [1]), ("forward", gathers, [1]), ("to_chips", gathers, [0]))
        for copy in gain_sends:
            copy.wait()
        spread_gains(boxes_in, gain, width, piece)
        document_starts(seg_ref, starts, trig, z // per_row, lax.rem(z, per_row) * own, own)
        if inside:
            each(
                ("to_chips", gathers, [1]), ("to_core", gathers, [0]), ("hop", gathers, [2]), ("forward", gathers, [2]),
                ("to_core", gathers, [1]), ("to_chips", gathers, [2]),
            )
        for step in range(1, width):
            for is_odd in (False, True):
                @pl.when(lax.rem(z, 2) == int(is_odd))
                def _(step=step, is_odd=is_odd):
                    stream_copy(step, z, is_odd).wait_recv()

                @pl.when(lax.rem(z + step, 2) == int(is_odd))
                def _(step=step, is_odd=is_odd):
                    stream_copy(step, lax.rem(z + step, width), is_odd).wait_send()

        cot_here.start()

    cot_sends = []
    for step in range(1, width):
        target = lax.rem(z + step, width)
        cols = pl.ds(pl.multiple_of(target * own, LANES), own)
        cot_sends.append(sends.make(cot_ref.at[:, cols], ct.at[mine, :], (r, target)))
    cot_here = pltpu.make_async_copy(
        cot_ref.at[:, pl.ds(pl.multiple_of(z * own, LANES), own)], ct.at[mine, :], here_sem
    )
    if not inside:
        given = pltpu.make_async_copy(given_ref, full, load_sem.at[3])
        given.start()
    pl.run_scoped(scoped_stream, pltpu.VMEM((3, layers, piece, cut), BF16), pltpu.VMEM((piece, tokens), BF16))

    norm_forward(st, 0, gain, 0, x_one, stat_one, ext)
    if not inside:
        given.wait()

    def send_cotangent():
        for copy in cot_sends:
            copy.start()

    def scoped_attend(bias):
        attend_bias(starts, bias)
        serve = at_steps({0: [send_cotangent]})
        if inside:
            serve = at_steps({
                0: [lambda: each(("hop", gathers, [3]), ("to_core", gathers, [2])), send_cotangent],
                1: [lambda: each(("to_chips", gathers, [3]))],
                2: [lambda: each(("to_core", gathers, [3]))],
            })

        def body(at):
            w = slab(at)
            serve(at)
            if inside:
                first.take(w)
            project(x_one, full.at[0], trig, q, k, v, wo, w, per)
            attend(q, k, v, bias, prob, ao, w, per)

        tiles(width, body)

    pl.run_scoped(scoped_attend, pltpu.VMEM((own // HALO, 2 * HALO, HALO), F32))
    out_project(st, full.at[0], ao, mid, width, per)
    gmid[...] = mid[...]
    if inside:
        tiles(width, first.clear)

    scatters = []
    if inside:
        scatters = [
            Scatter(sends, at, full.at[at], [box.at[at] for box in boxes], last_box.at[at], total_ref.at[at], z, r, width, rows)
            for at in range(3)
        ]
    attending, pair_back = scatters[:1], scatters[1:]

    def back(method, chosen, at):
        for one in chosen:
            getattr(one, method)(turned(at))

    def later(method, chosen, at):
        return lambda: back(method, chosen, at)

    def turned(at):
        return slab(width - 1 - at)


    def feed_before(at, w):
        if inside:
            second.take(w)
            third.take(w)

    def feed_between(at, w):
        if inside:
            second.clear(w)
            third.clear(w)

        feed_service(at)

    feed_service = at_steps({
        1: [later("take_core", pair_back, 0)],
        3: [later("take_chips", pair_back, 0), later("take_core", pair_back, 1)],
    })

    def feed_after(at, w):
        for scatter in pair_back:
            scatter.begin(w)

    blk_sends, gs_sends = [], []
    here = pl.ds(pl.multiple_of(z * own, LANES), own)
    for step in range(1, width):
        target = lax.rem(z + step, width)
        part = pl.ds(pl.multiple_of(target * piece, 16), piece)
        blk_sends.append(sends.make(blk.at[part, :], bout_ref.at[:, here], (r, target)))

    blk_here = pltpu.make_async_copy(blk.at[mine, :], bout_ref.at[:, here], load_sem.at[3])

    def scoped_feed(x_two, turn, pre, hid, slope, u_two):
        norm_forward(mid, 0, gain, 1, x_two, stat_two, own)
        turn[...] = jnp.transpose(x_two[...])
        feed_forward(turn, full.at[1], full.at[2], gmid, pre, hid, slope, width, slab, feed_before)
        blk[...] = gmid[...].astype(BF16)
        for copy in blk_sends:
            copy.start()
        blk_here.start()
        for copy in cot_sends:
            copy.wait()
        cot_here.wait()
        turn[...] = jnp.transpose(ct[...])
        feed_back(
            x_two, ct, turn, full.at[1], full.at[2], full.at[1], full.at[2], u_two, pre, hid, slope, width, turned, feed_between, feed_after
        )

        def write(cols, value):
            gmid[:, cols] = value
            low[:, cols] = value.astype(BF16)

        gacc_two[...] = jnp.zeros_like(gacc_two)
        norm_back(u_two, 0, mid, 0, stat_two, 0, gain, 1, lambda cols: ct[:, cols].astype(F32), write, gacc_two, 0, own)

    pl.run_scoped(
        scoped_feed, pltpu.VMEM((D, own), BF16), pltpu.VMEM((own, D), BF16), pltpu.VMEM((own, D), F32),
        pltpu.VMEM((width, own, D), BF16), pltpu.VMEM((width, own, D), BF16), pltpu.VMEM((D, own), F32),
    )

    when_attend = at_steps({
        2: [later("take_chips", pair_back, 1), later("take_core", pair_back, 2), later("take_last", pair_back, 0)],
    })
    when_mix = {
        3: [
            later("take_chips", attending, 0), later("take_chips", attending, 1), later("take_core", attending, 2),
            later("take_core", attending, 3), later("take_last", pair_back, 3),
        ],
        7: [
            later("take_chips", attending, 2), later("take_chips", attending, 3), later("take_last", attending, 0),
            later("take_last", attending, 1),
        ],
    }
    halo = sends.make(halo_out, halo_in, (r, flip(z, 1)))
    half = own // 2
    for part in range(2):
        columns = pl.ds(pl.multiple_of(z * own + part * half, LANES), half)
        for step in range(1, width):
            target = lax.rem(z + step, width)
            features = pl.ds(pl.multiple_of(target * piece, 16), piece)
            gs_sends.append(
                sends.make(blk.at[features, pl.ds(part * half, half)], gcol_ref.at[:, columns], (r, target))
            )

    def scoped_back(gp, u):
        def send_stream(part):
            def write(cols, value):
                blk[:, cols] = value.astype(BF16)

            norm_back(
                u, HALO, st, HALO, stat_one, HALO, gain, 0, lambda cols: gmid[:, cols], write, gacc_one, part * half, half
            )
            for copy in gs_sends[part * (width - 1) : (part + 1) * (width - 1)]:
                copy.start()
            columns = pl.ds(pl.multiple_of(z * own + part * half, LANES), half)
            gcol_ref[:, columns] = blk[mine, pl.ds(part * half, half)]

        attend_back(low, wo, prob, q, k, v, trig, gp, width, per, own, when_attend)
        stream_back(full.at[0], gp, u, 0, HALO, width)

        @pl.when(odd)
        def _():
            halo_out[...] = u[:, 0:HALO].astype(BF16)
            halo.start()

        stream_back(full.at[0], gp, u, HALO, own, width)
        gacc_one[...] = jnp.zeros_like(gacc_one)
        for copy in blk_sends:
            copy.wait_send()
        blk_here.wait()
        send_stream(0)
        back("take_chips", pair_back, 2)
        back("take_core", pair_back, 3)
        back("take_last", pair_back, 1)

        def after_project(at, w):
            for scatter in attending:
                scatter.begin(w)

        project_back(x_one, low, ao, gp, full.at[0], width, per, turned, lambda at, w: None, after_project)

        @pl.when(jnp.logical_not(odd))
        def _():
            halo.wait_recv()
            u[:, own : own + HALO] += halo_in[...].astype(F32)

        send_stream(1)
        back("take_chips", pair_back, 3)
        back("take_core", attending, 0)
        back("take_core", attending, 1)
        back("take_last", pair_back, 2)

    pl.run_scoped(scoped_back, pltpu.VMEM((width, 4 * per * HEAD, ext), BF16), pltpu.VMEM((D, ext), F32))

    macc[...] = jnp.zeros_like(macc)
    strip = 16

    def scoped_mix(pair):
        def place(at):
            chunk = lax.rem(z + width - at % width, width)
            return pl.ds(pl.multiple_of(chunk * own + (at // width) * half, LANES), half)

        def load(at):
            return pltpu.make_async_copy(hist_ref.at[:, :, place(at)], pair.at[at % 3], load_sem.at[at % 3])

        for at in range(3):
            load(at).start()
        for at in range(2 * width):
            if at % width:
                gs_sends[at // width * (width - 1) + at % width - 1].wait_recv()
            load(at).wait()
            cols = place(at)

            def body(row, at=at, cols=cols):
                part = pl.ds(pl.multiple_of(row * strip, strip), strip)
                g = gcol_ref[part, cols].astype(F32)
                for j in range(layers):
                    crossed = pair[at % 3, j, part, :].astype(F32) * g
                    folded = crossed[:8] + crossed[8:]
                    total = folded[:, :LANES]
                    for lane in range(1, cut // LANES):
                        total = total + folded[:, lane * LANES : (lane + 1) * LANES]
                    macc[j] += total

            tiles(piece // strip, body)
            if at + 3 < 2 * width:
                load(at + 3).start()
            for action in when_mix.get(at, ()):
                action()

    pl.run_scoped(scoped_mix, pltpu.VMEM((3, layers, piece, cut), BF16))

    small_out[...] = jnp.zeros_like(small_out)
    gain_one = jnp.sum(jnp.transpose(gacc_one[...]), 0, keepdims=True)
    gain_two = jnp.sum(jnp.transpose(gacc_two[...]), 0, keepdims=True)
    depth = jnp.sum(jnp.transpose(jnp.sum(macc[...], 1)), 0, keepdims=True)
    for w in range(width):
        small_out[w, 0:1, 0:piece] = gain_one[:, w * piece : (w + 1) * piece]
        small_out[w, 1:2, 0:piece] = gain_two[:, w * piece : (w + 1) * piece]
        small_out[w, 2:3, 0 : depth.shape[1]] = depth
    small_sends = [
        sends.make(small_out.at[lax.rem(z + step, width)], small_in.at[step - 1], (r, lax.rem(z + step, width)))
        for step in range(1, width)
    ]
    for copy in small_sends:
        copy.start()
    current = small_out[z]
    for step in range(1, width):
        small_sends[step - 1].wait_recv()
        current = current + small_in[step - 1]
    for at, bit in enumerate([core] + bits):
        small_step[at, 0] = current
        copy = sends.make(small_step.at[at, 0], small_step.at[at, 1], (flip(r, bit), z))
        copy.start()
        copy.wait_recv()
        current = current + small_step[at, 1]
        small_sends.append(copy)
    small_ref[...] = current
    back("take_last", attending, 2)
    back("take_last", attending, 3)
    for scatter in scatters:
        scatter.finish()
    for copy in blk_sends:
        copy.wait_recv()
    for copy in gs_sends + small_sends:
        copy.wait_send()

    @pl.when(odd)
    def _():
        halo.wait_send()

    for scatter in scatters:
        scatter.end()
    if not inside:
        leave = pltpu.make_async_copy(full, left_ref, load_sem.at[3])
        leave.start()
        leave.wait()


def vmem(count):
    return [pl.BlockSpec(memory_space=pltpu.VMEM)] * count


def shape(*sizes, dtype=F32):
    return jax.ShapeDtypeStruct(sizes, dtype)


def block(width, rows, mix, history, cotangent, segments, box, own_three):
    layers, piece, tokens = history.shape
    shard = own_three.shape[1]
    own = tokens // width
    ext = HALO + own
    heads = D // HEAD
    per = heads // width
    group = per * HEAD
    blocks = own // HALO
    digits = rows.bit_length() - 1
    inside = shard % 16 == 0
    any_space = pl.BlockSpec(memory_space=pl.ANY)
    ins = [mix, history, cotangent, segments, box]
    specs = [pl.BlockSpec(memory_space=pltpu.SMEM), any_space, any_space] + vmem(2)
    outs = [shape(piece, tokens, dtype=BF16), shape(piece, tokens, dtype=BF16), shape(8, 2 * LANES)]
    out_specs = vmem(1) + [any_space] + vmem(1)
    box_shapes = []
    if inside:
        ins, specs = ins + [own_three], specs + vmem(1)
        outs, out_specs = outs + [shape(3, shard, D)], out_specs + vmem(1)
        box_shapes = Scatter.box_shapes(width, rows, shard)
    else:
        gathered = lax.all_gather(lax.all_gather(own_three, "rows", axis=1, tiled=True), "width", axis=1)
        ins, specs = ins + [gathered], specs + [any_space]
        outs, out_specs = outs + [shape(3, width, D, D, dtype=BF16)], out_specs + [any_space]
    low = lambda *sizes: pltpu.VMEM(sizes, BF16)
    full = lambda *sizes: pltpu.VMEM(sizes, F32)
    scratch = [
        low(3, width, D, D), low(D, ext), low(D, own), full(width, 8, 2 * LANES), full(2, D, LANES), low(D, ext), full(8, ext),
        full(8, HALO + segments.shape[1]), full(2, HEAD // 2, ext), low(heads, HEAD, own), low(heads, HEAD, ext), low(heads, HEAD, ext),
        low(width, group, D), low(width, HEAD + group, own), low(heads, blocks, 2 * HALO, HALO), full(D, own), full(8, own),
        full(D, own), low(D, own), low(D, own), full(D, LANES), full(D, LANES), low(D, HALO), low(D, HALO), full(layers, 8, LANES),
        full(width, 8, 2 * LANES), full(width - 1, 8, 2 * LANES), full(digits, 2, 8, 2 * LANES),
    ]
    common = len(scratch)
    if inside:
        scratch += [low(3, width - 1, shard, D)] + [low(3, *one) for one in box_shapes]
    count = 6 * (width - 1) + 1 + (width - 1) + digits
    count += 3 * Gather.copies(width, rows) + 3 * Scatter.copies(width, rows)
    scratch += [
        pltpu.SemaphoreType.DMA((4,)), pltpu.SemaphoreType.DMA, pltpu.SemaphoreType.DMA((count,)), pltpu.SemaphoreType.DMA((count,)),
    ]

    def kernel(*refs):
        given, found, rest = refs[:6], refs[6:10], refs[10:]
        weights = (given[5], None) if inside else (None, given[5])
        results = (found[3], None) if inside else (None, found[3])
        kept, rest = rest[:common], rest[common:]
        last_box, boxes = None, ()
        if inside:
            last_box, boxes, rest = rest[0], rest[1 : 1 + len(box_shapes)], rest[1 + len(box_shapes) :]
        block_kernel(width, rows, per, *given[:5], *weights, *found[:3], *results, *kept, last_box, boxes, *rest)

    found = pl.pallas_call(
        kernel,
        out_shape=outs,
        in_specs=specs,
        out_specs=out_specs,
        scratch_shapes=scratch,
        compiler_params=pltpu.CompilerParams(collective_id=0, has_side_effects=True, vmem_limit_bytes=64 * MIB - 128 * 1024),
    )(*ins)
    if inside:
        return found
    total = lax.psum_scatter(found[3], "width", scatter_dimension=1)
    return (*found[:3], lax.psum_scatter(total, "rows", scatter_dimension=1, tiled=True).astype(F32))


def prepare_kernel(attend_ref, output_ref, expand_ref, reduce_ref, gains_ref, own_ref, box_ref):
    parts = [attend_ref[k] for k in range(3)] + [jnp.transpose(output_ref[...])]
    own_ref[0] = jnp.concatenate(parts, 1).astype(BF16)
    own_ref[1] = expand_ref[...].astype(BF16)
    own_ref[2] = reduce_ref[...].astype(BF16)
    box_ref[...] = jnp.zeros_like(box_ref)
    box_ref[0:2, 0 : gains_ref.shape[1]] = gains_ref[...]


def prepare(w_attend, w_output, w_expand, w_reduce, gains):
    shard, piece = w_expand.shape[0], gains.shape[1]
    if shard % 16 == 0:
        return pl.pallas_call(
            prepare_kernel,
            out_shape=[shape(3, shard, D, dtype=BF16), shape(8, 2 * LANES)],
            in_specs=vmem(5),
            out_specs=vmem(2),
            compiler_params=pltpu.CompilerParams(vmem_limit_bytes=60 * MIB),
        )(w_attend, w_output, w_expand, jnp.transpose(w_reduce), gains)
    first = jnp.concatenate([w_attend[0], w_attend[1], w_attend[2], jnp.transpose(w_output)], 1)
    own_three = jnp.stack([first, w_expand, jnp.transpose(w_reduce)]).astype(BF16)
    return own_three, jnp.pad(gains, ((0, 8 - gains.shape[0]), (0, 2 * LANES - piece)))


def finish_kernel(per_step, mix_ref, grad_ref, total_ref, out_ref, *refs):
    weights, (hist_ref, block_ref, *news) = refs[:12], refs[12:]
    at = pl.program_id(0)
    piece = grad_ref.shape[0]
    strip = 16

    def body(row):
        rows = pl.ds(pl.multiple_of(row * strip, strip), strip)
        g = grad_ref[rows, :].astype(F32)
        for j in range(per_step):
            hist_ref[j, rows, :] = (mix_ref[at * per_step + j] * g).astype(BF16)

    tiles(piece // strip, body)

    def update(which, gradient, rate):
        found = optimize(weights[3 * which][...], gradient, weights[3 * which + 1][...], weights[3 * which + 2][...], rate, DECAY)
        for ref, value in zip(news[3 * which : 3 * which + 3], found):
            ref[...] = value

    @pl.when(at == 0)
    def _():
        for k in range(3):
            gradient = total_ref[0, :, k * piece : (k + 1) * piece]
            found = optimize(weights[0][k], gradient, weights[1][k], weights[2][k], RATE_MATRIX, DECAY)
            for ref, value in zip(news[:3], found):
                ref[k] = value

    @pl.when(at == 1)
    def _():
        update(1, jnp.transpose(total_ref[0, :, 3 * piece :]), RATE_OUTPUT)

    @pl.when(at == 2)
    def _():
        update(2, total_ref[1], RATE_MATRIX)

    @pl.when(at == 3)
    def _():
        update(3, total_ref[2], RATE_MATRIX)
        block_ref[...] = out_ref[...]


def finish(mix, grad_stream, total, block_output, layers, weights):
    shard = total.shape[1]
    piece, tokens = grad_stream.shape
    if shard % 16 == 0 and layers % 5 == 0:
        weights = [jnp.transpose(one) if at // 3 == 3 else one for at, one in enumerate(weights)]
        held = [shape(*one.shape) for one in weights]
        per_step = layers // 5
        history_grad, block_output, *news = pl.pallas_call(
            functools.partial(finish_kernel, per_step),
            grid=(5,),
            out_shape=[shape(layers, piece, tokens, dtype=BF16), shape(piece, tokens, dtype=BF16)] + held,
            in_specs=[pl.BlockSpec(memory_space=pltpu.SMEM)] + vmem(3 + len(weights)),
            out_specs=[pl.BlockSpec((per_step, piece, tokens), lambda at: (at, 0, 0))] + vmem(1 + len(weights)),
            compiler_params=pltpu.CompilerParams(vmem_limit_bytes=60 * MIB),
        )(mix, grad_stream, total, block_output, *weights)
        return (history_grad, block_output, *[jnp.transpose(one) if at // 3 == 3 else one for at, one in enumerate(news)])
    history_grad = (mix[:, None, None] * grad_stream[None].astype(F32)).astype(BF16)
    first = total[0]
    gradients = (
        jnp.stack([first[:, k * piece : (k + 1) * piece] for k in range(3)]),
        jnp.transpose(first[:, 3 * piece :]), total[1], jnp.transpose(total[2]),
    )
    news = []
    for at, rate in enumerate((RATE_MATRIX, RATE_OUTPUT, RATE_MATRIX, RATE_MATRIX)):
        w, m, v = weights[3 * at : 3 * at + 3]
        news += optimize(w, gradients[at], m, v, rate, DECAY)
    return (history_grad, block_output, *news)


def on_device(
    width, rows, history, cotangent, segments, w_attend, m_attend, v_attend, w_output, m_output, v_output,
    w_expand, m_expand, v_expand, w_reduce, m_reduce, v_reduce, gains, m_gains, v_gains, mix, m_mix, v_mix,
):
    layers, piece, _ = history.shape
    own_three, box = prepare(w_attend, w_output, w_expand, w_reduce, gains)
    grad_stream, block_output, small, total = block(width, rows, mix, history, cotangent, segments, box, own_three)
    weights = (
        w_attend, m_attend, v_attend, w_output, m_output, v_output, w_expand, m_expand, v_expand, w_reduce, m_reduce, v_reduce,
    )
    history_grad, block_output, *news = finish(mix, grad_stream, total, block_output, layers, weights)
    new_gains = optimize(gains, small[0:2, :piece], m_gains, v_gains, RATE_GAIN, 0.0)
    new_mix = optimize(mix, small[2, :layers], m_mix, v_mix, RATE_MIX, 0.0)
    return (block_output, history_grad, *news, *new_gains, *new_mix)


def solution(mesh):
    square, tall, wide = P(None, "rows", "width"), P("width", "rows"), P("rows", "width")
    weights = (square,) * 3 + (tall,) * 3 + (wide,) * 3 + (tall,) * 3 + (P(None, "width"),) * 3 + (P(),) * 3
    return jax.shard_map(
        functools.partial(on_device, mesh.shape["width"], mesh.shape["rows"]),
        mesh=mesh,
        in_specs=(P(None, "width", "rows"), P("width", "rows"), P("rows", None)) + weights,
        out_specs=(P("width", "rows"), P(None, "width", "rows")) + weights,
        check_vma=False,
    )
```

time: 276 us -> 221 us (0.80)
  Pallas kernels: 247 us -> 217 us
  other arithmetic: 20.4 us -> 2.52 us
  local copies, waits for them, and re-layouts: 6.4 us -> 0.03 us
    pallas_call x1, Pallas kernels: 247 us -> 203 us  [block(): pl.pallas_call(kernel, out_shape=outs, in_specs=specs, out_specs=out_spec...]
    pallas_call x0 -> x2, Pallas kernels: none -> 13.7 us  [the longest x1 11.6 us: finish(): pl.pallas_call(functools.partial(finish_kernel, per_step), grid=(5,), out...]
    convert_element_type x2 -> x0, other arithmetic: 8.65 us -> none  [the longest x1 7.21 us: on_device(): (mix[:, None, None] * grad_stream[None].astype(F32)).astype(BF16)]
    sub x6 -> x2, other arithmetic: 7.85 us -> 2.52 us  [optimize(): weight - rate * (first_fixed / (jnp.sqrt(second_fixed) + EPS_ADAM) + deca...]
    unnamed x43 -> x12, local copies, waits for them, and re-layouts: 4.99 us -> 0.03 us
    another operation x5 -> x0, other arithmetic: 3.85 us -> none  [the longest x4 2.88 us: on_device(): jnp.stack([jnp.concatenate([w_attend[0], w_attend[1], w_attend[2], jnp.tr...]
where the time goes in v3:
time: 221 us; the launch traced here: 220 us
  Pallas kernels  217 us (98%)
  other arithmetic  2.52 us (1%)
    pallas_call x1, Pallas kernels, block(): pl.pallas_call(kernel, out_shape=outs, in_specs=specs, out_specs=out_spec...  203 us
    pallas_call x1, Pallas kernels, finish(): pl.pallas_call(functools.partial(finish_kernel, per_step), grid=(5,), out...  11.6 us

profile of v3, /device:TPU:0, one launch (start us, length us, event | category | flops | bytes accessed | tf_op | source)
XLA Modules:
  0.0 220.4 jit_solution(4770641851634918788)
XLA Ops:
  0.7 0.0 copy-start.1
  0.7 0.0 copy-start
  0.7 0.0 copy-start.5
  0.7 0.0 copy-start.4
  0.7 0.0 copy-start.3
  0.7 0.0 copy-start.2
  0.7 2.1 shard_map.356
  2.9 203.2 %shard_map.357 = (bf16[192,2048]{1,0:T(8,128)(2,1)}, bf16[192,2048]{1,0:T(8,128)(2,1)}, f32[8,256]{1,0:T(8,128)}, f32[3,96,768]{2,1,0:T(8,128)}) custom-call(f32[25]{0:T(128)} %mix_ref.1, bf16[25,192,2048]{2,1,0:T(8,128)(2,1)} %refs_1_.2, bf16[192,2048]{1,0:T(8,128)(2,1)} %refs_2_.2, s32[2,1024]{1,0:T(2,128)} %refs_3_.2, ...), custom_call_target="tpu_custom_call" | custom-call | tf_op jit(solution)/shard_map/pallas_call | solution.py:1064
  206.0 0.0 copy-done.1
  206.1 0.0 copy-done.5
  206.1 0.0 copy-done.4
  206.1 1.2 multiply_subtract_fusion.1
  207.3 0.0 copy-done
  207.3 0.0 copy-done.3
  207.3 0.0 copy-done.2
  207.3 1.3 multiply_subtract_fusion
  208.6 11.6 %shard_map.358 = (bf16[25,192,2048]{2,1,0:T(8,128)(2,1)}, bf16[192,2048]{1,0:T(8,128)(2,1)}, f32[3,96,192]{2,1,0:T(8,128)}, f32[3,96,192]{2,1,0:T(8,128)}, f32[3...) custom-call(f32[25]{0:T(128)} %mix_ref.1, ...), custom_call_target="tpu_custom_call" | custom-call | tf_op jit(solution)/shard_map/pallas_call | solution.py:1150
Async XLA Ops:
  0.7 205.4 %copy-start.1 = (f32[25]{0:T(128)S(1)}, f32[25]{0:T(128)}, u32[]{:S(2)}) copy-start(f32[25]{0:T(128)} %mix_ref.1) | copy-start | bytes 304
  0.7 206.6 %copy-start = (f32[2,192]{1,0:T(2,128)S(1)}, f32[2,192]{1,0:T(2,128)}, u32[]{:S(2)}) copy-start(f32[2,192]{1,0:T(2,128)} %gains_ref.1) | copy-start | bytes 4612
  0.7 205.4 %copy-start.5 = (f32[25]{0:T(128)S(1)}, f32[25]{0:T(128)}, u32[]{:S(2)}) copy-start(f32[25]{0:T(128)} %param.41) | copy-start | bytes 304
  0.7 205.4 %copy-start.4 = (f32[25]{0:T(128)S(1)}, f32[25]{0:T(128)}, u32[]{:S(2)}) copy-start(f32[25]{0:T(128)} %param.40) | copy-start | bytes 304
  0.7 206.6 %copy-start.3 = (f32[2,192]{1,0:T(2,128)S(1)}, f32[2,192]{1,0:T(2,128)}, u32[]{:S(2)}) copy-start(f32[2,192]{1,0:T(2,128)} %param.38) | copy-start | bytes 4612
  0.7 206.6 %copy-start.2 = (f32[2,192]{1,0:T(2,128)S(1)}, f32[2,192]{1,0:T(2,128)}, u32[]{:S(2)}) copy-start(f32[2,192]{1,0:T(2,128)} %param.37) | copy-start | bytes 4612

commit v4 on v3

--- a/solution.py
+++ b/solution.py
@@ -173,14 +173,14 @@
         at = self.line_base + (1 - up) * (self.width - 1) + distance
         return self.sends.copy(at, part, part, (self.r, target))
 
-    def start(self):
+    def hold(self):
         self.full[self.z, self.rows(self.r), :] = self.own[...]
+
+    def start(self, w):
         for up, there, target in ((1, self.z + 1 < self.width, self.z + 1), (0, self.z > 0, self.z - 1)):
             @pl.when(there)
             def _(up=up, target=target):
                 self.line(self.z, up, 0, target).start()
-
-        self.spread(self.z)
 
     def hop(self, w):
         up = jnp.where(w < self.z, 1, 0)
@@ -251,16 +251,17 @@
 
 
 class Scatter(Plane):
-    def __init__(self, sends, chunk, grads, boxes, last_box, total, z, r, width, rows):
+    def __init__(self, sends, chunk, along, grads, boxes, last_box, total, z, r, width, rows):
         super().__init__(chunk, z, r, width, rows, total.shape[0])
         self.sends, self.grads, self.boxes, self.last_box, self.total = sends, grads, boxes, last_box, total
+        self.along = along
         self.other = flip(r, self.core)
         self.slab_base = sends.reserve(width * self.per_slab)
-        self.width_base = sends.reserve(width - 1)
+        self.width_base = sends.reserve(width + 1)
 
     @staticmethod
     def copies(width, rows):
-        return width - 1 + width * (rows // 2 * 2 - 1)
+        return width + 1 + width * (rows // 2 * 2 - 1)
 
     @staticmethod
     def box_shapes(width, rows, shard):
@@ -282,10 +283,28 @@
         ]
 
     def over_width(self, w):
-        ahead = lax.rem(w - self.z + self.width, self.width)
-        return self.sends.copy(
-            self.width_base + ahead - 1, self.boxes[self.hops].at[0, w], self.last_box.at[ahead - 1], (self.r, w)
-        )
+        if self.along:
+            target = self.z + jnp.where(w > self.z, 1, -1)
+            slot = jnp.where((target == w) & (w < self.z), self.width, w)
+        else:
+            target = w
+            slot = lax.rem(w - self.z + self.width, self.width) - 1
+        return self.sends.copy(self.width_base + slot, self.boxes[self.hops].at[0, w], self.last_box.at[slot], (self.r, target))
+
+    def came(self, slot):
+        return self.sends.copy(self.width_base + slot, self.last_box.at[slot], self.last_box.at[slot], (self.r, flip(self.z, 1)))
+
+    def awaited(self, w):
+        return jnp.where(w > self.z, self.z, self.width - 1 - self.z) > 0
+
+    def relay(self, w):
+        if self.along:
+            @pl.when((w != self.z) & self.awaited(w))
+            def _():
+                self.came(w).wait_recv()
+                box = self.boxes[self.hops].at[0, w]
+                box[...] = (box[...].astype(F32) + self.last_box[w].astype(F32)).astype(BF16)
+                self.over_width(w).start()
 
     def begin(self, w):
         for copy in self.step(w, 0):
@@ -305,7 +324,7 @@
             for copy in self.step(w, at + 1):
                 copy.start()
         else:
-            @pl.when(w != self.z)
+            @pl.when((w != self.z) & jnp.logical_not(self.awaited(w)) if self.along else w != self.z)
             def _():
                 self.over_width(w).start()
 
@@ -321,12 +340,16 @@
             self.take(w, self.hops)
 
     def finish(self):
-        for ahead in range(1, self.width):
-            self.over_width(lax.rem(self.z + ahead, self.width)).wait_recv()
-        value = self.boxes[self.hops][0, self.z].astype(F32)
-        for ahead in range(1, self.width):
-            value = value + self.last_box[ahead - 1].astype(F32)
-        self.total[...] = value
+        self.total[...] = self.boxes[self.hops][0, self.z].astype(F32)
+        if self.along:
+            arrivals = ((self.z, self.z > 0), (self.width, self.z < self.width - 1))
+        else:
+            arrivals = [(slot, self.z >= 0) for slot in range(self.width - 1)]
+        for slot, there in arrivals:
+            @pl.when(there)
+            def _(slot=slot):
+                self.came(slot).wait_recv()
+                self.total[...] += self.last_box[slot].astype(F32)
 
     def end(self):
         def one(w):
@@ -430,11 +453,10 @@
     return jnp.concatenate([a * cosine - b * sine, b * cosine + a * sine], 0)
 
 
-def project(x_ref, wa_ref, trig_ref, q_ref, k_ref, v_ref, wo_ref, w, per):
+def project(x_ref, wa_ref, trig_ref, q_ref, k_ref, v_ref, w, per):
     group = per * HEAD
     scale = HEAD**-0.5
     turned = jnp.transpose(wa_ref[w])
-    wo_ref[w] = turned[3 * group :]
     queries = dot(turned[:group], x_ref[:, HALO:])
     cosine, sine = trig_ref[0], trig_ref[1]
     for i in range(per):
@@ -530,7 +552,7 @@
     tiles(width, body)
 
 
-def attend_back(low_ref, wo_ref, p_ref, q_ref, k_ref, v_ref, trig_ref, gp_ref, width, per, own, hook):
+def attend_back(low_ref, wa_ref, p_ref, q_ref, k_ref, v_ref, trig_ref, gp_ref, width, per, own, hook):
     ext = HALO + own
     group = per * HEAD
     blocks = own // HALO
@@ -540,7 +562,8 @@
         hook(w)
         gp_ref[w, 3 * group :, :] = jnp.zeros((group, ext), BF16)
         gp_ref[w, :group, :HALO] = jnp.zeros((group, HALO), BF16)
-        upstream = dot(wo_ref[w], low_ref[...]).astype(BF16)
+        turned = jnp.transpose(wa_ref[w, :, 3 * group - HEAD :])
+        upstream = dot(turned[HEAD:], low_ref[...]).astype(BF16)
         for i in range(per):
             h = w * per + i
             grad_keys, grad_values = [None] * (blocks + 1), [None] * (blocks + 1)
@@ -601,7 +624,7 @@
 
 def block_kernel(width, rows, per, mix_ref, hist_ref, cot_ref, seg_ref, box_ref, own_ref, given_ref,
                  gcol_ref, bout_ref, small_ref, total_ref, left_ref,
-                 full, st, ct, boxes_in, gain, x_one, stat_one, starts, trig, q, k, v, wo, ao, prob, mid, stat_two, gmid, low, blk,
+                 full, st, ct, boxes_in, gain, x_one, stat_one, starts, trig, q, k, v, ao, prob, mid, stat_two, gmid, low, blk,
                  gacc_one, gacc_two, halo_out, halo_in, macc, small_out, small_in, small_step,
                  last_box, boxes, load_sem, here_sem, send_sem, recv_sem):
     r, z = lax.axis_index("rows"), lax.axis_index("width")
@@ -619,6 +642,7 @@
     if inside:
         gathers = [Gather(sends, at, own_ref.at[at], full.at[at], z, r, width, rows) for at in range(3)]
         first, second, third = gathers
+    others = gathers[1:]
     slab = functools.partial(arrival, z, width=width)
 
     def each(*actions):
@@ -665,11 +689,17 @@
 
         for at in range(3):
             load(at).start()
-        for gather in gathers:
-            gather.start()
         for copy in gain_sends:
             copy.start()
         boxes_in[z] = box_ref[...]
+        when_stream = {}
+        if inside:
+            for gather in gathers:
+                gather.hold()
+            first.start(z)
+            for gather in gathers:
+                gather.spread(z)
+            when_stream = {4: [lambda: each(("hop", [first], [1]), ("forward", [first], [1]))]}
         for at in range(2 * width):
             load(at).wait()
             target = chunks[at // 2]
@@ -677,9 +707,13 @@
             mix_stream(mix_ref, pair.at[at % 3], mixed, pl.ds(start, cut), layers)
             if at + 3 < 2 * width:
                 load(at + 3).start()
-            if at % 2 == 0:
-                continue
-            is_odd = at // 2 % 2 == 1
+            for action in when_stream.get(at, ()):
+                action()
+
+        if inside:
+            each(("hop", [first], [2]), ("forward", [first], [2]))
+        for at in range(width):
+            target, is_odd = chunks[at], at % 2 == 1
             for step in range(1, width):
                 @pl.when(lax.rem(z + step, width) == target)
                 def _(step=step, target=target, is_odd=is_odd):
@@ -695,15 +729,16 @@
                     st[:, 0:HALO] = jnp.zeros((D, HALO), BF16)
 
         if inside:
-            each(("hop", gathers, [1]), ("forward", gathers, [1]), ("to_chips", gathers, [0]))
+            each(("to_chips", [first], [0]))
         for copy in gain_sends:
             copy.wait()
         spread_gains(boxes_in, gain, width, piece)
         document_starts(seg_ref, starts, trig, z // per_row, lax.rem(z, per_row) * own, own)
         if inside:
             each(
-                ("to_chips", gathers, [1]), ("to_core", gathers, [0]), ("hop", gathers, [2]), ("forward", gathers, [2]),
-                ("to_core", gathers, [1]), ("to_chips", gathers, [2]),
+                ("to_chips", [first], [1]), ("to_core", [first], [0]),
+                ("to_chips", others, [0]), ("hop", [first], [3]), ("start", others, [0]), ("to_chips", [first], [2]),
+                ("to_core", [first], [1]), ("to_core", others, [0]),
             )
         for step in range(1, width):
             for is_odd in (False, True):
@@ -740,26 +775,30 @@
 
     def scoped_attend(bias):
         attend_bias(starts, bias)
-        serve = at_steps({0: [send_cotangent]})
         if inside:
             serve = at_steps({
-                0: [lambda: each(("hop", gathers, [3]), ("to_core", gathers, [2])), send_cotangent],
-                1: [lambda: each(("to_chips", gathers, [3]))],
-                2: [lambda: each(("to_core", gathers, [3]))],
+                0: [lambda: each(("to_core", [first], [2]))],
+                1: [lambda: each(("to_chips", [first], [3]), ("hop", others, [1]), ("forward", others, [1]))],
+                2: [lambda: each(("to_core", [first], [3]))],
+                3: [lambda: each(("to_chips", others, [1]), ("hop", others, [2]), ("forward", others, [2]))],
             })
 
         def body(at):
             w = slab(at)
-            serve(at)
+            if inside:
+                serve(at)
             if inside:
                 first.take(w)
-            project(x_one, full.at[0], trig, q, k, v, wo, w, per)
+            project(x_one, full.at[0], trig, q, k, v, w, per)
             attend(q, k, v, bias, prob, ao, w, per)
 
         tiles(width, body)
 
     pl.run_scoped(scoped_attend, pltpu.VMEM((own // HALO, 2 * HALO, HALO), F32))
     out_project(st, full.at[0], ao, mid, width, per)
+    if inside:
+        each(("to_core", others, [1]), ("to_chips", others, [2]), ("hop", others, [3]))
+    send_cotangent()
     gmid[...] = mid[...]
     if inside:
         tiles(width, first.clear)
@@ -767,7 +806,7 @@
     scatters = []
     if inside:
         scatters = [
-            Scatter(sends, at, full.at[at], [box.at[at] for box in boxes], last_box.at[at], total_ref.at[at], z, r, width, rows)
+            Scatter(sends, at, at > 0, full.at[at], [box.at[at] for box in boxes], last_box.at[at], total_ref.at[at], z, r, width, rows)
             for at in range(3)
         ]
     attending, pair_back = scatters[:1], scatters[1:]
@@ -783,7 +822,16 @@
         return slab(width - 1 - at)
 
 
+    late = at_steps({})
+    if inside:
+        late = at_steps({
+            0: [lambda: each(("to_core", others, [2]))],
+            1: [lambda: each(("to_chips", others, [3]))],
+            2: [lambda: each(("to_core", others, [3]))],
+        })
+
     def feed_before(at, w):
+        late(at)
         if inside:
             second.take(w)
             third.take(w)
@@ -842,17 +890,13 @@
     )
 
     when_attend = at_steps({
-        2: [later("take_chips", pair_back, 1), later("take_core", pair_back, 2), later("take_last", pair_back, 0)],
+        1: [later("take_last", pair_back, 0)],
+        2: [later("take_chips", pair_back, 1), later("take_core", pair_back, 2)],
+        3: [later("relay", pair_back, 0)],
     })
+    when_project = at_steps({3: [later("take_core", attending, 0), later("take_core", attending, 1)]})
     when_mix = {
-        3: [
-            later("take_chips", attending, 0), later("take_chips", attending, 1), later("take_core", attending, 2),
-            later("take_core", attending, 3), later("take_last", pair_back, 3),
-        ],
-        7: [
-            later("take_chips", attending, 2), later("take_chips", attending, 3), later("take_last", attending, 0),
-            later("take_last", attending, 1),
-        ],
+        0: [later("take_chips", attending, 0), later("take_chips", attending, 1)],
     }
     halo = sends.make(halo_out, halo_in, (r, flip(z, 1)))
     half = own // 2
@@ -878,7 +922,7 @@
             columns = pl.ds(pl.multiple_of(z * own + part * half, LANES), half)
             gcol_ref[:, columns] = blk[mine, pl.ds(part * half, half)]
 
-        attend_back(low, wo, prob, q, k, v, trig, gp, width, per, own, when_attend)
+        attend_back(low, full.at[0], prob, q, k, v, trig, gp, width, per, own, when_attend)
         stream_back(full.at[0], gp, u, 0, HALO, width)
 
         @pl.when(odd)
@@ -886,21 +930,26 @@
             halo_out[...] = u[:, 0:HALO].astype(BF16)
             halo.start()
 
+        back("take_chips", pair_back, 2)
+        back("take_core", pair_back, 3)
         stream_back(full.at[0], gp, u, HALO, own, width)
         gacc_one[...] = jnp.zeros_like(gacc_one)
         for copy in blk_sends:
             copy.wait_send()
         blk_here.wait()
         send_stream(0)
-        back("take_chips", pair_back, 2)
-        back("take_core", pair_back, 3)
         back("take_last", pair_back, 1)
 
         def after_project(at, w):
             for scatter in attending:
                 scatter.begin(w)
 
-        project_back(x_one, low, ao, gp, full.at[0], width, per, turned, lambda at, w: None, after_project)
+        project_back(x_one, low, ao, gp, full.at[0], width, per, turned, lambda at, w: when_project(at), after_project)
+        back("relay", pair_back, 1)
+        back("take_last", pair_back, 2)
+        back("take_chips", pair_back, 3)
+        back("take_core", attending, 2)
+        back("take_core", attending, 3)
 
         @pl.when(jnp.logical_not(odd))
         def _():
@@ -908,10 +957,8 @@
             u[:, own : own + HALO] += halo_in[...].astype(F32)
 
         send_stream(1)
-        back("take_chips", pair_back, 3)
-        back("take_core", attending, 0)
-        back("take_core", attending, 1)
-        back("take_last", pair_back, 2)
+        back("relay", pair_back, 2)
+        back("take_last", pair_back, 3)
 
     pl.run_scoped(scoped_back, pltpu.VMEM((width, 4 * per * HEAD, ext), BF16), pltpu.VMEM((D, ext), F32))
 
@@ -967,6 +1014,8 @@
     ]
     for copy in small_sends:
         copy.start()
+    back("take_last", attending, 0)
+    back("take_last", attending, 1)
     current = small_out[z]
     for step in range(1, width):
         small_sends[step - 1].wait_recv()
@@ -975,6 +1024,9 @@
         small_step[at, 0] = current
         copy = sends.make(small_step.at[at, 0], small_step.at[at, 1], (flip(r, bit), z))
         copy.start()
+        if at == 0:
+            back("take_chips", attending, 2)
+            back("take_chips", attending, 3)
         copy.wait_recv()
         current = current + small_step[at, 1]
         small_sends.append(copy)
@@ -1038,13 +1090,13 @@
     scratch = [
         low(3, width, D, D), low(D, ext), low(D, own), full(width, 8, 2 * LANES), full(2, D, LANES), low(D, ext), full(8, ext),
         full(8, HALO + segments.shape[1]), full(2, HEAD // 2, ext), low(heads, HEAD, own), low(heads, HEAD, ext), low(heads, HEAD, ext),
-        low(width, group, D), low(width, HEAD + group, own), low(heads, blocks, 2 * HALO, HALO), full(D, own), full(8, own),
+        low(width, HEAD + group, own), low(heads, blocks, 2 * HALO, HALO), full(D, own), full(8, own),
         full(D, own), low(D, own), low(D, own), full(D, LANES), full(D, LANES), low(D, HALO), low(D, HALO), full(layers, 8, LANES),
         full(width, 8, 2 * LANES), full(width - 1, 8, 2 * LANES), full(digits, 2, 8, 2 * LANES),
     ]
     common = len(scratch)
     if inside:
-        scratch += [low(3, width - 1, shard, D)] + [low(3, *one) for one in box_shapes]
+        scratch += [low(3, width + 1, shard, D)] + [low(3, *one) for one in box_shapes]
     count = 6 * (width - 1) + 1 + (width - 1) + digits
     count += 3 * Gather.copies(width, rows) + 3 * Scatter.copies(width, rows)
     scratch += [

time: 221 us -> 200 us (0.905)
  Pallas kernels: 217 us -> 196 us
    pallas_call x1, Pallas kernels: 203 us -> 182 us  [block(): pl.pallas_call(kernel, out_shape=outs, in_specs=specs, out_specs=out_spec...]
where the time goes in v4:
time: 200 us
  Pallas kernels  196 us (98%)
  other arithmetic  2.52 us (1%)
    pallas_call x1, Pallas kernels, block(): pl.pallas_call(kernel, out_shape=outs, in_specs=specs, out_specs=out_spec...  182 us
    pallas_call x1, Pallas kernels, finish(): pl.pallas_call(functools.partial(finish_kernel, per_step), grid=(5,), out...  11.6 us

profile of v4, /device:TPU:0, one launch (start us, length us, event | category | flops | bytes accessed | tf_op | source)
XLA Modules:
  0.0 199.5 jit_solution(6578542443056357330)
XLA Ops:
  0.7 0.0 copy-start.1
  0.7 0.0 copy-start
  0.7 0.0 copy-start.5
  0.7 0.0 copy-start.4
  0.7 0.0 copy-start.3
  0.7 0.0 copy-start.2
  0.7 2.1 %shard_map.356 = (bf16[3,96,768]{2,1,0:T(8,128)(2,1)}, f32[8,256]{1,0:T(8,128)}) custom-call(f32[3,96,192]{2,1,0:T(8,128)} %refs_0_.3, f32[192,96]{1,0:T(8,128)} %refs_3_.3, f32[96,768]{1,0:T(8,128)} %refs_6_.1, f32[96,768]{1,0:T(8,128)} %bitcast.13, f32[2,192]{1,0:T(2,128)} %gains_ref.1), custom_call_target="tpu_custom_call" | custom-call | tf_op jit(solution)/shard_map/pallas_call | solution.py:1142
  2.9 182.3 %shard_map.357 = (bf16[192,2048]{1,0:T(8,128)(2,1)}, bf16[192,2048]{1,0:T(8,128)(2,1)}, f32[8,256]{1,0:T(8,128)}, f32[3,96,768]{2,1,0:T(8,128)}) custom-call(f32[25]{0:T(128)} %mix_ref.1, bf16[25,192,2048]{2,1,0:T(8,128)(2,1)} %refs_1_.2, bf16[192,2048]{1,0:T(8,128)(2,1)} %refs_2_.2, s32[2,1024]{1,0:T(2,128)} %refs_3_.2, ...), custom_call_target="tpu_custom_call" | custom-call | tf_op jit(solution)/shard_map/pallas_call | solution.py:1116
  185.2 0.0 copy-done.1
  185.2 0.0 copy-done.5
  185.2 0.0 copy-done.4
  185.2 1.2 multiply_subtract_fusion.1
  186.4 0.0 copy-done
  186.4 0.0 copy-done.3
  186.4 0.0 copy-done.2
  186.4 1.3 multiply_subtract_fusion
  187.7 11.6 %shard_map.358 = (bf16[25,192,2048]{2,1,0:T(8,128)(2,1)}, bf16[192,2048]{1,0:T(8,128)(2,1)}, f32[3,96,192]{2,1,0:T(8,128)}, f32[3,96,192]{2,1,0:T(8,128)}, f32[3...) custom-call(f32[25]{0:T(128)} %mix_ref.1, ...), custom_call_target="tpu_custom_call" | custom-call | tf_op jit(solution)/shard_map/pallas_call | solution.py:1202
Async XLA Ops:
  0.7 184.5 %copy-start.1 = (f32[25]{0:T(128)S(1)}, f32[25]{0:T(128)}, u32[]{:S(2)}) copy-start(f32[25]{0:T(128)} %mix_ref.1) | copy-start | bytes 304
  0.7 185.8 %copy-start = (f32[2,192]{1,0:T(2,128)S(1)}, f32[2,192]{1,0:T(2,128)}, u32[]{:S(2)}) copy-start(f32[2,192]{1,0:T(2,128)} %gains_ref.1) | copy-start | bytes 4612
  0.7 184.5 %copy-start.5 = (f32[25]{0:T(128)S(1)}, f32[25]{0:T(128)}, u32[]{:S(2)}) copy-start(f32[25]{0:T(128)} %param.41) | copy-start | bytes 304
  0.7 184.5 %copy-start.4 = (f32[25]{0:T(128)S(1)}, f32[25]{0:T(128)}, u32[]{:S(2)}) copy-start(f32[25]{0:T(128)} %param.40) | copy-start | bytes 304
  0.7 185.7 %copy-start.3 = (f32[2,192]{1,0:T(2,128)S(1)}, f32[2,192]{1,0:T(2,128)}, u32[]{:S(2)}) copy-start(f32[2,192]{1,0:T(2,128)} %param.38) | copy-start | bytes 4612
  0.7 185.7 %copy-start.2 = (f32[2,192]{1,0:T(2,128)S(1)}, f32[2,192]{1,0:T(2,128)}, u32[]{:S(2)}) copy-start(f32[2,192]{1,0:T(2,128)} %param.37) | copy-start | bytes 4612

commit v5 on v4

--- a/solution.py
+++ b/solution.py
@@ -88,9 +88,17 @@
     return lax.dot_general(a, b, (((0,), (0,)), ((), ())), preferred_element_type=F32)
 
 
-def greet(z, r, width, bits):
+def plane_peers(r, rows):
+    core, bits = row_bits(rows)
+    chosen = [one for one in subsets([core] + bits) if one]
+    if rows > 8:
+        chosen = [(bit,) for bit in [core] + bits]
+    return [flips(r, one) for one in chosen]
+
+
+def greet(z, r, width, rows):
     bar = pltpu.get_barrier_semaphore()
-    places = [(r, lax.rem(z + k, width)) for k in range(1, width)] + [(flip(r, b), z) for b in bits]
+    places = [(r, lax.rem(z + k, width)) for k in range(1, width)] + [(peer, z) for peer in plane_peers(r, rows)]
     for place in places:
         pl.semaphore_signal(bar, inc=1, device_id=place, device_id_type=MESH)
     pl.semaphore_wait(bar, len(places))
@@ -141,7 +149,7 @@
         self.core, self.bits = row_bits(rows)
         self.chunk, self.z, self.r, self.width, self.shard = chunk, z, r, width, shard
         self.hops = len(self.bits)
-        self.per_slab = 2 ** (self.hops + 1) - 1
+        self.per_slab = self.hops + 1
 
     def rows(self, index):
         return pl.ds(pl.multiple_of(index * self.shard, 16), self.shard)
@@ -166,7 +174,7 @@
 
     @staticmethod
     def copies(width, rows):
-        return 2 * (width - 1) + width * (rows // 2 * 2 - 1)
+        return 2 * (width - 1) + width * (rows.bit_length() - 1)
 
     def line(self, w, up, distance, target):
         part = self.full.at[w, self.rows(self.r)]
@@ -206,16 +214,19 @@
         found = []
         for code in range(2**at):
             part = self.full.at[w, self.rows(self.place(self.r, w, code))]
-            found.append(self.sends.copy(self.slab_base + w * self.per_slab + 2**at - 1 + code, part, part, (peer, self.z)))
+            found.append(self.sends.copy(self.slab_base + w * self.per_slab + at, part, part, (peer, self.z)))
         return found
+
+    def whole(self, w, at):
+        part = self.full.at[w, pl.ds(0, 2**at * self.shard)]
+        return self.sends.copy(self.slab_base + w * self.per_slab + at, part, part, (flip(self.r, self.core), self.z))
 
     def spread(self, w):
         for copy in self.step(w, 0):
             copy.start()
 
     def pass_on(self, w, at):
-        for copy in self.step(w, at - 1):
-            copy.wait_recv()
+        self.whole(w, at - 1).wait_recv()
         for copy in self.step(w, at):
             copy.start()
 
@@ -228,13 +239,11 @@
             self.pass_on(w, self.hops)
 
     def take(self, w):
-        for copy in self.step(w, self.hops):
-            copy.wait_recv()
+        self.whole(w, self.hops).wait_recv()
 
     def clear(self, w):
         for at in range(self.hops + 1):
-            for copy in self.step(w, at):
-                copy.wait_send()
+            self.whole(w, at).wait_send()
 
         @pl.when(w == self.z)
         def _():
@@ -261,7 +270,7 @@
 
     @staticmethod
     def copies(width, rows):
-        return width + 1 + width * (rows // 2 * 2 - 1)
+        return width + 1 + width * (rows.bit_length() - 1)
 
     @staticmethod
     def box_shapes(width, rows, shard):
@@ -269,18 +278,21 @@
         return [(2 ** (hops - at), width, shard, D) for at in range(hops + 1)]
 
     def step(self, w, at):
-        base = self.slab_base + w * self.per_slab
+        base = self.slab_base + w * self.per_slab + at
         if at == 0:
             return [
-                self.sends.copy(base + code, self.grads.at[w, self.rows(self.place(self.other, w, code))], self.boxes[0].at[code, w], (self.other, self.z))
+                self.sends.copy(base, self.grads.at[w, self.rows(self.place(self.other, w, code))], self.boxes[0].at[code, w], (self.other, self.z))
                 for code in range(2**self.hops)
             ]
-        base += sum(2 ** (self.hops - one) for one in range(at))
         peer = flip(self.r, self.bit(w, at - 1))
         return [
-            self.sends.copy(base + code, self.boxes[at - 1].at[2 * code + 1, w], self.boxes[at].at[code, w], (peer, self.z))
+            self.sends.copy(base, self.boxes[at - 1].at[2 * code + 1, w], self.boxes[at].at[code, w], (peer, self.z))
             for code in range(2 ** (self.hops - at))
         ]
+
+    def whole(self, w, at):
+        part = self.boxes[at].at[:, w]
+        return self.sends.copy(self.slab_base + w * self.per_slab + at, part, part, (self.other, self.z))
 
     def over_width(self, w):
         if self.along:
@@ -311,8 +323,7 @@
             copy.start()
 
     def take(self, w, at):
-        for copy in self.step(w, at):
-            copy.wait_recv()
+        self.whole(w, at).wait_recv()
         for code in range(2 ** (self.hops - at)):
             box = self.boxes[at].at[code, w]
             if at == 0:
@@ -354,8 +365,7 @@
     def end(self):
         def one(w):
             for at in range(self.hops + 1):
-                for copy in self.step(w, at):
-                    copy.wait_send()
+                self.whole(w, at).wait_send()
 
             @pl.when(w != self.z)
             def _():
@@ -552,80 +562,62 @@
     tiles(width, body)
 
 
-def attend_back(low_ref, wa_ref, p_ref, q_ref, k_ref, v_ref, trig_ref, gp_ref, width, per, own, hook):
-    ext = HALO + own
+def attend_back(low_ref, wa_ref, p_ref, q_ref, k_ref, v_ref, trig_ref, gp_ref, w, per):
     group = per * HEAD
-    blocks = own // HALO
+    ext = gp_ref.shape[2]
+    blocks = ext // HALO - 1
     scale = HEAD**-0.5
-
-    def body(w):
-        hook(w)
-        gp_ref[w, 3 * group :, :] = jnp.zeros((group, ext), BF16)
-        gp_ref[w, :group, :HALO] = jnp.zeros((group, HALO), BF16)
-        turned = jnp.transpose(wa_ref[w, :, 3 * group - HEAD :])
-        upstream = dot(turned[HEAD:], low_ref[...]).astype(BF16)
-        for i in range(per):
-            h = w * per + i
-            grad_keys, grad_values = [None] * (blocks + 1), [None] * (blocks + 1)
-            for b in range(blocks):
-                q = q_ref[h, :, b * HALO : (b + 1) * HALO]
-                k = k_ref[h, :, b * HALO : (b + 2) * HALO]
-                v = v_ref[h, :, b * HALO : (b + 2) * HALO]
-                up = upstream[i * HEAD : (i + 1) * HEAD, b * HALO : (b + 1) * HALO]
-                weights = p_ref[h, b]
-                wide = weights.astype(F32)
-                grad_weights = dot_cols(v, up)
-                inner = jnp.sum(wide * grad_weights, 0, keepdims=True)
-                grad_scores = (wide * (grad_weights - inner)).astype(BF16)
-                gv = dot_rows(up, weights)
-                gk = dot_rows(q, grad_scores)
-                gq = dot(k, grad_scores) * scale
-                cols = slice((b + 1) * HALO, (b + 2) * HALO)
-                gp_ref[w, i * HEAD : (i + 1) * HEAD, cols] = rotated(gq, trig_ref[0, :, cols], -trig_ref[1, :, cols]).astype(BF16)
-                for part in range(2):
-                    piece = slice(part * HALO, (part + 1) * HALO)
-                    at = b + part
-                    grad_keys[at] = gk[:, piece] if grad_keys[at] is None else grad_keys[at] + gk[:, piece]
-                    grad_values[at] = gv[:, piece] if grad_values[at] is None else grad_values[at] + gv[:, piece]
-            for at in range(blocks + 1):
-                cols = slice(at * HALO, (at + 1) * HALO)
-                gp_ref[w, group + i * HEAD : group + (i + 1) * HEAD, cols] = rotated(
-                    grad_keys[at], trig_ref[0, :, cols], -trig_ref[1, :, cols]
-                ).astype(BF16)
-                gp_ref[w, 2 * group + i * HEAD : 2 * group + (i + 1) * HEAD, cols] = grad_values[at].astype(BF16)
-
-    tiles(width, body)
-
-
-def stream_back(wa_ref, gp_ref, u_ref, start, size, width):
-    cols = slice(start, start + size)
-    u_ref[:, cols] = dot(wa_ref[0], gp_ref[0, :, cols])
-
-    def body(at):
-        u_ref[:, cols] += dot(wa_ref[at + 1], gp_ref[at + 1, :, cols])
-
-    tiles(width - 1, body)
-
-
-def project_back(x_ref, low_ref, ao_ref, gp_ref, ga_ref, width, per, slab, before, after):
+    gp_ref[w, 3 * group :, :] = jnp.zeros((group, ext), BF16)
+    gp_ref[w, :group, :HALO] = jnp.zeros((group, HALO), BF16)
+    turned = jnp.transpose(wa_ref[w, :, 3 * group - HEAD :])
+    upstream = dot(turned[HEAD:], low_ref[...]).astype(BF16)
+    for i in range(per):
+        h = w * per + i
+        grad_keys, grad_values = [None] * (blocks + 1), [None] * (blocks + 1)
+        for b in range(blocks):
+            q = q_ref[h, :, b * HALO : (b + 1) * HALO]
+            k = k_ref[h, :, b * HALO : (b + 2) * HALO]
+            v = v_ref[h, :, b * HALO : (b + 2) * HALO]
+            up = upstream[i * HEAD : (i + 1) * HEAD, b * HALO : (b + 1) * HALO]
+            weights = p_ref[h, b]
+            wide = weights.astype(F32)
+            grad_weights = dot_cols(v, up)
+            inner = jnp.sum(wide * grad_weights, 0, keepdims=True)
+            grad_scores = (wide * (grad_weights - inner)).astype(BF16)
+            gv = dot_rows(up, weights)
+            gk = dot_rows(q, grad_scores)
+            gq = dot(k, grad_scores) * scale
+            cols = slice((b + 1) * HALO, (b + 2) * HALO)
+            gp_ref[w, i * HEAD : (i + 1) * HEAD, cols] = rotated(gq, trig_ref[0, :, cols], -trig_ref[1, :, cols]).astype(BF16)
+            for part in range(2):
+                piece = slice(part * HALO, (part + 1) * HALO)
+                at = b + part
+                grad_keys[at] = gk[:, piece] if grad_keys[at] is None else grad_keys[at] + gk[:, piece]
+                grad_values[at] = gv[:, piece] if grad_values[at] is None else grad_values[at] + gv[:, piece]
+        for at in range(blocks + 1):
+            cols = slice(at * HALO, (at + 1) * HALO)
+            gp_ref[w, group + i * HEAD : group + (i + 1) * HEAD, cols] = rotated(
+                grad_keys[at], trig_ref[0, :, cols], -trig_ref[1, :, cols]
+            ).astype(BF16)
+            gp_ref[w, 2 * group + i * HEAD : 2 * group + (i + 1) * HEAD, cols] = grad_values[at].astype(BF16)
+
+
+def stream_back(wa_ref, gp_ref, u_ref, w):
+    u_ref[...] += dot(wa_ref[w], gp_ref[w])
+
+
+def project_back(x_ref, low_ref, ao_ref, gp_ref, ga_ref, w, per):
     group = 3 * per * HEAD - HEAD
-
-    def body(at):
-        w = slab(at)
-        before(at, w)
-        ga_ref[w, :, :group] = dot_rows(x_ref[...], gp_ref[w, :group, :]).astype(BF16)
-        ga_ref[w, :, group:] = (
-            dot_rows(x_ref[...], gp_ref[w, group:, :]) + dot_rows(low_ref[...], ao_ref[w])
-        ).astype(BF16)
-        after(at, w)
-
-    tiles(width, body)
+    ga_ref[w, :, :group] = dot_rows(x_ref[...], gp_ref[w, :group, :]).astype(BF16)
+    ga_ref[w, :, group:] = (
+        dot_rows(x_ref[...], gp_ref[w, group:, :]) + dot_rows(low_ref[...], ao_ref[w])
+    ).astype(BF16)
 
 
 def block_kernel(width, rows, per, mix_ref, hist_ref, cot_ref, seg_ref, box_ref, own_ref, given_ref,
                  gcol_ref, bout_ref, small_ref, total_ref, left_ref,
                  full, st, ct, boxes_in, gain, x_one, stat_one, starts, trig, q, k, v, ao, prob, mid, stat_two, gmid, low, blk,
-                 gacc_one, gacc_two, halo_out, halo_in, macc, small_out, small_in, small_step,
+                 gacc_one, gacc_two, gs, hcol, macc, small_out, small_in, small_step,
                  last_box, boxes, load_sem, here_sem, send_sem, recv_sem):
     r, z = lax.axis_index("rows"), lax.axis_index("width")
     layers, piece, tokens = hist_ref.shape
@@ -635,7 +627,7 @@
     core, bits = row_bits(rows)
     hops = len(bits)
     cut = own // 2
-    greet(z, r, width, [core] + bits)
+    greet(z, r, width, rows)
     sends = Sends(send_sem, recv_sem)
     inside = own_ref is not None
     gathers = []
@@ -806,7 +798,7 @@
     scatters = []
     if inside:
         scatters = [
-            Scatter(sends, at, at > 0, full.at[at], [box.at[at] for box in boxes], last_box.at[at], total_ref.at[at], z, r, width, rows)
+            Scatter(sends, at, True, full.at[at], [box.at[at] for box in boxes], last_box.at[at], total_ref.at[at], z, r, width, rows)
             for at in range(3)
         ]
     attending, pair_back = scatters[:1], scatters[1:]
@@ -889,76 +881,72 @@
         pltpu.VMEM((width, own, D), BF16), pltpu.VMEM((width, own, D), BF16), pltpu.VMEM((D, own), F32),
     )
 
-    when_attend = at_steps({
-        1: [later("take_last", pair_back, 0)],
-        2: [later("take_chips", pair_back, 1), later("take_core", pair_back, 2)],
-        3: [later("relay", pair_back, 0)],
+    slab_start = at_steps({3: [later("take_last", pair_back, 1), later("relay", pair_back, 0)]})
+    slab_middle = at_steps({
+        1: [later("take_chips", pair_back, 1), later("take_core", pair_back, 2), later("take_last", pair_back, 0)],
+        3: [later("take_chips", pair_back, 2), later("take_core", pair_back, 3)],
     })
-    when_project = at_steps({3: [later("take_core", attending, 0), later("take_core", attending, 1)]})
     when_mix = {
-        0: [later("take_chips", attending, 0), later("take_chips", attending, 1)],
+        3: [
+            later("take_chips", attending, 0), later("take_chips", attending, 1), later("take_last", pair_back, 3),
+            later("relay", pair_back, 2),
+        ]
     }
-    halo = sends.make(halo_out, halo_in, (r, flip(z, 1)))
     half = own // 2
-    for part in range(2):
-        columns = pl.ds(pl.multiple_of(z * own + part * half, LANES), half)
-        for step in range(1, width):
-            target = lax.rem(z + step, width)
-            features = pl.ds(pl.multiple_of(target * piece, 16), piece)
-            gs_sends.append(
-                sends.make(blk.at[features, pl.ds(part * half, half)], gcol_ref.at[:, columns], (r, target))
-            )
+    halo_sends = []
+    own_columns = pl.ds(HALO, own)
+    for step in range(1, width):
+        target = lax.rem(z + step, width)
+        features = pl.ds(pl.multiple_of(target * piece, 16), piece)
+        gs_sends.append(sends.make(gs.at[features, own_columns], gcol_ref.at[:, here], (r, target)))
+        halo_sends.append(sends.make(gs.at[features, pl.ds(0, HALO)], hcol.at[lax.div(z, 2)], (r, target)))
 
     def scoped_back(gp, u):
-        def send_stream(part):
-            def write(cols, value):
-                blk[:, cols] = value.astype(BF16)
-
-            norm_back(
-                u, HALO, st, HALO, stat_one, HALO, gain, 0, lambda cols: gmid[:, cols], write, gacc_one, part * half, half
-            )
-            for copy in gs_sends[part * (width - 1) : (part + 1) * (width - 1)]:
-                copy.start()
-            columns = pl.ds(pl.multiple_of(z * own + part * half, LANES), half)
-            gcol_ref[:, columns] = blk[mine, pl.ds(part * half, half)]
-
-        attend_back(low, full.at[0], prob, q, k, v, trig, gp, width, per, own, when_attend)
-        stream_back(full.at[0], gp, u, 0, HALO, width)
+        def weights_back(at):
+            w = turned(at)
+            project_back(x_one, low, ao, gp, full.at[0], w, per)
+            for scatter in attending:
+                scatter.begin(w)
+
+        def body(at):
+            w = turned(at)
+            slab_start(at)
+            attend_back(low, full.at[0], prob, q, k, v, trig, gp, w, per)
+            slab_middle(at)
+            stream_back(full.at[0], gp, u, w)
+
+        u[...] = jnp.zeros_like(u)
+        tiles(width, body)
+
+        gs_own, gs_halo = gs.at[:, own_columns], gs.at[:, pl.ds(0, HALO)]
+
+        def write_own(cols, value):
+            gs_own[:, cols] = value.astype(BF16)
+
+        def write_halo(cols, value):
+            gs_halo[:, cols] = value.astype(BF16)
+
+        gacc_one[...] = jnp.zeros_like(gacc_one)
+        norm_back(u, 0, st, 0, stat_one, 0, gain, 0, lambda cols: 0.0, write_halo, gacc_one, 0, HALO)
+        norm_back(u, HALO, st, HALO, stat_one, HALO, gain, 0, lambda cols: gmid[:, cols], write_own, gacc_one, 0, own)
+        for copy in gs_sends:
+            copy.start()
+        gcol_ref[:, here] = gs[mine, own_columns]
 
         @pl.when(odd)
         def _():
-            halo_out[...] = u[:, 0:HALO].astype(BF16)
-            halo.start()
-
-        back("take_chips", pair_back, 2)
-        back("take_core", pair_back, 3)
-        stream_back(full.at[0], gp, u, HALO, own, width)
-        gacc_one[...] = jnp.zeros_like(gacc_one)
-        for copy in blk_sends:
-            copy.wait_send()
-        blk_here.wait()
-        send_stream(0)
-        back("take_last", pair_back, 1)
-
-        def after_project(at, w):
-            for scatter in attending:
-                scatter.begin(w)
-
-        project_back(x_one, low, ao, gp, full.at[0], width, per, turned, lambda at, w: when_project(at), after_project)
+            for copy in halo_sends:
+                copy.start()
+            hcol[lax.div(z, 2)] = gs[mine, pl.ds(0, HALO)]
+
+        tiles(width, weights_back)
+        back("take_core", attending, 0)
+        back("take_core", attending, 1)
+        back("take_last", pair_back, 2)
         back("relay", pair_back, 1)
-        back("take_last", pair_back, 2)
         back("take_chips", pair_back, 3)
         back("take_core", attending, 2)
         back("take_core", attending, 3)
-
-        @pl.when(jnp.logical_not(odd))
-        def _():
-            halo.wait_recv()
-            u[:, own : own + HALO] += halo_in[...].astype(F32)
-
-        send_stream(1)
-        back("relay", pair_back, 2)
-        back("take_last", pair_back, 3)
 
     pl.run_scoped(scoped_back, pltpu.VMEM((width, 4 * per * HEAD, ext), BF16), pltpu.VMEM((D, ext), F32))
 
@@ -976,8 +964,17 @@
         for at in range(3):
             load(at).start()
         for at in range(2 * width):
-            if at % width:
-                gs_sends[at // width * (width - 1) + at % width - 1].wait_recv()
+            if 0 < at < width:
+                gs_sends[at - 1].wait_recv()
+            if at == width:
+                for step in range(1, width):
+                    @pl.when(lax.rem(z + step, 2) == 1)
+                    def _(step=step):
+                        halo_sends[step - 1].wait_recv()
+
+                for pair_at in range(width // 2):
+                    cols = pl.ds((2 * pair_at + 1) * own - HALO, HALO)
+                    gcol_ref[:, cols] = (gcol_ref[:, cols].astype(F32) + hcol[pair_at].astype(F32)).astype(BF16)
             load(at).wait()
             cols = place(at)
 
@@ -1016,33 +1013,50 @@
         copy.start()
     back("take_last", attending, 0)
     back("take_last", attending, 1)
+    back("take_chips", attending, 2)
+    back("take_chips", attending, 3)
     current = small_out[z]
     for step in range(1, width):
         small_sends[step - 1].wait_recv()
         current = current + small_in[step - 1]
-    for at, bit in enumerate([core] + bits):
-        small_step[at, 0] = current
-        copy = sends.make(small_step.at[at, 0], small_step.at[at, 1], (flip(r, bit), z))
-        copy.start()
-        if at == 0:
-            back("take_chips", attending, 2)
-            back("take_chips", attending, 3)
-        copy.wait_recv()
-        current = current + small_step[at, 1]
-        small_sends.append(copy)
+    peers = plane_peers(r, rows)
+    small_step[0, 0] = current
+    if rows > 8:
+        for at, peer in enumerate(peers):
+            small_step[at, 0] = current
+            copy = sends.make(small_step.at[at, 0], small_step.at[at, 1], (peer, z))
+            copy.start()
+            copy.wait_recv()
+            current = current + small_step[at, 1]
+            small_sends.append(copy)
+    else:
+        plane_sends = [
+            sends.make(small_step.at[0, 0], small_step.at[at, 1], (peer, z)) for at, peer in enumerate(peers)
+        ]
+        for copy in plane_sends:
+            copy.start()
+        for at, copy in enumerate(plane_sends):
+            copy.wait_recv()
+            current = current + small_step[at, 1]
+        small_sends += plane_sends
     small_ref[...] = current
+    back("relay", attending, 0)
+    back("relay", attending, 1)
     back("take_last", attending, 2)
     back("take_last", attending, 3)
+    back("relay", attending, 2)
     for scatter in scatters:
         scatter.finish()
     for copy in blk_sends:
-        copy.wait_recv()
+        copy.wait()
+    blk_here.wait()
     for copy in gs_sends + small_sends:
         copy.wait_send()
 
     @pl.when(odd)
     def _():
-        halo.wait_send()
+        for copy in halo_sends:
+            copy.wait_send()
 
     for scatter in scatters:
         scatter.end()
@@ -1091,13 +1105,13 @@
         low(3, width, D, D), low(D, ext), low(D, own), full(width, 8, 2 * LANES), full(2, D, LANES), low(D, ext), full(8, ext),
         full(8, HALO + segments.shape[1]), full(2, HEAD // 2, ext), low(heads, HEAD, own), low(heads, HEAD, ext), low(heads, HEAD, ext),
         low(width, HEAD + group, own), low(heads, blocks, 2 * HALO, HALO), full(D, own), full(8, own),
-        full(D, own), low(D, own), low(D, own), full(D, LANES), full(D, LANES), low(D, HALO), low(D, HALO), full(layers, 8, LANES),
-        full(width, 8, 2 * LANES), full(width - 1, 8, 2 * LANES), full(digits, 2, 8, 2 * LANES),
+        full(D, own), low(D, own), low(D, own), full(D, LANES), full(D, LANES), low(D, ext), low(width // 2, piece, HALO), full(layers, 8, LANES),
+        full(width, 8, 2 * LANES), full(width - 1, 8, 2 * LANES), full(max(digits, rows - 1 if rows <= 8 else 0), 2, 8, 2 * LANES),
     ]
     common = len(scratch)
     if inside:
         scratch += [low(3, width + 1, shard, D)] + [low(3, *one) for one in box_shapes]
-    count = 6 * (width - 1) + 1 + (width - 1) + digits
+    count = 6 * (width - 1) + (width - 1) + max(digits, rows - 1 if rows <= 8 else 0)
     count += 3 * Gather.copies(width, rows) + 3 * Scatter.copies(width, rows)
     scratch += [
         pltpu.SemaphoreType.DMA((4,)), pltpu.SemaphoreType.DMA, pltpu.SemaphoreType.DMA((count,)), pltpu.SemaphoreType.DMA((count,)),
@@ -1151,63 +1165,67 @@
     return own_three, jnp.pad(gains, ((0, 8 - gains.shape[0]), (0, 2 * LANES - piece)))
 
 
-def finish_kernel(per_step, mix_ref, grad_ref, total_ref, out_ref, *refs):
-    weights, (hist_ref, block_ref, *news) = refs[:12], refs[12:]
-    at = pl.program_id(0)
+def finish_kernel(mix_ref, grad_ref, total_ref, out_ref, *refs):
+    weights, small_ref, rest, (hist_ref, block_ref, *news) = refs[:12], refs[12], refs[13:19], refs[19:-2]
+    made, sems = refs[-2:]
     piece = grad_ref.shape[0]
+    layers = hist_ref.shape[0]
     strip = 16
 
-    def body(row):
-        rows = pl.ds(pl.multiple_of(row * strip, strip), strip)
-        g = grad_ref[rows, :].astype(F32)
-        for j in range(per_step):
-            hist_ref[j, rows, :] = (mix_ref[at * per_step + j] * g).astype(BF16)
-
-    tiles(piece // strip, body)
+    def cut(at):
+        return pl.ds(pl.multiple_of(at * strip, strip), strip)
+
+    def store(at):
+        return pltpu.make_async_copy(made.at[:, cut(at), :], hist_ref.at[:, cut(at), :], sems.at[at])
+
+    def part(at):
+        g = grad_ref[cut(at), :].astype(F32)
+        for j in range(layers):
+            made[j, cut(at), :] = (mix_ref[j] * g).astype(BF16)
+        store(at).start()
+
+    tiles(piece // strip, part)
+    block_ref[...] = out_ref[...]
 
     def update(which, gradient, rate):
         found = optimize(weights[3 * which][...], gradient, weights[3 * which + 1][...], weights[3 * which + 2][...], rate, DECAY)
         for ref, value in zip(news[3 * which : 3 * which + 3], found):
             ref[...] = value
 
-    @pl.when(at == 0)
-    def _():
-        for k in range(3):
-            gradient = total_ref[0, :, k * piece : (k + 1) * piece]
-            found = optimize(weights[0][k], gradient, weights[1][k], weights[2][k], RATE_MATRIX, DECAY)
-            for ref, value in zip(news[:3], found):
-                ref[k] = value
-
-    @pl.when(at == 1)
-    def _():
-        update(1, jnp.transpose(total_ref[0, :, 3 * piece :]), RATE_OUTPUT)
-
-    @pl.when(at == 2)
-    def _():
-        update(2, total_ref[1], RATE_MATRIX)
-
-    @pl.when(at == 3)
-    def _():
-        update(3, total_ref[2], RATE_MATRIX)
-        block_ref[...] = out_ref[...]
-
-
-def finish(mix, grad_stream, total, block_output, layers, weights):
+    for k in range(3):
+        gradient = total_ref[0, :, k * piece : (k + 1) * piece]
+        found = optimize(weights[0][k], gradient, weights[1][k], weights[2][k], RATE_MATRIX, DECAY)
+        for ref, value in zip(news[:3], found):
+            ref[k] = value
+    update(1, jnp.transpose(total_ref[0, :, 3 * piece :]), RATE_OUTPUT)
+    update(2, total_ref[1], RATE_MATRIX)
+    update(3, total_ref[2], RATE_MATRIX)
+    sums = (small_ref[0:2, 0:piece], small_ref[2:3, 0 : rest[3].shape[1]])
+    for which, rate in enumerate((RATE_GAIN, RATE_MIX)):
+        w, m, v = rest[3 * which : 3 * which + 3]
+        found = optimize(w[...], sums[which], m[...], v[...], rate, 0.0)
+        for ref, value in zip(news[12 + 3 * which : 15 + 3 * which], found):
+            ref[...] = value
+    tiles(piece // strip, lambda at: store(at).wait())
+
+
+def finish(mix, grad_stream, total, small, block_output, layers, weights, rest):
     shard = total.shape[1]
     piece, tokens = grad_stream.shape
-    if shard % 16 == 0 and layers % 5 == 0:
-        weights = [jnp.transpose(one) if at // 3 == 3 else one for at, one in enumerate(weights)]
-        held = [shape(*one.shape) for one in weights]
-        per_step = layers // 5
+    if shard % 16 == 0:
+        given = [jnp.transpose(one) if at // 3 == 3 else one for at, one in enumerate(weights)]
+        given += [small] + list(rest[:3]) + [jnp.reshape(one, (1, layers)) for one in rest[3:]]
+        held = [shape(*one.shape) for at, one in enumerate(given) if at != 12]
         history_grad, block_output, *news = pl.pallas_call(
-            functools.partial(finish_kernel, per_step),
-            grid=(5,),
+            finish_kernel,
             out_shape=[shape(layers, piece, tokens, dtype=BF16), shape(piece, tokens, dtype=BF16)] + held,
-            in_specs=[pl.BlockSpec(memory_space=pltpu.SMEM)] + vmem(3 + len(weights)),
-            out_specs=[pl.BlockSpec((per_step, piece, tokens), lambda at: (at, 0, 0))] + vmem(1 + len(weights)),
+            in_specs=[pl.BlockSpec(memory_space=pltpu.SMEM)] + vmem(3 + len(given)),
+            out_specs=[pl.BlockSpec(memory_space=pl.ANY)] + vmem(1 + len(held)),
+            scratch_shapes=[pltpu.VMEM((layers, piece, tokens), BF16), pltpu.SemaphoreType.DMA((piece // 16,))],
             compiler_params=pltpu.CompilerParams(vmem_limit_bytes=60 * MIB),
-        )(mix, grad_stream, total, block_output, *weights)
-        return (history_grad, block_output, *[jnp.transpose(one) if at // 3 == 3 else one for at, one in enumerate(news)])
+        )(mix, grad_stream, total, block_output, *given)
+        news = [jnp.transpose(one) if at // 3 == 3 else one for at, one in enumerate(news)]
+        return (block_output, history_grad, *news[:15], *[jnp.reshape(one, (layers,)) for one in news[15:]])
     history_grad = (mix[:, None, None] * grad_stream[None].astype(F32)).astype(BF16)
     first = total[0]
     gradients = (
@@ -1218,7 +1236,9 @@
     for at, rate in enumerate((RATE_MATRIX, RATE_OUTPUT, RATE_MATRIX, RATE_MATRIX)):
         w, m, v = weights[3 * at : 3 * at + 3]
         news += optimize(w, gradients[at], m, v, rate, DECAY)
-    return (history_grad, block_output, *news)
+    news += optimize(rest[0], small[0:2, :piece], rest[1], rest[2], RATE_GAIN, 0.0)
+    news += optimize(rest[3], small[2, :layers], rest[4], rest[5], RATE_MIX, 0.0)
+    return (block_output, history_grad, *news)
 
 
 def on_device(
@@ -1231,10 +1251,8 @@
     weights = (
         w_attend, m_attend, v_attend, w_output, m_output, v_output, w_expand, m_expand, v_expand, w_reduce, m_reduce, v_reduce,
     )
-    history_grad, block_output, *news = finish(mix, grad_stream, total, block_output, layers, weights)
-    new_gains = optimize(gains, small[0:2, :piece], m_gains, v_gains, RATE_GAIN, 0.0)
-    new_mix = optimize(mix, small[2, :layers], m_mix, v_mix, RATE_MIX, 0.0)
-    return (block_output, history_grad, *news, *new_gains, *new_mix)
+    rest = (gains, m_gains, v_gains, mix, m_mix, v_mix)
+    return finish(mix, grad_stream, total, small, block_output, layers, weights, rest)
 
 
 def solution(mesh):

time: 200 us -> 193 us (0.965)
  Pallas kernels: 196 us -> 192 us
  other arithmetic: 2.52 us -> 0 us
    pallas_call x1, Pallas kernels: 182 us -> 179 us  [block(): pl.pallas_call(kernel, out_shape=outs, in_specs=specs, out_specs=out_spec...]
    sub x2 -> x0, other arithmetic: 2.52 us -> none  [optimize(): weight - rate * (first_fixed / (jnp.sqrt(second_fixed) + EPS_ADAM) + deca...]
where the time goes in v5:
time: 193 us
  Pallas kernels  192 us (99%)
    pallas_call x1, Pallas kernels, block(): pl.pallas_call(kernel, out_shape=outs, in_specs=specs, out_specs=out_spec...  179 us
    pallas_call x1, Pallas kernels, finish(): pl.pallas_call(finish_kernel, out_shape=[shape(layers, piece, tokens, dty...  11.5 us

profile of v5, /device:TPU:0, one launch (start us, length us, event | category | flops | bytes accessed | tf_op | source)
XLA Modules:
  0.0 193.0 jit_solution(5793496525765838674)
XLA Ops:
  0.7 2.1 %shard_map.356 = (bf16[3,96,768]{2,1,0:T(8,128)(2,1)}, f32[8,256]{1,0:T(8,128)}) custom-call(f32[3,96,192]{2,1,0:T(8,128)} %refs_0_.3, f32[192,96]{1,0:T(8,128)} %refs_3_.3, f32[96,768]{1,0:T(8,128)} %refs_6_.1, f32[96,768]{1,0:T(8,128)} %bitcast.12, f32[2,192]{1,0:T(2,128)} %refs_13_.1), custom_call_target="tpu_custom_call" | custom-call | tf_op jit(solution)/shard_map/pallas_call | solution.py:1156
  2.8 178.5 %shard_map.357 = (bf16[192,2048]{1,0:T(8,128)(2,1)}, bf16[192,2048]{1,0:T(8,128)(2,1)}, f32[8,256]{1,0:T(8,128)}, f32[3,96,768]{2,1,0:T(8,128)}) custom-call(f32[25]{0:T(128)} %mix_ref.1, bf16[25,192,2048]{2,1,0:T(8,128)(2,1)} %refs_1_.2, bf16[192,2048]{1,0:T(8,128)(2,1)} %refs_2_.2, s32[2,1024]{1,0:T(2,128)} %refs_3_.2, ...), custom_call_target="tpu_custom_call" | custom-call | tf_op jit(solution)/shard_map/pallas_call | solution.py:1130
  181.3 11.5 %shard_map.358 = (bf16[25,192,2048]{2,1,0:T(8,128)(2,1)}, bf16[192,2048]{1,0:T(8,128)(2,1)}, f32[3,96,192]{2,1,0:T(8,128)}, f32[3,96,192]{2,1,0:T(8,128)}, f32[3...) custom-call(f32[25]{0:T(128)} %mix_ref.1, ...), custom_call_target="tpu_custom_call" | custom-call | tf_op jit(solution)/shard_map/pallas_call | solution.py:1219

commit v6 on v5

--- a/solution.py
+++ b/solution.py
@@ -1013,8 +1013,10 @@
         copy.start()
     back("take_last", attending, 0)
     back("take_last", attending, 1)
+    back("relay", attending, 0)
     back("take_chips", attending, 2)
     back("take_chips", attending, 3)
+    back("relay", attending, 1)
     current = small_out[z]
     for step in range(1, width):
         small_sends[step - 1].wait_recv()
@@ -1040,8 +1042,6 @@
             current = current + small_step[at, 1]
         small_sends += plane_sends
     small_ref[...] = current
-    back("relay", attending, 0)
-    back("relay", attending, 1)
     back("take_last", attending, 2)
     back("take_last", attending, 3)
     back("relay", attending, 2)

time: 193 us -> 192 us (level)
  Pallas kernels: 192 us -> 190 us
where the time goes in v6:
time: 192 us; the launch traced here: 191 us
  Pallas kernels  190 us (99%)
    pallas_call x1, Pallas kernels, block(): pl.pallas_call(kernel, out_shape=outs, in_specs=specs, out_specs=out_spec...  177 us
    pallas_call x1, Pallas kernels, finish(): pl.pallas_call(finish_kernel, out_shape=[shape(layers, piece, tokens, dty...  11.5 us

profile of v6, /device:TPU:0, one launch (start us, length us, event | category | flops | bytes accessed | tf_op | source)
XLA Modules:
  0.0 191.2 jit_solution(13353439851630885031)
XLA Ops:
  0.7 2.1 %shard_map.356 = (bf16[3,96,768]{2,1,0:T(8,128)(2,1)}, f32[8,256]{1,0:T(8,128)}) custom-call(f32[3,96,192]{2,1,0:T(8,128)} %refs_0_.3, f32[192,96]{1,0:T(8,128)} %refs_3_.3, f32[96,768]{1,0:T(8,128)} %refs_6_.1, f32[96,768]{1,0:T(8,128)} %bitcast.12, f32[2,192]{1,0:T(2,128)} %refs_13_.1), custom_call_target="tpu_custom_call" | custom-call | tf_op jit(solution)/shard_map/pallas_call | solution.py:1156
  2.8 176.7 %shard_map.357 = (bf16[192,2048]{1,0:T(8,128)(2,1)}, bf16[192,2048]{1,0:T(8,128)(2,1)}, f32[8,256]{1,0:T(8,128)}, f32[3,96,768]{2,1,0:T(8,128)}) custom-call(f32[25]{0:T(128)} %mix_ref.1, bf16[25,192,2048]{2,1,0:T(8,128)(2,1)} %refs_1_.2, bf16[192,2048]{1,0:T(8,128)(2,1)} %refs_2_.2, s32[2,1024]{1,0:T(2,128)} %refs_3_.2, ...), custom_call_target="tpu_custom_call" | custom-call | tf_op jit(solution)/shard_map/pallas_call | solution.py:1130
  179.5 11.5 %shard_map.358 = (bf16[25,192,2048]{2,1,0:T(8,128)(2,1)}, bf16[192,2048]{1,0:T(8,128)(2,1)}, f32[3,96,192]{2,1,0:T(8,128)}, f32[3,96,192]{2,1,0:T(8,128)}, f32[3...) custom-call(f32[25]{0:T(128)} %mix_ref.1, ...), custom_call_target="tpu_custom_call" | custom-call | tf_op jit(solution)/shard_map/pallas_call | solution.py:1219
